TPU v7x, 32 devices: a whole 2x2x4 slice. The times are simulated.
32 devices in a mesh: row: 8 (over y, x, core), col: 4 (over z).
Axes of the slice: x: 2, y: 2, z: 4, core: 2. Of those that a mesh axis runs over, the one named last changes fastest.
Arguments:
- pair_activation: bfloat16 [1024, 1024, 128], P('row', 'col'), may hold values from -80 to 80
- target_distance_bins: int32 [1024, 1024], P('row', 'col'), may hold values from 0 to 63, as said below
- distogram_weight: bfloat16 [128, 64], replicated, may hold values from -2 to 2
- distogram_bias: float32 [64], replicated, may hold values from -0.25 to 0.25
- outer_pair_weight: bfloat16 [1024, 128], replicated, may hold values from -0.1875 to 0.1875
- stored_lhs_operand: bfloat16 [64, 32, 1024], P('row', None, 'col'), may hold values from -6 to 6
- stored_rhs_operand: bfloat16 [64, 32, 1024], P('row', None, 'col'), may hold values from -6 to 6
- left_projection_weight: bfloat16 [64, 32], replicated, may hold values from -0.75 to 0.75
- right_projection_weight: bfloat16 [64, 32], replicated, may hold values from -0.75 to 0.75
- outer_mean_norm_gain: float32 [64], replicated, may hold values from 0.25 to 1.75
- transition_norm_gain: float32 [64], replicated, may hold values from 0.25 to 1.75
- gate_weight: bfloat16 [64, 256], replicated, may hold values from -0.75 to 0.75
- up_weight: bfloat16 [64, 256], replicated, may hold values from -0.75 to 0.75
- down_weight: bfloat16 [256, 64], replicated, may hold values from -0.375 to 0.375
- side_stack_entry: bfloat16 [64, 64, 1024], P(('row', 'col')), may hold values from -6 to 6
- arriving_stack_derivative: bfloat16 [64, 64, 1024], P(('row', 'col')), may hold values from -4 to 4
Outputs:
- pair_activation_gradient: bfloat16 [1024, 1024, 128], P('row', 'col')
- alignment_gradient: bfloat16 [64, 64, 1024], P(('row', 'col'))
Inputs may be any that keep to these rules, and one draw needn't show every extreme that they name: target_distance_bins[i, j] equals target_distance_bins[j, i].
All inputs are finite; a program needn't handle non-finite values.
Results may differ from a plain program's by a relative error of at most 0.0098.
Values may be sent and summed in bfloat16 or wider, within the bound.
No kernel may reach another device: no remote copies, remote signals or barrier semaphores. Data moves between devices by JAX's collectives and lax.ppermute only.
A program may use at most 64 MiB of HBM per device.

v0:
```python
import jax
import jax.numpy as jnp
from jax import lax
from jax.sharding import PartitionSpec as P


def apply_layer_norm(features):
    centered = features - jnp.mean(features, axis=1, keepdims=True)
    scale_inv = lax.rsqrt(jnp.mean(centered * centered, axis=1, keepdims=True) + 1e-05)
    return (centered * scale_inv, scale_inv)


def norm_backward_step(incoming, normed_field, scale_inv):
    first_mean = jnp.mean(incoming, axis=1, keepdims=True)
    second_mean = jnp.mean(incoming * normed_field, axis=1, keepdims=True)
    return scale_inv * (incoming - first_mean - normed_field * second_mean)


def regroup(logit_tile):
    return lax.all_to_all(logit_tile, "col", split_axis=1, concat_axis=2, tiled=True)


def regroup_seqs(factor, row_devices, col_devices):
    split_form = factor.reshape((row_devices, col_devices, -1) + factor.shape[1:])
    return jnp.swapaxes(split_form, 0, 1).reshape(factor.shape)


def per_device(
    pair_activation,
    target_distance_bins,
    distogram_weight,
    distogram_bias,
    outer_pair_weight,
    stored_lhs_operand,
    stored_rhs_operand,
    left_projection_weight,
    right_projection_weight,
    outer_mean_norm_gain,
    transition_norm_gain,
    gate_weight,
    up_weight,
    down_weight,
    side_stack_entry,
    arriving_stack_derivative,
):
    pair_rows = pair_activation.shape[0]
    pair_cols = pair_activation.shape[1]
    bin_count = distogram_weight.shape[1]
    factor_width = stored_lhs_operand.shape[1]
    row_devices = lax.axis_size("row")
    col_devices = lax.axis_size("col")
    seq_total = stored_lhs_operand.shape[0] * row_devices
    alignment_widened = side_stack_entry.astype(jnp.float32)
    first_normed_rows, first_inverse_scale = apply_layer_norm(alignment_widened)
    normed_input = (first_normed_rows * transition_norm_gain[None, :, None]).astype(jnp.bfloat16)
    gate_value = jnp.einsum(
        "smi,mh->shi", normed_input, gate_weight, preferred_element_type=jnp.float32
    )
    upward = jnp.einsum("smi,mh->shi", normed_input, up_weight, preferred_element_type=jnp.float32)
    hidden_state = (jax.nn.silu(gate_value) * upward).astype(jnp.bfloat16)
    alignment_output = alignment_widened + jnp.einsum(
        "ajc,jr->arc", hidden_state, down_weight, preferred_element_type=jnp.float32
    )
    second_normed_rows, second_inverse_scale = apply_layer_norm(alignment_output)
    logits = jnp.einsum(
        "ijp,pb->bij", pair_activation, distogram_weight, preferred_element_type=jnp.float32
    )
    logits = (logits + distogram_bias[:, None, None]).astype(jnp.bfloat16)
    flipped = lax.all_to_all(
        regroup(logits), ("row", "col"), split_axis=2, concat_axis=1, tiled=True
    )
    mirrored = jnp.swapaxes(regroup(flipped), 1, 2)
    symmetric = logits.astype(jnp.float32) + mirrored.astype(jnp.float32)
    probability = jax.nn.softmax(symmetric, axis=0)
    bin_levels = lax.broadcasted_iota(jnp.int32, (bin_count, 1, 1), 0)
    one_hot = (target_distance_bins[None, :, :] == bin_levels).astype(jnp.float32)
    logit_grad = (2.0 * (probability - one_hot)).astype(jnp.bfloat16)
    pair_activation_gradient = jnp.einsum(
        "bij,pb->ijp", logit_grad, distogram_weight, preferred_element_type=jnp.float32
    ).astype(jnp.bfloat16)
    left_all, right_all = (
        lax.all_gather(stored_lhs_operand, "row", axis=0, tiled=True),
        lax.all_gather(stored_rhs_operand, "row", axis=0, tiled=True),
    )
    left_all = regroup_seqs(left_all, row_devices, col_devices)
    right_all = regroup_seqs(right_all, row_devices, col_devices)
    seq_count = left_all.shape[0]
    step_rows = 8

    def single_tile(block_index, contribution):
        row_start = block_index * step_rows
        grad_rows = lax.dynamic_slice_in_dim(pair_activation_gradient, row_start, step_rows, 0)
        tensor_product_derivative = jnp.einsum(
            "ijp,kp->ijk", grad_rows, outer_pair_weight, preferred_element_type=jnp.float32
        ).astype(jnp.bfloat16)
        tensor_product_derivative = tensor_product_derivative.reshape(
            step_rows, pair_cols, factor_width, factor_width
        )
        lhs_portion = jnp.einsum(
            "tdpa,wad->wpt",
            tensor_product_derivative,
            right_all,
            preferred_element_type=jnp.float32,
        )
        rhs_portion = jnp.einsum(
            "ijce,scj->sei", tensor_product_derivative, left_all, preferred_element_type=jnp.float32
        )
        joined = jnp.concatenate([lhs_portion, rhs_portion], axis=1)
        return lax.dynamic_update_slice_in_dim(contribution, joined, row_start, 2)

    contribution = lax.fori_loop(
        0,
        pair_rows // step_rows,
        single_tile,
        jnp.zeros((seq_count, 2 * factor_width, pair_rows), jnp.float32),
    )
    both_weights = jnp.concatenate(
        [left_projection_weight, right_projection_weight], axis=1
    ).astype(jnp.float32)
    partial_terms = (
        jnp.einsum("mc,sci->smi", both_weights, contribution, precision=lax.Precision.HIGHEST)
        / seq_total
    )
    reduced_part = lax.psum_scatter(partial_terms, "col", scatter_dimension=0, tiled=True)
    sequence_grad = lax.all_to_all(
        reduced_part.astype(jnp.bfloat16), "row", split_axis=0, concat_axis=2, tiled=True
    )
    norm_input_gradient = sequence_grad.astype(jnp.float32)
    middle_gradient = arriving_stack_derivative.astype(jnp.float32) + norm_backward_step(
        norm_input_gradient * outer_mean_norm_gain[None, :, None],
        second_normed_rows,
        second_inverse_scale,
    )
    mid_half = middle_gradient.astype(jnp.bfloat16)
    hidden_grad = jnp.einsum(
        "smi,hm->shi", mid_half, down_weight, preferred_element_type=jnp.float32
    )
    sigmoid_gate = jax.nn.sigmoid(gate_value)
    gate_grad = (
        hidden_grad * upward * sigmoid_gate * (1.0 + gate_value * (1.0 - sigmoid_gate))
    ).astype(jnp.bfloat16)
    up_grad = (hidden_grad * gate_value * sigmoid_gate).astype(jnp.bfloat16)
    normed_rows_gradient = jnp.einsum(
        "shi,mh->smi", gate_grad, gate_weight, preferred_element_type=jnp.float32
    )
    normed_rows_gradient = normed_rows_gradient + jnp.einsum(
        "shi,mh->smi", up_grad, up_weight, preferred_element_type=jnp.float32
    )
    alignment_gradient = middle_gradient + norm_backward_step(
        normed_rows_gradient * transition_norm_gain[None, :, None],
        first_normed_rows,
        first_inverse_scale,
    )
    return (pair_activation_gradient, alignment_gradient.astype(jnp.bfloat16))


def solution(mesh):
    return jax.shard_map(
        per_device,
        mesh=mesh,
        in_specs=(
            P("row", "col", None),
            P("row", "col"),
            P(),
            P(),
            P(),
            P("row", None, "col"),
            P("row", None, "col"),
            P(),
            P(),
            P(),
            P(),
            P(),
            P(),
            P(),
            P(("row", "col"), None, None),
            P(("row", "col"), None, None),
        ),
        out_specs=(P("row", "col", None), P(("row", "col"), None, None)),
        check_vma=False,
    )
```

profile of v0, /device:TPU:0, one launch (start us, length us, event | category | flops | bytes accessed | tf_op | source)
XLA Modules:
  0.0 818.6 jit_solution(13754875309703898385)
XLA Ops:
  13.6 99.3 %all_to_all.54 = bf16[64,128,256]{2,0,1:T(8,128)(2,1)S(1)} all-to-all(bf16[64,128,256]{2,0,1:T(8,128)(2,1)S(1)} %add_convert_fusion), channel_id=1, replica_groups=mesh['row'=8,'col'=4] {'col'}, dimensions={1} | all-to-all | bytes 8388608 | tf_op jit(solution)/shard_map/all_to_all | solution.py:20
  118.0 11.2 %copy.136 = bf16[64,32,4,256]{0,1,3,2:T(8,128)(2,1)} copy(bf16[64,32,4,256]{3,2,1,0:T(4,128)(2,1)} %bitcast.193) | data formatting | bytes 8388608 | tf_op jit(solution)/shard_map/all_to_all | solution.py:20
  129.2 13.9 %reshape.104 = bf16[32,2,32768]{2,1,0:T(2,128)(2,1)} reshape(bf16[1024,32,64]{2,1,0:T(8,128)(2,1)} %bitcast.188) | data formatting | bytes 8388608
  143.1 96.7 %all_to_all.55 = bf16[32,2,32768]{2,1,0:T(2,128)(2,1)} all-to-all(bf16[32,2,32768]{2,1,0:T(2,128)(2,1)} %reshape.104), channel_id=1, replica_groups=mesh['row'=8,'col'=4] {'row','col'}, dimensions={0} | all-to-all | bytes 8388608 | tf_op jit(solution)/shard_map/all_to_all | solution.py:69
  239.8 13.6 %reshape.105 = bf16[1024,32,64]{2,1,0:T(8,128)(2,1)} reshape(bf16[32,2,32768]{2,1,0:T(2,128)(2,1)} %all_to_all.55) | data formatting | bytes 8388608
  253.4 10.5 %copy.119 = bf16[64,32,32,32]{0,3,2,1:T(8,128)(2,1)} copy(bf16[64,32,32,32]{0,2,3,1:T(8,128)(2,1)} %bitcast.190) | data formatting | bytes 8388608 | tf_op jit(solution)/shard_map/all_to_all | solution.py:69
  264.0 9.5 %reshape.106 = bf16[4,2,262144]{2,1,0:T(2,128)(2,1)} reshape(bf16[1024,32,64]{2,1,0:T(8,128)(2,1)} %bitcast.191) | data formatting | bytes 8388608
  280.2 25.9 %all-gather.3.cloned.1.call-done = bf16[64,32,256]{2,1,0:T(8,128)(2,1)} async-done(((bf16[8,32,256]{2,1,0:T(8,128)(2,1)}), bf16[64,32,256]{2,1,0:T(8,128)(2,1)}) %all-gather.3.cloned.1.call-update) | async-done | bytes 1048592 | tf_op jit(solution)/shard_map/all_gather | solution.py:83
  309.0 22.4 %all-gather.5.cloned.1.call-done = bf16[64,32,256]{2,1,0:T(8,128)(2,1)} async-done(((bf16[8,32,256]{2,1,0:T(8,128)(2,1)}), bf16[64,32,256]{2,1,0:T(8,128)(2,1)}) %all-gather.5.cloned.1.call-update) | async-done | bytes 1048592 | tf_op jit(solution)/shard_map/all_gather | solution.py:82
  335.0 37.5 %all-to-all-done.2 = bf16[4,2,262144]{2,1,0:T(2,128)(2,1)} async-done(((bf16[4,2,262144]{2,1,0:T(2,128)(2,1)}), bf16[4,2,262144]{2,1,0:T(2,128)(2,1)}, u32[]{:S(2)}, u32[]{:S(2)}) %all-to-all-start.2) | async-done | bytes 4194336 | tf_op jit(solution)/shard_map/all_to_all | solution.py:20
  372.5 9.3 %reshape.107 = bf16[1024,32,64]{2,1,0:T(8,128)(2,1)} reshape(bf16[4,2,262144]{2,1,0:T(2,128)(2,1)} %all-to-all-done.2) | data formatting | bytes 8388608
  381.8 12.0 %copy.120 = bf16[64,1024,32]{1,2,0:T(8,128)(2,1)} copy(bf16[64,1024,32]{0,2,1:T(8,128)(2,1)} %bitcast.189) | data formatting | bytes 8388608 | tf_op jit(solution)/shard_map/all_to_all | solution.py:20
  393.8 8.8 %reshape.93 = f32[64,4,256,32]{2,1,3,0:T(4,128)} reshape(bf16[64,1024,32]{1,2,0:T(8,128)(2,1)} %copy.120) | data formatting | bytes 12582912 | tf_op jit(solution)/shard_map/convert_element_type | solution.py:73
  402.6 8.4 %copy.121 = f32[64,256,4,32]{1,0,3,2:T(8,128)S(1)} copy(f32[64,256,4,32]{1,2,3,0:T(4,128)} %bitcast.192) | data formatting | bytes 16777216 | tf_op jit(solution)/shard_map/convert_element_type | solution.py:73
  416.9 10.9 %convolution_convert_fusion.1 = bf16[128,256,128]{2,1,0:T(8,128)(2,1)} fusion(s32[128,256]{1,0:T(8,128)S(1)} %copy-done.19, bf16[128,64]{0,1:T(8,128)(2,1)S(1)} %copy-done.14, f32[64,128,256]{2,0,1:T(8,128)} %bitcast_add_fusion), kind=kOutput, calls=%fused_computation.18 | convolution fusion | flops 555810944 | bytes 16924672 | tf_op jit(solution)/shard_map/bij,pb->ijp/dot_general | solution.py:78
  430.3 313.1 %while.13 = (s32[]{:T(128)}, f32[64,64,128]{0,1,2:T(8,128)}, bf16[128,256,128]{2,1,0:T(8,128)(2,1)}, bf16[1024,128]{1,0:T(8,128)(2,1)S(1)}, bf16[64,32,256]{2,0,...) while((s32[]{:T(128)}, f32[64,64,128]{0,1,2:T(8,128)}, ...), condition=%wide.region_7.8_spmd, body=%wide.region_6.7_spmd.sunk | while | flops 1075871744 | bytes 41156796 | solution.py:111
  434.5 6.5 copy.158
  454.1 6.5 copy.158
  473.7 6.5 copy.158
  493.2 6.5 copy.158
  512.8 6.5 copy.158
  532.3 6.5 copy.158
  753.5 40.5 %reduce-scatter.2.cloned.1.call-done = f32[16,64,128]{2,1,0:T(8,128)} async-done(((f32[64,64,128]{2,1,0:T(8,128)}), f32[16,64,128]{2,1,0:T(8,128)}) %reduce-scatter.2.cloned.1.call-update) | async-done | bytes 524304 | tf_op jit(solution)/shard_map/reduce_scatter | solution.py:124
  799.6 6.8 all-to-all-done.3
  (185 shorter events, 327.5 us)
Async XLA Ops:
  7.2 743.8 %copy-start = (bf16[64,256]{1,0:T(8,128)(2,1)S(1)}, bf16[64,256]{1,0:T(8,128)(2,1)}, u32[]{:S(2)}) copy-start(bf16[64,256]{1,0:T(8,128)(2,1)} %param.30) | copy-start | bytes 98308
  13.6 99.3 %copy-start.2 = (bf16[64,128,256]{2,0,1:T(8,128)(2,1)}, bf16[64,128,256]{2,0,1:T(8,128)(2,1)S(1)}, u32[]{:S(2)}) copy-start(bf16[64,128,256]{2,0,1:T(8,128)(2,1)S(1)} %add_convert_fusion) | copy-start | bytes 12582916
  273.5 6.5 copy-start.15
  273.5 6.6 copy-start.16
  273.5 99.1 %all-to-all-start.2 = ((bf16[4,2,262144]{2,1,0:T(2,128)(2,1)}), bf16[4,2,262144]{2,1,0:T(2,128)(2,1)}, u32[]{:S(2)}, u32[]{:S(2)}) async-start(bf16[4,2,262144]{2,1,0:T(2,128)(2,1)} %reshape.106), calls=%async_computation.2 | async-start | bytes 8388608 | tf_op jit(solution)/shard_map/all_to_all | solution.py:20
  278.4 27.6 %all-gather.3.cloned.1.call-start = ((), (), s32[]{:S(2)}) async-start(), calls=%async_computation.5 | async-start | bytes 1179648 | tf_op jit(solution)/shard_map/all_gather | solution.py:83
  279.2 52.3 %all-gather.5.cloned.1.call-start = ((), (), s32[]{:S(2)}) async-start(), calls=%async_computation.6 | async-start | bytes 1179648 | tf_op jit(solution)/shard_map/all_gather | solution.py:82
  279.9 514.1 %reduce-scatter.2.cloned.1.call-start = ((), (), s32[]{:S(2)}) async-start(), calls=%async_computation.7 | async-start | bytes 2621440 | tf_op jit(solution)/shard_map/reduce_scatter | solution.py:124
  402.6 8.4 %copy-start.3 = (bf16[64,128,256]{2,0,1:T(8,128)(2,1)S(1)}, bf16[64,128,256]{2,0,1:T(8,128)(2,1)}, u32[]{:S(2)}) copy-start(bf16[64,128,256]{2,0,1:T(8,128)(2,1)} %copy-done.2) | copy-start | bytes 12582916
  411.0 5.9 copy-start.14
  411.1 5.9 copy-start.19
  460.6 3.6 copy-start.1
  480.1 3.6 copy-start.1
  499.7 3.6 copy-start.1
  558.4 3.6 copy-start.1
  578.0 3.6 copy-start.1
  597.5 3.6 copy-start.1
  617.1 3.6 copy-start.1
  636.7 3.6 copy-start.1
  656.2 3.6 copy-start.1
  715.0 3.6 copy-start.1
  752.1 54.3 %copy-start.17 = (f32[64]{0:T(128)S(1)}, f32[64]{0:T(128)}, u32[]{:S(2)}) copy-start(f32[64]{0:T(128)} %param.27) | copy-start | bytes 772
  753.5 53.3 %copy-start.11 = (bf16[2,64,1024]{2,1,0:T(8,128)(2,1)S(1)}, bf16[2,64,1024]{2,1,0:T(8,128)(2,1)}, u32[]{:S(2)}) copy-start(bf16[2,64,1024]{2,1,0:T(8,128)(2,1)} %param.33) | copy-start | bytes 786436
  795.8 10.6 %all-to-all-start.3 = ((bf16[16,64,128]{2,1,0:T(8,128)(2,1)}), bf16[16,64,128]{2,1,0:T(8,128)(2,1)S(1)}, u32[]{:S(2)}, u32[]{:S(2)}) async-start(bf16[16,64,128]{2,1,0:T(8,128)(2,1)} %convert_element_type.96), calls=%async_computation.4 | async-start | bytes 524288 | tf_op jit(solution)/shard_map/all_to_all | solution.py:125
  (16 other events, 43.1 us)
Sparse Core Ops, SparseCore 0:
  281.2 24.8 all-gather.2
  307.9 23.4 all-gather.4
  750.9 43.0 reduce-scatter.1
where the time goes:
time: 829 us; the launch traced here: 819 us
  local copies, waits for them, and re-layouts  222 us (27%)
  matrix products  221 us (27%)
  blocking collectives  196 us (24%)
  waiting for transfers between devices  135 us (16%)
  other arithmetic  21.2 us (3%)
  between operations  14.5 us (2%)
  starting transfers between devices  8.75 us (1%)
    convert_element_type x16, local copies, waits for them, and re-layouts, single_tile(): tensor_product_derivative = jnp.einsum('ijp,kp->ijk', grad_rows, outer_pa...  104 us
    all_to_all x1, blocking collectives, regroup(): lax.all_to_all(logit_tile, 'col', split_axis=1, concat_axis=2, tiled=True)  99.3 us
    all_to_all x1, blocking collectives, per_device(): lax.all_to_all(regroup(logits), ('row', 'col'), split_axis=2, concat_axis...  96.7 us
    dot_general x16, matrix products, single_tile(): jnp.einsum('tdpa,wad->wpt', tensor_product_derivative, right_all, preferr...  72.1 us
    dot_general x16, matrix products, single_tile(): jnp.einsum('ijp,kp->ijk', grad_rows, outer_pair_weight, preferred_element...  68.1 us
    dot_general x16, matrix products, single_tile(): jnp.einsum('ijce,scj->sei', tensor_product_derivative, left_all, preferre...  56.8 us
    unnamed x44, local copies, waits for them, and re-layouts  48.4 us
    reduce_scatter x1, waiting for transfers between devices, per_device(): lax.psum_scatter(partial_terms, 'col', scatter_dimension=0, tiled=True)  40.5 us
  transfers between devices with their start and end apart: 5, of which 5 were waited for; matrix products, arithmetic and copies ran while one was open for 1% of the time, Pallas kernels for 0%

commit v1 on v0

v1 whole, which is shorter than its diff:
```python
import functools

import jax
import jax.numpy as jnp
from jax import lax
from jax.experimental import pallas as pl
from jax.experimental.pallas import tpu as pltpu
from jax.sharding import PartitionSpec as P

BF16, F32 = jnp.bfloat16, jnp.float32
VMEM_BYTES = 56 * 1024 * 1024
AXES = ("row", "col")
GROUP = 4


def contract(lhs, rhs, lhs_dim, rhs_dim):
    return lax.dot_general(
        lhs, rhs, (((lhs_dim,), (rhs_dim,)), ((), ())), preferred_element_type=F32
    )


def relay(block, z, blocks):
    if blocks % 4:
        return z, block
    low_block = ((1 - (block & 1)) << 1) | (z & 1)
    low_z = (z & 2) | ((block >> 1) & 1)
    return (z >> 2 << 2) | low_block, (block >> 2 << 2) | low_z


def first_leg(blocks, parts):
    pairs = []
    for block in range(blocks):
        for z in range(blocks):
            to_block, to_z = relay(block, z, blocks)
            for h in range(parts):
                pairs.append(
                    ((block * parts + h) * blocks + z, (to_block * parts + h) * blocks + to_z)
                )
    return pairs


def second_leg(blocks, parts, shift):
    pairs = []
    for block in range(blocks):
        for z in range(blocks):
            via_block, via_z = relay(block, z, blocks)
            for h in range(parts):
                pairs.append(
                    (
                        (via_block * parts + h) * blocks + via_z,
                        (z * parts + (h + shift) % parts) * blocks + block,
                    )
                )
    return pairs


def mirror_logits_kernel(part_ref, pair_ref, weight_ref, bias_ref, out_ref, widened):
    own_rows, step_cols, width = pair_ref.shape
    widened[...] = pair_ref[...].astype(F32).reshape(own_rows * step_cols, width)
    weight = weight_ref[...]
    bias = bias_ref[...]
    for j in range(step_cols):
        column = widened[pl.ds(j, own_rows, stride=step_cols), :].astype(BF16)
        out_ref[j] = (contract(weight, column, 1, 1) + bias).astype(BF16)


def mirror_logits(part, pair_activation, weight_t, bias, chunk, chunks, shift, parts):
    rows, cols, width = pair_activation.shape
    bins = weight_t.shape[0]
    chunk_rows = rows // chunks
    step = min(16, chunk_rows)
    steps = chunk_rows // step

    def block(s, part_ref):
        half = lax.rem(part_ref[0] + shift, parts)
        return (0, half * (rows // step) + chunk * steps + s, 0)

    return pl.pallas_call(
        mirror_logits_kernel,
        grid_spec=pltpu.PrefetchScalarGridSpec(
            num_scalar_prefetch=1,
            grid=(steps,),
            in_specs=[
                pl.BlockSpec((rows, step, width), block),
                pl.BlockSpec((bins, width), lambda s, p: (0, 0)),
                pl.BlockSpec((bins, 1), lambda s, p: (0, 0)),
            ],
            out_specs=pl.BlockSpec((step, bins, rows), lambda s, p: (s, 0, 0)),
            scratch_shapes=[pltpu.VMEM((rows * step, width), F32)],
        ),
        out_shape=jax.ShapeDtypeStruct((chunk_rows, bins, rows), BF16),
        compiler_params=pltpu.CompilerParams(vmem_limit_bytes=VMEM_BYTES),
        cost_estimate=pl.CostEstimate(
            flops=2 * chunk_rows * rows * bins * width * 4,
            bytes_accessed=chunk_rows * rows * (width + bins) * 2,
            transcendentals=0,
        ),
        name="mirror_logits",
    )(part, pair_activation, weight_t, bias)


def pair_kernel(
    parts, part_ref, pair_ref, *refs
):
    received = refs[:parts]
    target_ref, weight_t_ref, weight_ref, bias_ref, factor_ref, mix_ref = refs[parts : parts + 6]
    grad_ref, norm_ref, slopes, mixed, total = refs[-5:]
    step = pl.program_id(0)
    steps = pl.num_programs(0)
    chunk_rows, cols, _ = pair_ref.shape
    bins = weight_t_ref.shape[0]
    own_rows = cols // parts
    groups = chunk_rows // GROUP
    seqs = norm_ref.shape[0]
    lanes = GROUP * norm_ref.shape[1] // chunk_rows
    xs = factor_ref.shape[0] // seqs

    @pl.when(step == 0)
    def _():
        h = part_ref[0]
        weight_t = weight_t_ref[...]
        weight = weight_ref[...]
        bias = bias_ref[...]
        levels = lax.broadcasted_iota(jnp.int32, (bins, cols), 0)
        for g in range(groups):
            for r in range(GROUP):
                i = g * GROUP + r
                own = (contract(weight_t, pair_ref[i], 1, 1) + bias).astype(BF16).astype(F32)
                halves = []
                for u in range(parts):
                    half = received[0][i]
                    for shift in range(1, parts):
                        half = jnp.where(lax.rem(h + parts - u, parts) == shift, received[shift][i], half)
                    halves.append(half)
                symmetric = own + jnp.concatenate(halves, axis=1).astype(F32)
                top = jnp.max(symmetric, axis=0, keepdims=True)
                raised = jnp.exp(symmetric - top)
                scale = 2.0 / jnp.sum(raised, axis=0, keepdims=True)
                hit = jnp.where(levels == target_ref[i : i + 1, :], 2.0, 0.0)
                slope = (raised * scale - hit).astype(BF16)
                slopes[g, r * bins : (r + 1) * bins, :] = slope
                grad_ref[i] = contract(slope, weight, 0, 1).astype(BF16)
        total[...] = jnp.zeros_like(total)

    factor = factor_ref[...]
    for g in range(groups):
        spread = contract(factor, slopes[g], 1, 1).astype(BF16)
        for x in range(xs):
            mixed[g * seqs : (g + 1) * seqs, x * GROUP * bins : (x + 1) * GROUP * bins] = (
                spread[x * seqs : (x + 1) * seqs, :]
            )
    total[...] += contract(mixed[...], mix_ref[...], 1, 0)

    @pl.when(step == steps - 1)
    def _():
        for g in range(groups):
            norm_ref[:, g * lanes : (g + 1) * lanes] = (
                total[g * seqs : (g + 1) * seqs, :].astype(BF16)
            )


def pair_step(
    part, pair_activation, received, targets, weight_t, weight, bias, factors, mix, grad, chunk,
    chunks, seqs, features, tile,
):
    rows, cols, width = pair_activation.shape
    bins = weight_t.shape[0]
    parts = len(received)
    chunk_rows = rows // chunks
    groups = chunk_rows // GROUP
    xs = factors.shape[0] // seqs
    steps = xs // tile
    const2 = lambda s, p: (0, 0)
    const3 = lambda s, p: (0, 0, 0)
    return pl.pallas_call(
        functools.partial(pair_kernel, parts),
        grid_spec=pltpu.PrefetchScalarGridSpec(
            num_scalar_prefetch=1,
            grid=(steps,),
            in_specs=[pl.BlockSpec((chunk_rows, cols, width), lambda s, p: (chunk, 0, 0))]
            + [pl.BlockSpec((chunk_rows, bins, cols // parts), const3)] * parts
            + [
                pl.BlockSpec((chunk_rows, cols), lambda s, p: (chunk, 0)),
                pl.BlockSpec((bins, width), const2),
                pl.BlockSpec((width, bins), const2),
                pl.BlockSpec((bins, 1), const2),
                pl.BlockSpec((tile * seqs, cols), lambda s, p: (s, 0)),
                pl.BlockSpec((tile * GROUP * bins, GROUP * features), lambda s, p: (s, 0)),
            ]
            + [pl.BlockSpec(memory_space=pl.ANY)] * len(grad),
            out_specs=[
                pl.BlockSpec((chunk_rows, cols, width), lambda s, p: (chunk, 0, 0)),
                pl.BlockSpec((seqs, chunk_rows * features), const2),
            ],
            scratch_shapes=[
                pltpu.VMEM((groups, GROUP * bins, cols), BF16),
                pltpu.VMEM((groups * seqs, tile * GROUP * bins), BF16),
                pltpu.VMEM((groups * seqs, GROUP * features), F32),
            ],
        ),
        out_shape=[
            jax.ShapeDtypeStruct(pair_activation.shape, BF16),
            jax.ShapeDtypeStruct((seqs, chunk_rows * features), BF16),
        ],
        input_output_aliases={parts + 8: 0} if grad else {},
        compiler_params=pltpu.CompilerParams(vmem_limit_bytes=VMEM_BYTES),
        cost_estimate=pl.CostEstimate(
            flops=4 * xs * seqs * cols * chunk_rows * bins,
            bytes_accessed=chunk_rows * cols * width * 6,
            transcendentals=chunk_rows * cols * bins,
        ),
        name="pair_step",
    )(part, pair_activation, *received, targets, weight_t, weight, bias, factors, mix, *grad)


def norm_forward(features):
    centered = features - jnp.mean(features, axis=0, keepdims=True)
    scale_inv = lax.rsqrt(jnp.mean(centered * centered, axis=0, keepdims=True) + 1e-05)
    return centered * scale_inv, scale_inv


def norm_backward(incoming, normed, scale_inv):
    first_mean = jnp.mean(incoming, axis=0, keepdims=True)
    second_mean = jnp.mean(incoming * normed, axis=0, keepdims=True)
    return scale_inv * (incoming - first_mean - normed * second_mean)


def transition_kernel(
    entry_ref, arriving_ref, incoming_ref, mean_gain_ref, gain_ref, gate_up_t_ref, gate_up_ref,
    down_ref, down_t_ref, out_ref,
):
    hidden = down_ref.shape[0]
    entry = entry_ref[0].astype(F32)
    normed, scale_inv = norm_forward(entry)
    gain = gain_ref[...]
    normed_input = (normed * gain).astype(BF16)
    both = contract(gate_up_t_ref[...], normed_input, 1, 0)
    gate, up = both[:hidden], both[hidden:]
    sig = jax.nn.sigmoid(gate)
    silu = gate * sig
    msa_out = entry + contract(down_t_ref[...], (silu * up).astype(BF16), 1, 0)
    second_normed, second_scale = norm_forward(msa_out)
    middle = arriving_ref[0].astype(F32) + norm_backward(
        incoming_ref[0].astype(F32) * mean_gain_ref[...], second_normed, second_scale
    )
    hidden_grad = contract(down_ref[...], middle.astype(BF16), 1, 0)
    gate_grad = (hidden_grad * up * sig * (1.0 + gate * (1.0 - sig))).astype(BF16)
    up_grad = (hidden_grad * silu).astype(BF16)
    normed_grad = contract(gate_up_ref[...], jnp.concatenate([gate_grad, up_grad], axis=0), 1, 0)
    out = middle + norm_backward(normed_grad * gain, normed, scale_inv)
    out_ref[0] = out.astype(BF16)


def transition(entry, arriving, incoming, mean_gain, gain, gate_weight, up_weight, down_weight):
    seqs, features, positions = entry.shape
    hidden = down_weight.shape[0]
    gate_up = jnp.concatenate([gate_weight, up_weight], axis=1)
    step = min(512, positions)
    field = pl.BlockSpec((1, features, step), lambda s, i: (s, 0, i))
    whole = lambda shape: pl.BlockSpec(shape, lambda s, i: (0, 0))
    return pl.pallas_call(
        transition_kernel,
        grid=(seqs, positions // step),
        in_specs=[field, field, field, whole((features, 1)), whole((features, 1)),
                  whole((2 * hidden, features)), whole((features, 2 * hidden)),
                  whole((hidden, features)), whole((features, hidden))],
        out_specs=field,
        out_shape=jax.ShapeDtypeStruct(entry.shape, BF16),
        compiler_params=pltpu.CompilerParams(vmem_limit_bytes=VMEM_BYTES),
        name="transition",
    )(entry, arriving, incoming, mean_gain[:, None], gain[:, None], gate_up.T, gate_up,
      down_weight, down_weight.T)


def per_device(
    pair_activation,
    target_distance_bins,
    distogram_weight,
    distogram_bias,
    outer_pair_weight,
    stored_lhs_operand,
    stored_rhs_operand,
    left_projection_weight,
    right_projection_weight,
    outer_mean_norm_gain,
    transition_norm_gain,
    gate_weight,
    up_weight,
    down_weight,
    side_stack_entry,
    arriving_stack_derivative,
):
    rows, cols, _ = pair_activation.shape
    width, bins = distogram_weight.shape
    factor_width = stored_lhs_operand.shape[1]
    features = left_projection_weight.shape[0]
    row_devices = lax.axis_size("row")
    col_devices = lax.axis_size("col")
    parts = row_devices // col_devices
    seqs = stored_lhs_operand.shape[0] * row_devices
    chunks = max(1, min(4, rows // 16))
    chunk_rows = rows // chunks
    part = (lax.axis_index("row") % parts).astype(jnp.int32)[None]
    weight_t = distogram_weight.T
    bias = distogram_bias[:, None]

    leg_pairs = first_leg(col_devices, parts)
    received = []
    landed = []
    for chunk in range(chunks):
        pieces = [
            mirror_logits(part, pair_activation, weight_t, bias, chunk, chunks, shift, parts)
            for shift in range(parts)
        ]
        if chunk >= 2:
            *pieces, _ = lax.optimization_barrier((*pieces, landed[chunk - 2][0]))
        relayed = [lax.ppermute(piece, AXES, leg_pairs) for piece in pieces]
        landed.append(relayed)
        received.append(
            [
                lax.ppermute(piece, AXES, second_leg(col_devices, parts, shift))
                for shift, piece in enumerate(relayed)
            ]
        )

    left_all = lax.all_gather(stored_lhs_operand, "row", axis=0, tiled=True)
    right_all = lax.all_gather(stored_rhs_operand, "row", axis=0, tiled=True)
    factors = jnp.concatenate(
        [jnp.swapaxes(right_all, 0, 1), jnp.swapaxes(left_all, 0, 1)], axis=0
    ).reshape(2 * factor_width * seqs, cols)

    outer_weight = outer_pair_weight.astype(F32).reshape(factor_width, factor_width, width)
    by_bin = jnp.einsum(
        "pb,cep->bce", distogram_weight.astype(F32), outer_weight, precision=lax.Precision.HIGHEST
    )
    mix_right = jnp.einsum(
        "mc,bce->ebm", left_projection_weight.astype(F32), by_bin, precision=lax.Precision.HIGHEST
    )
    mix_left = jnp.einsum(
        "me,bce->cbm", right_projection_weight.astype(F32), by_bin, precision=lax.Precision.HIGHEST
    )
    mix = (jnp.concatenate([mix_right, mix_left], axis=0) / seqs).astype(BF16)
    same = jnp.eye(GROUP, dtype=BF16)
    mix = (mix[:, None, :, None, :] * same[None, :, None, :, None]).reshape(
        2 * factor_width * GROUP * bins, GROUP * features
    )

    grad = None
    tile = max(1, min(8, 512 // seqs))
    fields = []
    for chunk in range(chunks):
        grad, norm_part = pair_step(
            part, pair_activation, received[chunk], target_distance_bins, weight_t,
            distogram_weight, bias, factors, mix, () if grad is None else (grad,), chunk, chunks,
            seqs, features, tile,
        )
        parts_in = lax.all_to_all(norm_part, AXES, split_axis=0, concat_axis=0, tiled=True)
        fields.append(
            parts_in.reshape(row_devices, col_devices, -1, chunk_rows, features)
            .astype(F32)
            .sum(axis=1)
        )
    incoming = jnp.stack(fields).astype(BF16).transpose(2, 4, 1, 0, 3)
    incoming = incoming.reshape(side_stack_entry.shape)
    alignment_gradient = transition(
        side_stack_entry, arriving_stack_derivative, incoming, outer_mean_norm_gain,
        transition_norm_gain, gate_weight, up_weight, down_weight,
    )
    return grad, alignment_gradient


def solution(mesh):
    return jax.shard_map(
        per_device,
        mesh=mesh,
        in_specs=(
            P("row", "col", None),
            P("row", "col"),
            P(),
            P(),
            P(),
            P("row", None, "col"),
            P("row", None, "col"),
            P(),
            P(),
            P(),
            P(),
            P(),
            P(),
            P(),
            P(AXES, None, None),
            P(AXES, None, None),
        ),
        out_specs=(P("row", "col", None), P(AXES, None, None)),
        check_vma=False,
    )
```

time: 829 us -> 334 us (0.40); the launches traced: 819 us -> 333 us
  matrix products: 221 us -> 2.38 us
  blocking collectives: 196 us -> 0 us
  local copies, waits for them, and re-layouts: 222 us -> 41.5 us
  Pallas kernels: 0 us -> 125 us
  waiting for transfers between devices: 135 us -> 54.1 us
  starting transfers between devices: 8.75 us -> 84.1 us
  other arithmetic: 21.2 us -> 11.4 us
    dot_general x57 -> x3, matrix products: 221 us -> 2.38 us  [the longest x1 1.16 us: per_device(): jnp.einsum('mc,bce->ebm', left_projection_weight.astype(F32), by_bin, pre...]
    all_to_all x2 -> x0, blocking collectives: 196 us -> none  [the longest x1 99.3 us: regroup(): lax.all_to_all(logit_tile, 'col', split_axis=1, concat_axis=2, tiled=True)]
    pallas_call x0 -> x13, Pallas kernels: none -> 125 us  [the longest x4 95.5 us: pair_step(): pl.pallas_call(functools.partial(pair_kernel, parts), grid_spec=pltpu.Pre...]
    convert_element_type x18 -> x4, local copies, waits for them, and re-layouts: 121 us -> 1.4 us  [per_device(): fields.append(parts_in.reshape(row_devices, col_devices, -1, chunk_rows,...]
    ppermute x0 -> x16, starting transfers between devices: none -> 65.4 us  [the longest x8 54.9 us: per_device(): lax.ppermute(piece, AXES, second_leg(col_devices, parts, shift))]
    all_gather x2, waiting for transfers between devices: 48.3 us -> 2.45 us  [the longest x1 2.43 us: per_device(): left_all = lax.all_gather(stored_lhs_operand, 'row', axis=0, tiled=True)]
    unnamed x44 -> x51, local copies, waits for them, and re-layouts: 48.4 us -> 4.25 us
    reduce_scatter x1 -> x0, waiting for transfers between devices: 40.5 us -> none  [per_device(): lax.psum_scatter(partial_terms, 'col', scatter_dimension=0, tiled=True)]
  transfers between devices with their start and end apart: 5 -> 22, of which waited for: 5 -> 7; matrix products, arithmetic and copies ran while one was open for 1% -> 14% of each run, Pallas kernels for 0% -> 28%
where the time goes in v1:
time: 334 us; the launch traced here: 333 us
  Pallas kernels  125 us (37%)
  starting transfers between devices  84.1 us (25%)
  waiting for transfers between devices  54.1 us (16%)
  local copies, waits for them, and re-layouts  41.5 us (12%)
  between operations  14.4 us (4%)
  other arithmetic  11.4 us (3%)
    pallas_call x4, Pallas kernels, pair_step(): pl.pallas_call(functools.partial(pair_kernel, parts), grid_spec=pltpu.Pre...  95.5 us
    ppermute x8, starting transfers between devices, per_device(): lax.ppermute(piece, AXES, second_leg(col_devices, parts, shift))  54.9 us
    all_to_all x4, waiting for transfers between devices, per_device(): lax.all_to_all(norm_part, AXES, split_axis=0, concat_axis=0, tiled=True)  33.4 us
    mul x1, local copies, waits for them, and re-layouts, per_device(): mix[:, None, :, None, :] * same[None, :, None, :, None]  24.3 us
    pallas_call x8, Pallas kernels, mirror_logits(): pl.pallas_call(mirror_logits_kernel, grid_spec=pltpu.PrefetchScalarGridSp...  23.2 us
    all_to_all x4, starting transfers between devices, per_device(): lax.all_to_all(norm_part, AXES, split_axis=0, concat_axis=0, tiled=True)  18.6 us
    ppermute x8, waiting for transfers between devices, per_device(): relayed = [lax.ppermute(piece, AXES, leg_pairs) for piece in pieces]  17.5 us
    ppermute x8, starting transfers between devices, per_device(): relayed = [lax.ppermute(piece, AXES, leg_pairs) for piece in pieces]  10.5 us
  transfers between devices with their start and end apart: 22, of which 7 were waited for; matrix products, arithmetic and copies ran while one was open for 14% of the time, Pallas kernels for 28%

profile of v1, /device:TPU:0, one launch (start us, length us, event | category | flops | bytes accessed | tf_op | source)
XLA Modules:
  0.0 332.9 jit_solution(593588712112709988)
XLA Ops:
  12.2 3.0 collective-permute-start.5
  15.2 2.9 mirror_logits.15
  19.6 2.9 mirror_logits.10
  24.1 2.9 mirror_logits.14
  30.3 4.2 %collective-permute-start.13 = (bf16[32,64,128]{2,1,0:T(8,128)(2,1)}, bf16[32,64,128]{2,1,0:T(8,128)(2,1)}, u32[]{:S(2)}, u32[]{:S(2)}) collective-permute-start(bf16[32,64,128]{2,1,0:T(8,128)(2,1)} %collective-permute-done.5), channel_id=1, source_target_pairs={{16,0},{20,4},{24,8},{28,12},{18,16},{22,20},{26,24},{30,28},{0,1}... | collective-permute-start | bytes 1572872 | tf_op jit(solution)/shard_map/ppermute | solution.py:321
  34.5 6.2 %collective-permute-done.14 = bf16[32,64,128]{2,1,0:T(8,128)(2,1)S(1)} collective-permute-done((bf16[32,64,128]{2,1,0:T(8,128)(2,1)}, bf16[32,64,128]{2,1,0:T(8,128)(2,1)S(1)}, u32[]{:S(2)}, u32[]{:S(2)}) %collective-permute-start.14) | collective-permute-done | bytes 524320 | tf_op jit(solution)/shard_map/ppermute | solution.py:317
  40.7 11.2 %collective-permute-done = bf16[32,64,128]{2,1,0:T(8,128)(2,1)S(1)} collective-permute-done((bf16[32,64,128]{2,1,0:T(8,128)(2,1)}, bf16[32,64,128]{2,1,0:T(8,128)(2,1)S(1)}, u32[]{:S(2)}, u32[]{:S(2)}) %collective-permute-start) | collective-permute-done | bytes 524320 | tf_op jit(solution)/shard_map/ppermute | solution.py:317
  54.7 8.6 %broadcast_multiply_fusion = bf16[64,4,64,4,64]{4,3,2,1,0:T(4,128)(2,1)} fusion(bf16[4,4]{1,0:T(4,128)(2,1)S(1)} %fusion.6, bf16[64,64,64]{2,1,0:T(8,128)(2,1)S(1)} %fusion), kind=kLoop, calls=%fused_computation | loop fusion | flops 4194304 | bytes 8912928 | tf_op jit(solution)/shard_map/mul | solution.py:344
  64.0 24.3 %mul.20.refs_7_ = bf16[16384,256]{1,0:T(8,128)(2,1)} reshape(bf16[64,4,64,4,64]{4,3,2,1,0:T(4,128)(2,1)} %broadcast_multiply_fusion) | data formatting | bytes 16777216 | tf_op jit(solution)/shard_map/mul | solution.py:344
  88.3 2.9 mirror_logits.11
  94.1 2.9 mirror_logits.8
  97.0 3.0 mirror_logits.9
  112.3 23.9 %pair_step.4 = (bf16[128,256,128]{2,1,0:T(8,128)(2,1)}, bf16[64,2048]{1,0:T(8,128)(2,1)}) custom-call(s32[1]{0:T(128)} %bitcast.part_ref, bf16[128,256,128]{2,1,0:T(8,128)(2,1)} %pair_ref.23, bf16[32,64,128]{2,1,0:T(8,128)(2,1)} %collective-permute-done.13.refs_0_, bf16[32,64,128]{2,1,0:T(8,128)(2,1)} %collective-permute-done.15.refs_1_, ...), custom_call_target="tpu_custom_call" | custom-call | flops 8589934592 | bytes 6291456 | tf_op jit(solution)/shard_map/pair_step/pallas_call | solution.py:175
  138.9 41.7 %collective-permute-start.9 = (bf16[32,64,128]{2,1,0:T(8,128)(2,1)S(1)}, bf16[32,64,128]{2,1,0:T(8,128)(2,1)S(1)}, u32[]{:S(2)}, u32[]{:S(2)}) collective-permute-start(bf16[32,64,128]{2,1,0:T(8,128)(2,1)S(1)} %collective-permute-done.8), channel_id=1, source_target_pairs={{16,4},{20,0},{24,12},{28,8},{18,20},{22,16},{26,28},{30,24},{0,5}... | collective-permute-start | bytes 1572872 | tf_op jit(solution)/shard_map/ppermute | solution.py:321
  183.4 23.9 %pair_step.5 = (bf16[128,256,128]{2,1,0:T(8,128)(2,1)}, bf16[64,2048]{1,0:T(8,128)(2,1)}) custom-call(s32[1]{0:T(128)} %bitcast.part_ref, bf16[128,256,128]{2,1,0:T(8,128)(2,1)} %pair_ref.23, bf16[32,64,128]{2,1,0:T(8,128)(2,1)} %copy-done.18, bf16[32,64,128]{2,1,0:T(8,128)(2,1)} %copy-done.20, ...), custom_call_target="tpu_custom_call", output_to_operand_aliasing={{0}: (10, {})} | custom-call | flops 8589934592 | bytes 6291456 | tf_op jit(solution)/shard_map/pair_step/pallas_call | solution.py:175
  208.2 23.8 %pair_step.6 = (bf16[128,256,128]{2,1,0:T(8,128)(2,1)}, bf16[64,2048]{1,0:T(8,128)(2,1)}) custom-call(s32[1]{0:T(128)} %bitcast.part_ref, bf16[128,256,128]{2,1,0:T(8,128)(2,1)} %pair_ref.23, bf16[32,64,128]{2,1,0:T(8,128)(2,1)} %copy-done.21, bf16[32,64,128]{2,1,0:T(8,128)(2,1)} %copy-done.23, ...), custom_call_target="tpu_custom_call", output_to_operand_aliasing={{0}: (10, {})} | custom-call | flops 8589934592 | bytes 6291456 | tf_op jit(solution)/shard_map/pair_step/pallas_call | solution.py:175
  233.1 23.9 %pair_step.7 = (bf16[128,256,128]{2,1,0:T(8,128)(2,1)}, bf16[64,2048]{1,0:T(8,128)(2,1)}) custom-call(s32[1]{0:T(128)} %bitcast.part_ref, bf16[128,256,128]{2,1,0:T(8,128)(2,1)} %pair_ref.23, bf16[32,64,128]{2,1,0:T(8,128)(2,1)} %copy-done.19, bf16[32,64,128]{2,1,0:T(8,128)(2,1)} %copy-done.22, ...), custom_call_target="tpu_custom_call", output_to_operand_aliasing={{0}: (10, {})} | custom-call | flops 8589934592 | bytes 6291456 | tf_op jit(solution)/shard_map/pair_step/pallas_call | solution.py:175
  258.9 10.2 %all-to-all-start.3 = ((bf16[32,2,2048]{2,1,0:T(2,128)(2,1)}), bf16[32,2,2048]{2,1,0:T(2,128)(2,1)S(1)}, u32[]{:S(2)}, u32[]{:S(2)}) async-start(bf16[32,2,2048]{2,1,0:T(2,128)(2,1)} %all_to_all.30), calls=%async_computation.3 | async-start | bytes 524288 | tf_op jit(solution)/shard_map/all_to_all | solution.py:357
  270.1 9.3 %all-to-all-done.3 = bf16[32,2,2048]{2,1,0:T(2,128)(2,1)S(1)} async-done(((bf16[32,2,2048]{2,1,0:T(2,128)(2,1)}), bf16[32,2,2048]{2,1,0:T(2,128)(2,1)S(1)}, u32[]{:S(2)}, u32[]{:S(2)}) %all-to-all-start.3) | async-done | bytes 262176 | tf_op jit(solution)/shard_map/all_to_all | solution.py:357
  283.0 9.3 %all-to-all-done.2 = bf16[32,2,2048]{2,1,0:T(2,128)(2,1)S(1)} async-done(((bf16[32,2,2048]{2,1,0:T(2,128)(2,1)}), bf16[32,2,2048]{2,1,0:T(2,128)(2,1)S(1)}, u32[]{:S(2)}, u32[]{:S(2)}) %all-to-all-start.2) | async-done | bytes 262176 | tf_op jit(solution)/shard_map/all_to_all | solution.py:357
  295.9 9.3 %all-to-all-done.1 = bf16[32,2,2048]{2,1,0:T(2,128)(2,1)S(1)} async-done(((bf16[32,2,2048]{2,1,0:T(2,128)(2,1)}), bf16[32,2,2048]{2,1,0:T(2,128)(2,1)S(1)}, u32[]{:S(2)}, u32[]{:S(2)}) %all-to-all-start.1) | async-done | bytes 262176 | tf_op jit(solution)/shard_map/all_to_all | solution.py:357
  305.2 2.9 all-to-all-start
  312.6 5.6 %all-to-all-done = bf16[32,2,2048]{2,1,0:T(2,128)(2,1)S(1)} async-done(((bf16[32,2,2048]{2,1,0:T(2,128)(2,1)}), bf16[32,2,2048]{2,1,0:T(2,128)(2,1)S(1)}, u32[]{:S(2)}, u32[]{:S(2)}) %all-to-all-start) | async-done | bytes 262176 | tf_op jit(solution)/shard_map/all_to_all | solution.py:357
  319.7 6.3 %transition.1 = bf16[2,64,1024]{2,1,0:T(8,128)(2,1)} custom-call(bf16[2,64,1024]{2,1,0:T(8,128)(2,1)} %entry_ref.1, bf16[2,64,1024]{2,1,0:T(8,128)(2,1)} %arriving_ref.1, bf16[2,64,1024]{2,1,0:T(8,128)(2,1)} %copy.86.incoming_ref, f32[64,1]{1,0:T(8,128)} %copy.87.mean_gain_ref, f32[64,1]{1,0:T(8,128)} %copy.88.gain_ref, bf16[512,64]{1,0:T(8,128)(2,1)} %copy.89.gate_up_t_ref, ...), custom_call_target="tpu_custom_call" | custom-call | tf_op jit(solution)/shard_map/transition/pallas_call | solution.py:261
  (115 shorter events, 53.4 us)
Async XLA Ops:
  7.2 92.8 %all-gather.3.cloned.1.call-start = ((), (), s32[]{:S(2)}) async-start(), calls=%async_computation.4 | async-start | bytes 1179648 | tf_op jit(solution)/shard_map/all_gather | solution.py:327
  7.9 94.5 %all-gather.5.cloned.1.call-start = ((), (), s32[]{:S(2)}) async-start(), calls=%async_computation.5 | async-start | bytes 1179648 | tf_op jit(solution)/shard_map/all_gather | solution.py:326
  12.2 18.1 %collective-permute-start.5 = (bf16[32,64,128]{2,1,0:T(8,128)(2,1)}, bf16[32,64,128]{2,1,0:T(8,128)(2,1)}, u32[]{:S(2)}, u32[]{:S(2)}) collective-permute-start(bf16[32,64,128]{2,1,0:T(8,128)(2,1)} %mirror_logits.13), channel_id=1, source_target_pairs={{0,16},{4,20},{1,24},{5,28},{2,18},{6,22},{3,26},{7,30},{8,0},{12,... | collective-permute-start | bytes 1572872 | tf_op jit(solution)/shard_map/ppermute | solution.py:317
  18.1 22.7 %collective-permute-start.14 = (bf16[32,64,128]{2,1,0:T(8,128)(2,1)}, bf16[32,64,128]{2,1,0:T(8,128)(2,1)S(1)}, u32[]{:S(2)}, u32[]{:S(2)}) collective-permute-start(bf16[32,64,128]{2,1,0:T(8,128)(2,1)} %mirror_logits.15), channel_id=1, source_target_pairs={{0,16},{4,20},{1,24},{5,28},{2,18},{6,22},{3,26},{7,30},{8,0},{12,... | collective-permute-start | bytes 1572872 | tf_op jit(solution)/shard_map/ppermute | solution.py:317
  22.5 29.4 %collective-permute-start = (bf16[32,64,128]{2,1,0:T(8,128)(2,1)}, bf16[32,64,128]{2,1,0:T(8,128)(2,1)S(1)}, u32[]{:S(2)}, u32[]{:S(2)}) collective-permute-start(bf16[32,64,128]{2,1,0:T(8,128)(2,1)} %mirror_logits.10), channel_id=1, source_target_pairs={{0,16},{4,20},{1,24},{5,28},{2,18},{6,22},{3,26},{7,30},{8,0},{12,... | collective-permute-start | bytes 1572872 | tf_op jit(solution)/shard_map/ppermute | solution.py:317
  27.0 79.8 %collective-permute-start.11 = (bf16[32,64,128]{2,1,0:T(8,128)(2,1)}, bf16[32,64,128]{2,1,0:T(8,128)(2,1)S(1)}, u32[]{:S(2)}, u32[]{:S(2)}) collective-permute-start(bf16[32,64,128]{2,1,0:T(8,128)(2,1)} %mirror_logits.14), channel_id=1, source_target_pairs={{0,16},{4,20},{1,24},{5,28},{2,18},{6,22},{3,26},{7,30},{8,0},{12,... | collective-permute-start | bytes 1572872 | tf_op jit(solution)/shard_map/ppermute | solution.py:317
  30.3 77.6 %collective-permute-start.13 = (bf16[32,64,128]{2,1,0:T(8,128)(2,1)}, bf16[32,64,128]{2,1,0:T(8,128)(2,1)}, u32[]{:S(2)}, u32[]{:S(2)}) collective-permute-start(bf16[32,64,128]{2,1,0:T(8,128)(2,1)} %collective-permute-done.5), channel_id=1, source_target_pairs={{16,0},{20,4},{24,8},{28,12},{18,16},{22,20},{26,24},{30,28},{0,1}... | collective-permute-start | bytes 1572872 | tf_op jit(solution)/shard_map/ppermute | solution.py:321
  40.7 68.7 %collective-permute-start.15 = (bf16[32,64,128]{2,1,0:T(8,128)(2,1)S(1)}, bf16[32,64,128]{2,1,0:T(8,128)(2,1)}, u32[]{:S(2)}, u32[]{:S(2)}) collective-permute-start(bf16[32,64,128]{2,1,0:T(8,128)(2,1)S(1)} %collective-permute-done.14), channel_id=1, source_target_pairs={{16,4},{20,0},{24,12},{28,8},{18,20},{22,16},{26,28},{30,24},{0,5}... | collective-permute-start | bytes 1572872 | tf_op jit(solution)/shard_map/ppermute | solution.py:321
  52.0 58.8 %collective-permute-start.10 = (bf16[32,64,128]{2,1,0:T(8,128)(2,1)S(1)}, bf16[32,64,128]{2,1,0:T(8,128)(2,1)S(1)}, u32[]{:S(2)}, u32[]{:S(2)}) collective-permute-start(bf16[32,64,128]{2,1,0:T(8,128)(2,1)S(1)} %collective-permute-done), channel_id=1, source_target_pairs={{16,0},{20,4},{24,8},{28,12},{18,16},{22,20},{26,24},{30,28},{0,1}... | collective-permute-start | bytes 1572872 | tf_op jit(solution)/shard_map/ppermute | solution.py:321
  99.9 36.2 %collective-permute-start.6 = (bf16[32,64,128]{2,1,0:T(8,128)(2,1)S(1)}, bf16[32,64,128]{2,1,0:T(8,128)(2,1)S(1)}, u32[]{:S(2)}, u32[]{:S(2)}) collective-permute-start(bf16[32,64,128]{2,1,0:T(8,128)(2,1)S(1)} %copy-done.6), channel_id=1, source_target_pairs={{0,16},{4,20},{1,24},{5,28},{2,18},{6,22},{3,26},{7,30},{8,0},{12,... | collective-permute-start | bytes 1572872 | tf_op jit(solution)/shard_map/ppermute | solution.py:317
  106.8 32.0 %collective-permute-start.8 = (bf16[32,64,128]{2,1,0:T(8,128)(2,1)S(1)}, bf16[32,64,128]{2,1,0:T(8,128)(2,1)S(1)}, u32[]{:S(2)}, u32[]{:S(2)}) collective-permute-start(bf16[32,64,128]{2,1,0:T(8,128)(2,1)S(1)} %copy-done.5), channel_id=1, source_target_pairs={{0,16},{4,20},{1,24},{5,28},{2,18},{6,22},{3,26},{7,30},{8,0},{12,... | collective-permute-start | bytes 1572872 | tf_op jit(solution)/shard_map/ppermute | solution.py:317
  107.9 72.6 %collective-permute-start.1 = (bf16[32,64,128]{2,1,0:T(8,128)(2,1)S(1)}, bf16[32,64,128]{2,1,0:T(8,128)(2,1)S(1)}, u32[]{:S(2)}, u32[]{:S(2)}) collective-permute-start(bf16[32,64,128]{2,1,0:T(8,128)(2,1)S(1)} %copy-done.4), channel_id=1, source_target_pairs={{0,16},{4,20},{1,24},{5,28},{2,18},{6,22},{3,26},{7,30},{8,0},{12,... | collective-permute-start | bytes 1572872 | tf_op jit(solution)/shard_map/ppermute | solution.py:317
  109.5 73.1 %collective-permute-start.3 = (bf16[32,64,128]{2,1,0:T(8,128)(2,1)S(1)}, bf16[32,64,128]{2,1,0:T(8,128)(2,1)S(1)}, u32[]{:S(2)}, u32[]{:S(2)}) collective-permute-start(bf16[32,64,128]{2,1,0:T(8,128)(2,1)S(1)} %copy-done.3), channel_id=1, source_target_pairs={{0,16},{4,20},{1,24},{5,28},{2,18},{6,22},{3,26},{7,30},{8,0},{12,... | collective-permute-start | bytes 1572872 | tf_op jit(solution)/shard_map/ppermute | solution.py:317
  110.7 71.8 %collective-permute-start.12 = (bf16[32,64,128]{2,1,0:T(8,128)(2,1)S(1)}, bf16[32,64,128]{2,1,0:T(8,128)(2,1)S(1)}, u32[]{:S(2)}, u32[]{:S(2)}) collective-permute-start(bf16[32,64,128]{2,1,0:T(8,128)(2,1)S(1)} %collective-permute-done.11), channel_id=1, source_target_pairs={{16,4},{20,0},{24,12},{28,8},{18,20},{22,16},{26,28},{30,24},{0,5}... | collective-permute-start | bytes 1572872 | tf_op jit(solution)/shard_map/ppermute | solution.py:321
  136.2 71.1 %collective-permute-start.7 = (bf16[32,64,128]{2,1,0:T(8,128)(2,1)S(1)}, bf16[32,64,128]{2,1,0:T(8,128)(2,1)S(1)}, u32[]{:S(2)}, u32[]{:S(2)}) collective-permute-start(bf16[32,64,128]{2,1,0:T(8,128)(2,1)S(1)} %collective-permute-done.6), channel_id=1, source_target_pairs={{16,0},{20,4},{24,8},{28,12},{18,16},{22,20},{26,24},{30,28},{0,1}... | collective-permute-start | bytes 1572872 | tf_op jit(solution)/shard_map/ppermute | solution.py:321
  138.9 68.4 %collective-permute-start.9 = (bf16[32,64,128]{2,1,0:T(8,128)(2,1)S(1)}, bf16[32,64,128]{2,1,0:T(8,128)(2,1)S(1)}, u32[]{:S(2)}, u32[]{:S(2)}) collective-permute-start(bf16[32,64,128]{2,1,0:T(8,128)(2,1)S(1)} %collective-permute-done.8), channel_id=1, source_target_pairs={{16,4},{20,0},{24,12},{28,8},{18,20},{22,16},{26,28},{30,24},{0,5}... | collective-permute-start | bytes 1572872 | tf_op jit(solution)/shard_map/ppermute | solution.py:321
  180.5 51.5 %collective-permute-start.2 = (bf16[32,64,128]{2,1,0:T(8,128)(2,1)S(1)}, bf16[32,64,128]{2,1,0:T(8,128)(2,1)S(1)}, u32[]{:S(2)}, u32[]{:S(2)}) collective-permute-start(bf16[32,64,128]{2,1,0:T(8,128)(2,1)S(1)} %collective-permute-done.1), channel_id=1, source_target_pairs={{16,0},{20,4},{24,8},{28,12},{18,16},{22,20},{26,24},{30,28},{0,1}... | collective-permute-start | bytes 1572872 | tf_op jit(solution)/shard_map/ppermute | solution.py:321
  182.5 49.5 %collective-permute-start.4 = (bf16[32,64,128]{2,1,0:T(8,128)(2,1)S(1)}, bf16[32,64,128]{2,1,0:T(8,128)(2,1)S(1)}, u32[]{:S(2)}, u32[]{:S(2)}) collective-permute-start(bf16[32,64,128]{2,1,0:T(8,128)(2,1)S(1)} %collective-permute-done.3), channel_id=1, source_target_pairs={{16,4},{20,0},{24,12},{28,8},{18,20},{22,16},{26,28},{30,24},{0,5}... | collective-permute-start | bytes 1572872 | tf_op jit(solution)/shard_map/ppermute | solution.py:321
  233.0 62.0 %copy-start.8 = (bf16[64,2048]{1,0:T(8,128)(2,1)S(1)}, bf16[64,2048]{1,0:T(8,128)(2,1)}, u32[]{:S(2)}) copy-start(bf16[64,2048]{1,0:T(8,128)(2,1)} %get-tuple-element.22) | copy-start | bytes 786436
  257.0 53.4 %copy-start.17 = (f32[64]{0:T(128)S(1)}, f32[64]{0:T(128)}, u32[]{:S(2)}) copy-start(f32[64]{0:T(128)} %param.26) | copy-start | bytes 772
  258.9 20.4 %all-to-all-start.3 = ((bf16[32,2,2048]{2,1,0:T(2,128)(2,1)}), bf16[32,2,2048]{2,1,0:T(2,128)(2,1)S(1)}, u32[]{:S(2)}, u32[]{:S(2)}) async-start(bf16[32,2,2048]{2,1,0:T(2,128)(2,1)} %all_to_all.30), calls=%async_computation.3 | async-start | bytes 524288 | tf_op jit(solution)/shard_map/all_to_all | solution.py:357
  279.3 12.9 %all-to-all-start.2 = ((bf16[32,2,2048]{2,1,0:T(2,128)(2,1)}), bf16[32,2,2048]{2,1,0:T(2,128)(2,1)S(1)}, u32[]{:S(2)}, u32[]{:S(2)}) async-start(bf16[32,2,2048]{2,1,0:T(2,128)(2,1)} %all_to_all.28), calls=%async_computation.2 | async-start | bytes 524288 | tf_op jit(solution)/shard_map/all_to_all | solution.py:357
  292.3 12.9 %all-to-all-start.1 = ((bf16[32,2,2048]{2,1,0:T(2,128)(2,1)}), bf16[32,2,2048]{2,1,0:T(2,128)(2,1)S(1)}, u32[]{:S(2)}, u32[]{:S(2)}) async-start(bf16[32,2,2048]{2,1,0:T(2,128)(2,1)} %all_to_all.26), calls=%async_computation.1 | async-start | bytes 524288 | tf_op jit(solution)/shard_map/all_to_all | solution.py:357
  305.2 12.9 %all-to-all-start = ((bf16[32,2,2048]{2,1,0:T(2,128)(2,1)}), bf16[32,2,2048]{2,1,0:T(2,128)(2,1)S(1)}, u32[]{:S(2)}, u32[]{:S(2)}) async-start(bf16[32,2,2048]{2,1,0:T(2,128)(2,1)} %all_to_all.24), calls=%async_computation | async-start | bytes 524288 | tf_op jit(solution)/shard_map/all_to_all | solution.py:357
  (22 other events, 404.9 us)
Sparse Core Ops, SparseCore 0:
  9.9 66.7 all-gather.2
  78.6 23.8 all-gather.4

commit v2 on v1

v2 whole, which is shorter than its diff:
```python
import functools

import jax
import jax.numpy as jnp
from jax import lax
from jax.experimental import pallas as pl
from jax.experimental.pallas import tpu as pltpu
from jax.sharding import PartitionSpec as P

BF16, F32 = jnp.bfloat16, jnp.float32
VMEM_BYTES = 56 * 1024 * 1024
AXES = ("row", "col")
GROUP = 4


def contract(lhs, rhs, lhs_dim, rhs_dim):
    return lax.dot_general(
        lhs, rhs, (((lhs_dim,), (rhs_dim,)), ((), ())), preferred_element_type=F32
    )


def relay(block, z, blocks):
    if blocks % 4:
        return z, block
    low_block = ((1 - (block & 1)) << 1) | (z & 1)
    low_z = (z & 2) | ((block >> 1) & 1)
    return (z >> 2 << 2) | low_block, (block >> 2 << 2) | low_z


def first_leg(blocks, parts):
    pairs = []
    for block in range(blocks):
        for z in range(blocks):
            to_block, to_z = relay(block, z, blocks)
            for h in range(parts):
                pairs.append(
                    ((block * parts + h) * blocks + z, (to_block * parts + h) * blocks + to_z)
                )
    return pairs


def second_leg(blocks, parts, shift):
    pairs = []
    for block in range(blocks):
        for z in range(blocks):
            via_block, via_z = relay(block, z, blocks)
            for h in range(parts):
                pairs.append(
                    (
                        (via_block * parts + h) * blocks + via_z,
                        (z * parts + (h + shift) % parts) * blocks + block,
                    )
                )
    return pairs


def mirror_logits_kernel(part_ref, pair_ref, weight_ref, bias_ref, out_ref, widened):
    own_rows, step_cols, width = pair_ref.shape
    widened[...] = pair_ref[...].astype(F32).reshape(own_rows * step_cols, width)
    weight = weight_ref[...]
    bias = bias_ref[...]
    for j in range(step_cols):
        column = widened[pl.ds(j, own_rows, stride=step_cols), :].astype(BF16)
        out_ref[j] = (contract(weight, column, 1, 1) + bias).astype(BF16)


def mirror_logits(part, pair_activation, weight_t, bias, first_row, chunk_rows, shift, parts):
    rows, cols, width = pair_activation.shape
    bins = weight_t.shape[0]
    step = min(16, chunk_rows)
    steps = chunk_rows // step

    def block(s, part_ref):
        half = lax.rem(part_ref[0] + shift, parts)
        return (0, half * (rows // step) + first_row // step + s, 0)

    return pl.pallas_call(
        mirror_logits_kernel,
        grid_spec=pltpu.PrefetchScalarGridSpec(
            num_scalar_prefetch=1,
            grid=(steps,),
            in_specs=[
                pl.BlockSpec((rows, step, width), block),
                pl.BlockSpec((bins, width), lambda s, p: (0, 0)),
                pl.BlockSpec((bins, 1), lambda s, p: (0, 0)),
            ],
            out_specs=pl.BlockSpec((step, bins, rows), lambda s, p: (s, 0, 0)),
            scratch_shapes=[pltpu.VMEM((rows * step, width), F32)],
        ),
        out_shape=jax.ShapeDtypeStruct((chunk_rows, bins, rows), BF16),
        compiler_params=pltpu.CompilerParams(vmem_limit_bytes=VMEM_BYTES),
        cost_estimate=pl.CostEstimate(
            flops=2 * chunk_rows * rows * bins * width * 4,
            bytes_accessed=chunk_rows * rows * (width + bins) * 2,
            transcendentals=0,
        ),
        name="mirror_logits",
    )(part, pair_activation, weight_t, bias)


def pair_kernel(parts, front, tile, part_ref, pair_ref, *refs):
    received = refs[:parts]
    target_ref, weight_t_ref, weight_wide_ref, bias_ref, factor_hbm, mix_hbm = refs[parts : parts + 6]
    grad_ref, norm_ref, slopes, factors, mix, mix_wide, mixed, total, sems = refs[-9:]
    step = pl.program_id(0)
    step_rows, cols, width = pair_ref.shape
    bins = weight_t_ref.shape[0]
    groups = slopes.shape[0]
    step_groups = step_rows // GROUP
    features = total.shape[0] * total.shape[2] // GROUP
    devices, device_rows, _ = norm_ref.shape
    device_seqs = device_rows // groups
    seqs = devices * device_seqs
    xs = mix.shape[0]
    copies = [
        pltpu.make_async_copy(factor_hbm, factors, sems.at[0]),
        pltpu.make_async_copy(mix_hbm, mix, sems.at[1]),
    ]

    @pl.when(step == 0)
    def _():
        for copy in copies:
            copy.start()
        total[...] = jnp.zeros_like(total)
        mix_wide[...] = jnp.zeros_like(mix_wide)

    @pl.when(step < front)
    def _():
        h = part_ref[0]
        weight_t = weight_t_ref[...]
        bias = bias_ref[...]
        levels = lax.broadcasted_iota(jnp.int32, (bins, cols), 0)
        for g in range(step_groups):
            group = []
            for r in range(GROUP):
                i = g * GROUP + r
                own = (contract(weight_t, pair_ref[i], 1, 1) + bias).astype(BF16).astype(F32)
                halves = []
                for u in range(parts):
                    half = received[0][i]
                    for shift in range(1, parts):
                        half = jnp.where(
                            lax.rem(h + parts - u, parts) == shift, received[shift][i], half
                        )
                    halves.append(half)
                symmetric = own + jnp.concatenate(halves, axis=1).astype(F32)
                top = jnp.max(symmetric, axis=0, keepdims=True)
                raised = jnp.exp(symmetric - top)
                scale = 2.0 / jnp.sum(raised, axis=0, keepdims=True)
                hit = jnp.where(levels == target_ref[i : i + 1, :], 2.0, 0.0)
                group.append((raised * scale - hit).astype(BF16))
            slope = jnp.concatenate(group, axis=0).T
            slopes[step * step_groups + g] = slope
            out = contract(slope, weight_wide_ref[...], 1, 0).astype(BF16)
            for r in range(GROUP):
                grad_ref[g * GROUP + r] = out[:, r * width : (r + 1) * width]

    @pl.when(step == front)
    def _():
        for copy in copies:
            copy.wait()
        half_groups = max(1, min(groups, 256 // seqs))

        def add_tile(t, carry):
            for x in range(tile):
                for r in range(GROUP):
                    rows = pl.ds((x * GROUP + r) * bins, bins)
                    at = r * features
                    mix_wide[rows, at : at + features] = (
                        mix[t * tile + x, :, at % 128 : at % 128 + features]
                    )
            factor = factors[pl.ds(pl.multiple_of(t * tile * seqs, tile * seqs), tile * seqs), :]
            for g in range(groups):
                spread = contract(factor, slopes[g], 1, 0).astype(BF16)
                for x in range(tile):
                    mixed[g * seqs : (g + 1) * seqs, x * GROUP * bins : (x + 1) * GROUP * bins] = (
                        spread[x * seqs : (x + 1) * seqs, :]
                    )
            for g in range(0, groups, half_groups):
                rows = slice(g * seqs, (g + half_groups) * seqs)
                term = contract(mixed[rows, :], mix_wide[...], 1, 0)
                for c in range(total.shape[0]):
                    total[c, rows, :] += term[:, c * 128 : (c + 1) * 128]
            return carry

        lax.fori_loop(0, xs // tile, add_tile, 0)
        for s in range(seqs):
            device, k = divmod(s, device_seqs)
            for c in range(total.shape[0]):
                norm_ref[device, k * groups : (k + 1) * groups, c * 128 : (c + 1) * 128] = (
                    total[c, pl.ds(s, groups, stride=seqs), :].astype(BF16)
                )


def pair_step(
    part, pair_activation, received, targets, weight_t, weight_wide, bias, factors, mix, grad,
    first_row, seqs, devices,
):
    _, cols, width = pair_activation.shape
    bins = weight_t.shape[0]
    features = mix.shape[2] // 2
    parts = len(received)
    chunk_rows = received[0].shape[0]
    step_rows = min(16, chunk_rows)
    groups = chunk_rows // GROUP
    xs = factors.shape[0] // seqs
    tile = max(1, min(8, 512 // seqs))
    front = chunk_rows // step_rows
    near = lambda s: jnp.minimum(s, front - 1)
    there = lambda s: first_row // step_rows + jnp.minimum(s, front - 1)
    const2 = lambda s, p: (0, 0)
    norm_shape = (devices, seqs // devices * groups, GROUP * features)
    return pl.pallas_call(
        functools.partial(pair_kernel, parts, front, tile),
        grid_spec=pltpu.PrefetchScalarGridSpec(
            num_scalar_prefetch=1,
            grid=(front + 1,),
            in_specs=[pl.BlockSpec((step_rows, cols, width), lambda s, p: (there(s), 0, 0))]
            + [pl.BlockSpec((step_rows, bins, cols // parts), lambda s, p: (near(s), 0, 0))] * parts
            + [
                pl.BlockSpec((step_rows, cols), lambda s, p: (there(s), 0)),
                pl.BlockSpec((bins, width), const2),
                pl.BlockSpec((GROUP * bins, GROUP * width), const2),
                pl.BlockSpec((bins, 1), const2),
            ]
            + [pl.BlockSpec(memory_space=pl.ANY)] * (2 + len(grad)),
            out_specs=[
                pl.BlockSpec((step_rows, cols, width), lambda s, p: (there(s), 0, 0)),
                pl.BlockSpec(norm_shape, lambda s, p: (0, 0, 0)),
            ],
            scratch_shapes=[
                pltpu.VMEM((groups, cols, GROUP * bins), BF16),
                pltpu.VMEM(factors.shape, BF16),
                pltpu.VMEM(mix.shape, BF16),
                pltpu.VMEM((tile * GROUP * bins, GROUP * features), BF16),
                pltpu.VMEM((groups * seqs, tile * GROUP * bins), BF16),
                pltpu.VMEM((GROUP * features // 128, groups * seqs, 128), F32),
                pltpu.SemaphoreType.DMA((2,)),
            ],
        ),
        out_shape=[
            jax.ShapeDtypeStruct(pair_activation.shape, BF16),
            jax.ShapeDtypeStruct(norm_shape, BF16),
        ],
        input_output_aliases={parts + 8: 0} if grad else {},
        compiler_params=pltpu.CompilerParams(vmem_limit_bytes=VMEM_BYTES),
        cost_estimate=pl.CostEstimate(
            flops=4 * xs * seqs * cols * chunk_rows * bins,
            bytes_accessed=chunk_rows * cols * width * 6,
            transcendentals=chunk_rows * cols * bins,
        ),
        name="pair_step",
    )(part, pair_activation, *received, targets, weight_t, weight_wide, bias, factors, mix, *grad)


def norm_forward(features):
    centered = features - jnp.mean(features, axis=0, keepdims=True)
    scale_inv = lax.rsqrt(jnp.mean(centered * centered, axis=0, keepdims=True) + 1e-05)
    return centered * scale_inv, scale_inv


def norm_backward(incoming, normed, scale_inv):
    first_mean = jnp.mean(incoming, axis=0, keepdims=True)
    second_mean = jnp.mean(incoming * normed, axis=0, keepdims=True)
    return scale_inv * (incoming - first_mean - normed * second_mean)


def transition_kernel(
    pieces, rows, col_devices, entry_ref, arriving_ref, mean_gain_ref, gain_ref, gate_up_t_ref,
    gate_up_ref, down_ref, down_t_ref, *refs,
):
    arrived, (out_ref, incoming) = refs[:-2], refs[-2:]
    hidden = down_ref.shape[0]
    seqs, features, positions = out_ref.shape
    groups = rows // GROUP
    row = lax.broadcasted_iota(jnp.int32, (groups, rows), 0)
    col = lax.broadcasted_iota(jnp.int32, (groups, rows), 1)
    spread = [jnp.where(col == GROUP * row + r, 1.0, 0.0).astype(BF16) for r in range(GROUP)]

    for s in range(seqs):
        for block in range(positions // rows):
            sums = []
            for which, at, count in pieces:
                at += s * count
                sums.append(
                    sum(
                        arrived[which][block * col_devices + c, at : at + count, :].astype(F32)
                        for c in range(col_devices)
                    )
                )
            field = jnp.concatenate(sums, axis=0).astype(BF16)
            incoming[s, :, block * rows : (block + 1) * rows] = sum(
                contract(field[:, r * features : (r + 1) * features], spread[r], 0, 0)
                for r in range(GROUP)
            )

    gain = gain_ref[...]
    for s in range(seqs):
        entry = entry_ref[s].astype(F32)
        normed, scale_inv = norm_forward(entry)
        normed_input = (normed * gain).astype(BF16)
        both = contract(gate_up_t_ref[...], normed_input, 1, 0)
        gate, up = both[:hidden], both[hidden:]
        sig = jax.nn.sigmoid(gate)
        silu = gate * sig
        msa_out = entry + contract(down_t_ref[...], (silu * up).astype(BF16), 1, 0)
        second_normed, second_scale = norm_forward(msa_out)
        middle = arriving_ref[s].astype(F32) + norm_backward(
            incoming[s] * mean_gain_ref[...], second_normed, second_scale
        )
        hidden_grad = contract(down_ref[...], middle.astype(BF16), 1, 0)
        gate_grad = (hidden_grad * up * sig * (1.0 + gate * (1.0 - sig))).astype(BF16)
        up_grad = (hidden_grad * silu).astype(BF16)
        normed_grad = contract(
            gate_up_ref[...], jnp.concatenate([gate_grad, up_grad], axis=0), 1, 0
        )
        out = middle + norm_backward(normed_grad * gain, normed, scale_inv)
        out_ref[s] = out.astype(BF16)


def transition(
    entry, arriving, arrived, pieces, rows, col_devices, mean_gain, gain, gate_weight, up_weight,
    down_weight,
):
    features = entry.shape[1]
    gate_up = jnp.concatenate([gate_weight, up_weight], axis=1)
    return pl.pallas_call(
        functools.partial(transition_kernel, pieces, rows, col_devices),
        out_shape=jax.ShapeDtypeStruct(entry.shape, BF16),
        scratch_shapes=[pltpu.VMEM(entry.shape, F32)],
        compiler_params=pltpu.CompilerParams(vmem_limit_bytes=VMEM_BYTES),
        name="transition",
    )(entry, arriving, mean_gain[:, None], gain[:, None], gate_up.T, gate_up, down_weight,
      down_weight.T, *arrived)


def chunk_plan(rows):
    sizes = []
    while rows - sum(sizes) > 32:
        sizes.append(32)
    left = rows - sum(sizes)
    sizes += [16, left - 16] if left > 16 else [left]
    return [(sum(sizes[:n]), size) for n, size in enumerate(sizes)]


def per_device(
    pair_activation,
    target_distance_bins,
    distogram_weight,
    distogram_bias,
    outer_pair_weight,
    stored_lhs_operand,
    stored_rhs_operand,
    left_projection_weight,
    right_projection_weight,
    outer_mean_norm_gain,
    transition_norm_gain,
    gate_weight,
    up_weight,
    down_weight,
    side_stack_entry,
    arriving_stack_derivative,
):
    rows, cols, _ = pair_activation.shape
    width, bins = distogram_weight.shape
    factor_width = stored_lhs_operand.shape[1]
    features = left_projection_weight.shape[0]
    row_devices = lax.axis_size("row")
    col_devices = lax.axis_size("col")
    parts = row_devices // col_devices
    seqs = stored_lhs_operand.shape[0] * row_devices
    part = (lax.axis_index("row") % parts).astype(jnp.int32)[None]
    weight_t = distogram_weight.T
    bias = distogram_bias[:, None]
    same = jnp.eye(GROUP, dtype=BF16)
    weight_wide = (same[:, None, :, None] * weight_t[None, :, None, :]).reshape(
        GROUP * bins, GROUP * width
    )

    factors = jnp.swapaxes(jnp.concatenate([stored_rhs_operand, stored_lhs_operand], axis=1), 0, 1)
    factors = lax.all_gather(factors, "row", axis=1, tiled=True)
    factors = factors.reshape(2 * factor_width * seqs, cols)

    chunks = chunk_plan(rows)
    leg_pairs = first_leg(col_devices, parts)
    received = []
    for first_row, chunk_rows in chunks:
        pieces = [
            mirror_logits(
                part, pair_activation, weight_t, bias, first_row, chunk_rows, shift, parts
            )
            for shift in range(parts)
        ]
        relayed = [lax.ppermute(piece, AXES, leg_pairs) for piece in pieces]
        received.append(
            [
                lax.ppermute(piece, AXES, second_leg(col_devices, parts, shift))
                for shift, piece in enumerate(relayed)
            ]
        )

    outer_weight = outer_pair_weight.astype(F32).reshape(factor_width, factor_width, width)
    by_bin = jnp.einsum(
        "pb,cep->bce", distogram_weight.astype(F32), outer_weight, precision=lax.Precision.HIGHEST
    )
    mix_right = jnp.einsum(
        "mc,bce->ebm", left_projection_weight.astype(F32), by_bin, precision=lax.Precision.HIGHEST
    )
    mix_left = jnp.einsum(
        "me,bce->cbm", right_projection_weight.astype(F32), by_bin, precision=lax.Precision.HIGHEST
    )
    mix = (jnp.concatenate([mix_right, mix_left], axis=0) / seqs).astype(BF16)
    mix = jnp.concatenate([mix, mix], axis=2)

    devices = row_devices * col_devices
    grad = ()
    norm_parts = []
    for (first_row, chunk_rows), pieces in zip(chunks, received):
        *grad, norm_part = pair_step(
            part, pair_activation, pieces, target_distance_bins, weight_t, weight_wide, bias,
            factors, mix, grad, first_row, seqs, devices,
        )
        norm_parts.append(norm_part)
    early = jnp.concatenate(norm_parts[:-1], axis=1) if len(chunks) > 2 else norm_parts[0]
    sent = [early] + norm_parts[1:][-1:] if len(chunks) > 1 else [early]
    arrived = [lax.all_to_all(x, AXES, split_axis=0, concat_axis=0, tiled=True) for x in sent]
    pieces = []
    for n, part_sums in enumerate(norm_parts):
        last = n == len(chunks) - 1 and n > 0
        at = 0 if last else sum(x.shape[1] for x in norm_parts[:n])
        pieces.append((int(last), at, chunks[n][1] // GROUP))
    alignment_gradient = transition(
        side_stack_entry, arriving_stack_derivative, arrived, pieces, rows, col_devices,
        outer_mean_norm_gain, transition_norm_gain, gate_weight, up_weight, down_weight,
    )
    return grad[0], alignment_gradient


def solution(mesh):
    return jax.shard_map(
        per_device,
        mesh=mesh,
        in_specs=(
            P("row", "col", None),
            P("row", "col"),
            P(),
            P(),
            P(),
            P("row", None, "col"),
            P("row", None, "col"),
            P(),
            P(),
            P(),
            P(),
            P(),
            P(),
            P(),
            P(AXES, None, None),
            P(AXES, None, None),
        ),
        out_specs=(P("row", "col", None), P(AXES, None, None)),
        check_vma=False,
    )
```

time: 334 us -> 250 us (0.75)
  starting transfers between devices: 84.1 us -> 39.2 us
  local copies, waits for them, and re-layouts: 41.5 us -> 12.5 us
  Pallas kernels: 125 us -> 110 us
  waiting for transfers between devices: 54.1 us -> 65 us
  other arithmetic: 11.4 us -> 4.83 us
    ppermute x8 -> x10, starting transfers between devices: 54.9 us -> 19.6 us  [per_device(): lax.ppermute(piece, AXES, second_leg(col_devices, parts, shift))]
    all_gather x2 -> x1, waiting for transfers between devices: 2.45 us -> 37.6 us  [per_device(): factors = lax.all_gather(factors, 'row', axis=1, tiled=True)]
    mul x1 -> x0, local copies, waits for them, and re-layouts: 24.3 us -> none  [per_device(): mix[:, None, :, None, :] * same[None, :, None, :, None]]
    pallas_call x5 -> x6, Pallas kernels: 102 us -> 83 us  [the longest x5 77.9 us: pair_step(): pl.pallas_call(functools.partial(pair_kernel, parts, front, tile), grid_s...]
    ppermute x8 -> x10, waiting for transfers between devices: 17.5 us -> 0.03 us  [per_device(): relayed = [lax.ppermute(piece, AXES, leg_pairs) for piece in pieces]]
    all_to_all x4 -> x2, starting transfers between devices: 18.6 us -> 8.46 us  [per_device(): lax.all_to_all(x, AXES, split_axis=0, concat_axis=0, tiled=True)]
    mul x1, other arithmetic: 8.62 us -> 0.17 us  [per_device(): same[:, None, :, None] * weight_t[None, :, None, :]]
    all_to_all x4 -> x2, waiting for transfers between devices: 33.4 us -> 26.7 us  [per_device(): lax.all_to_all(x, AXES, split_axis=0, concat_axis=0, tiled=True)]
  transfers between devices with their start and end apart: 22 -> 23, of which waited for: 7 -> 4; matrix products, arithmetic and copies ran while one was open for 14% -> 6% of each run, Pallas kernels for 28% -> 36%
where the time goes in v2:
time: 250 us; the launch traced here: 248 us
  Pallas kernels  110 us (44%)
  waiting for transfers between devices  65 us (26%)
  starting transfers between devices  39.2 us (16%)
  between operations  14.4 us (6%)
  local copies, waits for them, and re-layouts  12.5 us (5%)
  other arithmetic  4.83 us (2%)
    pallas_call x5, Pallas kernels, pair_step(): pl.pallas_call(functools.partial(pair_kernel, parts, front, tile), grid_s...  77.9 us
    all_gather x1, waiting for transfers between devices, per_device(): factors = lax.all_gather(factors, 'row', axis=1, tiled=True)  37.6 us
    all_to_all x2, waiting for transfers between devices, per_device(): lax.all_to_all(x, AXES, split_axis=0, concat_axis=0, tiled=True)  26.7 us
    pallas_call x10, Pallas kernels, mirror_logits(): pl.pallas_call(mirror_logits_kernel, grid_spec=pltpu.PrefetchScalarGridSp...  26.6 us
    ppermute x10, starting transfers between devices, per_device(): lax.ppermute(piece, AXES, second_leg(col_devices, parts, shift))  19.6 us
    ppermute x10, starting transfers between devices, per_device(): relayed = [lax.ppermute(piece, AXES, leg_pairs) for piece in pieces]  11.1 us
    all_to_all x2, starting transfers between devices, per_device(): lax.all_to_all(x, AXES, split_axis=0, concat_axis=0, tiled=True)  8.46 us
    pallas_call x1, Pallas kernels, transition(): pl.pallas_call(functools.partial(transition_kernel, pieces, rows, col_dev...  5.06 us
  transfers between devices with their start and end apart: 23, of which 4 were waited for; matrix products, arithmetic and copies ran while one was open for 6% of the time, Pallas kernels for 36%

profile of v2, /device:TPU:0, one launch (start us, length us, event | category | flops | bytes accessed | tf_op | source)
XLA Modules:
  0.0 247.9 jit_solution(1059384103683748122)
XLA Ops:
  10.3 2.9 %mirror_logits.18 = bf16[32,64,128]{2,1,0:T(8,128)(2,1)} custom-call(s32[1]{0:T(128)} %bitcast.part_ref, bf16[128,256,128]{2,1,0:T(8,128)(2,1)} %pair_ref.29, bf16[64,128]{1,0:T(8,128)(2,1)} %bitcast.37, f32[64,1]{1,0:T(8,128)} %copy.43.bias_ref.refs_5_), custom_call_target="tpu_custom_call" | custom-call | flops 268435456 | bytes 1572864 | tf_op jit(solution)/shard_map/mirror_logits/pallas_call | solution.py:77
  13.2 3.0 %collective-permute-start.16 = (bf16[32,64,128]{2,1,0:T(8,128)(2,1)}, bf16[32,64,128]{2,1,0:T(8,128)(2,1)}, u32[]{:S(2)}, u32[]{:S(2)}) collective-permute-start(bf16[32,64,128]{2,1,0:T(8,128)(2,1)} %mirror_logits.18), channel_id=1, source_target_pairs={{0,16},{4,20},{1,24},{5,28},{2,18},{6,22},{3,26},{7,30},{8,0},{12,... | collective-permute-start | bytes 1572872 | tf_op jit(solution)/shard_map/ppermute | solution.py:394
  16.2 2.9 %mirror_logits.19 = bf16[32,64,128]{2,1,0:T(8,128)(2,1)} custom-call(s32[1]{0:T(128)} %bitcast.part_ref, bf16[128,256,128]{2,1,0:T(8,128)(2,1)} %pair_ref.29, bf16[64,128]{1,0:T(8,128)(2,1)} %bitcast.38, f32[64,1]{1,0:T(8,128)} %copy.43.bias_ref.refs_5_), custom_call_target="tpu_custom_call" | custom-call | flops 268435456 | bytes 1572864 | tf_op jit(solution)/shard_map/mirror_logits/pallas_call | solution.py:77
  20.7 2.9 %mirror_logits.16 = bf16[32,64,128]{2,1,0:T(8,128)(2,1)} custom-call(s32[1]{0:T(128)} %bitcast.part_ref, bf16[128,256,128]{2,1,0:T(8,128)(2,1)} %pair_ref.29, bf16[64,128]{1,0:T(8,128)(2,1)} %bitcast.39, f32[64,1]{1,0:T(8,128)} %copy.43.bias_ref.refs_5_), custom_call_target="tpu_custom_call" | custom-call | flops 268435456 | bytes 1572864 | tf_op jit(solution)/shard_map/mirror_logits/pallas_call | solution.py:77
  25.0 2.9 %mirror_logits.17 = bf16[32,64,128]{2,1,0:T(8,128)(2,1)} custom-call(s32[1]{0:T(128)} %bitcast.part_ref, bf16[128,256,128]{2,1,0:T(8,128)(2,1)} %pair_ref.29, bf16[64,128]{1,0:T(8,128)(2,1)} %bitcast.40, f32[64,1]{1,0:T(8,128)} %copy.43.bias_ref.refs_5_), custom_call_target="tpu_custom_call" | custom-call | flops 268435456 | bytes 1572864 | tf_op jit(solution)/shard_map/mirror_logits/pallas_call | solution.py:77
  28.4 2.9 %mirror_logits.15 = bf16[32,64,128]{2,1,0:T(8,128)(2,1)} custom-call(s32[1]{0:T(128)} %bitcast.part_ref, bf16[128,256,128]{2,1,0:T(8,128)(2,1)} %pair_ref.29, bf16[64,128]{1,0:T(8,128)(2,1)} %bitcast.41, f32[64,1]{1,0:T(8,128)} %copy.43.bias_ref.refs_5_), custom_call_target="tpu_custom_call" | custom-call | flops 268435456 | bytes 1572864 | tf_op jit(solution)/shard_map/mirror_logits/pallas_call | solution.py:77
  36.4 2.9 %mirror_logits.14 = bf16[32,64,128]{2,1,0:T(8,128)(2,1)} custom-call(s32[1]{0:T(128)} %bitcast.part_ref, bf16[128,256,128]{2,1,0:T(8,128)(2,1)} %pair_ref.29, bf16[64,128]{1,0:T(8,128)(2,1)} %bitcast.44, f32[64,1]{1,0:T(8,128)} %copy.43.bias_ref.refs_5_), custom_call_target="tpu_custom_call" | custom-call | flops 268435456 | bytes 1572864 | tf_op jit(solution)/shard_map/mirror_logits/pallas_call | solution.py:77
  39.5 2.3 mirror_logits.10
  42.5 2.3 mirror_logits.11
  46.1 6.0 %collective-permute-start.17 = (bf16[32,64,128]{2,1,0:T(8,128)(2,1)}, bf16[32,64,128]{2,1,0:T(8,128)(2,1)}, u32[]{:S(2)}, u32[]{:S(2)}) collective-permute-start(bf16[32,64,128]{2,1,0:T(8,128)(2,1)} %collective-permute-done.16), channel_id=1, source_target_pairs={{16,0},{20,4},{24,8},{28,12},{18,16},{22,20},{26,24},{30,28},{0,1}... | collective-permute-start | bytes 1572872 | tf_op jit(solution)/shard_map/ppermute | solution.py:397
  55.6 37.6 %all-gather.2.cloned.1.call-done = bf16[64,64,256]{2,0,1:T(8,128)(2,1)} async-done(((bf16[64,8,256]{2,0,1:T(8,128)(2,1)}), bf16[64,64,256]{2,0,1:T(8,128)(2,1)}) %all-gather.2.cloned.1.call-update) | async-done | bytes 2097168 | tf_op jit(solution)/shard_map/all_gather | solution.py:381
  93.2 4.1 %copy.45 = bf16[64,64,256]{2,1,0:T(8,128)(2,1)} copy(bf16[64,64,256]{2,0,1:T(8,128)(2,1)} %all-gather.2.cloned.1.call-done) | data formatting | bytes 4194304 | tf_op jit(solution)/shard_map/all_gather | solution.py:381
  100.3 2.4 collective-permute-start.13
  104.1 16.6 %pair_step.5 = (bf16[128,256,128]{2,1,0:T(8,128)(2,1)}, bf16[32,16,256]{2,1,0:T(8,128)(2,1)}) custom-call(s32[1]{0:T(128)} %bitcast.part_ref, bf16[128,256,128]{2,1,0:T(8,128)(2,1)} %pair_ref.29, bf16[32,64,128]{2,1,0:T(8,128)(2,1)} %collective-permute-done.17.refs_0_, bf16[32,64,128]{2,1,0:T(8,128)(2,1)} %collective-permute-done.19.refs_1_, ...), custom_call_target="tpu_custom_call" | custom-call | flops 8589934592 | bytes 6291456 | tf_op jit(solution)/shard_map/pair_step/pallas_call | solution.py:213
  122.0 3.1 %collective-permute-start.11 = (bf16[32,64,128]{2,1,0:T(8,128)(2,1)S(1)}, bf16[32,64,128]{2,1,0:T(8,128)(2,1)S(1)}, u32[]{:S(2)}, u32[]{:S(2)}) collective-permute-start(bf16[32,64,128]{2,1,0:T(8,128)(2,1)S(1)} %collective-permute-done.10), channel_id=1, source_target_pairs={{16,4},{20,0},{24,12},{28,8},{18,20},{22,16},{26,28},{30,24},{0,5}... | collective-permute-start | bytes 1572872 | tf_op jit(solution)/shard_map/ppermute | solution.py:397
  127.4 16.6 %pair_step.6 = (bf16[128,256,128]{2,1,0:T(8,128)(2,1)}, bf16[32,16,256]{2,1,0:T(8,128)(2,1)}) custom-call(s32[1]{0:T(128)} %bitcast.part_ref, bf16[128,256,128]{2,1,0:T(8,128)(2,1)} %pair_ref.29, bf16[32,64,128]{2,1,0:T(8,128)(2,1)} %copy-done.26, bf16[32,64,128]{2,1,0:T(8,128)(2,1)} %copy-done.28, ...), custom_call_target="tpu_custom_call", output_to_operand_aliasing={{0}: (10, {})} | custom-call | flops 8589934592 | bytes 6291456 | tf_op jit(solution)/shard_map/pair_step/pallas_call | solution.py:213
  149.4 16.6 %pair_step.7 = (bf16[128,256,128]{2,1,0:T(8,128)(2,1)}, bf16[32,16,256]{2,1,0:T(8,128)(2,1)}) custom-call(s32[1]{0:T(128)} %bitcast.part_ref, bf16[128,256,128]{2,1,0:T(8,128)(2,1)} %pair_ref.29, bf16[32,64,128]{2,1,0:T(8,128)(2,1)} %copy-done.29, bf16[32,64,128]{2,1,0:T(8,128)(2,1)} %copy-done.27, ...), custom_call_target="tpu_custom_call", output_to_operand_aliasing={{0}: (10, {})} | custom-call | flops 8589934592 | bytes 6291456 | tf_op jit(solution)/shard_map/pair_step/pallas_call | solution.py:213
  166.8 14.0 %pair_step.8 = (bf16[128,256,128]{2,1,0:T(8,128)(2,1)}, bf16[32,8,256]{2,1,0:T(8,128)(2,1)}) custom-call(s32[1]{0:T(128)} %bitcast.part_ref, bf16[128,256,128]{2,1,0:T(8,128)(2,1)} %pair_ref.29, bf16[16,64,128]{2,1,0:T(8,128)(2,1)} %copy-done.8, bf16[16,64,128]{2,1,0:T(8,128)(2,1)} %copy-done.10, ...), custom_call_target="tpu_custom_call", output_to_operand_aliasing={{0}: (10, {})} | custom-call | flops 4294967296 | bytes 3145728 | tf_op jit(solution)/shard_map/pair_step/pallas_call | solution.py:213
  181.7 14.1 %pair_step.9 = (bf16[128,256,128]{2,1,0:T(8,128)(2,1)}, bf16[32,8,256]{2,1,0:T(8,128)(2,1)}) custom-call(s32[1]{0:T(128)} %bitcast.part_ref, bf16[128,256,128]{2,1,0:T(8,128)(2,1)} %pair_ref.29, bf16[16,64,128]{2,1,0:T(8,128)(2,1)} %copy-done.7, bf16[16,64,128]{2,1,0:T(8,128)(2,1)} %copy-done.9, ...), custom_call_target="tpu_custom_call", output_to_operand_aliasing={{0}: (10, {})} | custom-call | flops 4294967296 | bytes 3145728 | tf_op jit(solution)/shard_map/pair_step/pallas_call | solution.py:213
  195.8 5.8 %all-to-all-start.1 = ((bf16[32,8,256]{2,1,0:T(8,128)(2,1)}), bf16[32,8,256]{2,1,0:T(8,128)(2,1)S(1)}, u32[]{:S(2)}, u32[]{:S(2)}) async-start(bf16[32,8,256]{2,1,0:T(8,128)(2,1)} %get-tuple-element.21), calls=%async_computation.1 | async-start | bytes 262144 | tf_op jit(solution)/shard_map/all_to_all | solution.py:426
  202.7 7.3 %all-to-all-done.1.refs_1_ = bf16[32,8,256]{2,1,0:T(8,128)(2,1)S(1)} async-done(((bf16[32,8,256]{2,1,0:T(8,128)(2,1)}), bf16[32,8,256]{2,1,0:T(8,128)(2,1)S(1)}, u32[]{:S(2)}, u32[]{:S(2)}) %all-to-all-start.1) | async-done | bytes 131104 | tf_op jit(solution)/shard_map/all_to_all | solution.py:426
  210.1 2.6 %all-to-all-start = ((bf16[32,56,256]{2,1,0:T(8,128)(2,1)}), bf16[32,56,256]{2,1,0:T(8,128)(2,1)S(1)}, u32[]{:S(2)}, u32[]{:S(2)}) async-start(bf16[32,56,256]{2,1,0:T(8,128)(2,1)} %pad_maximum_fusion.1), calls=%async_computation | async-start | bytes 1835008 | tf_op jit(solution)/shard_map/all_to_all | solution.py:426
  215.7 19.4 %all-to-all-done.refs_0_ = bf16[32,56,256]{2,1,0:T(8,128)(2,1)S(1)} async-done(((bf16[32,56,256]{2,1,0:T(8,128)(2,1)}), bf16[32,56,256]{2,1,0:T(8,128)(2,1)S(1)}, u32[]{:S(2)}, u32[]{:S(2)}) %all-to-all-start) | async-done | bytes 917536 | tf_op jit(solution)/shard_map/all_to_all | solution.py:426
  236.0 5.1 %transition.1 = bf16[2,64,1024]{2,1,0:T(8,128)(2,1)} custom-call(bf16[2,64,1024]{2,1,0:T(8,128)(2,1)} %entry_ref.1, bf16[2,64,1024]{2,1,0:T(8,128)(2,1)} %arriving_ref.1, f32[64,1]{1,0:T(8,128)} %copy.60.mean_gain_ref, f32[64,1]{1,0:T(8,128)} %copy.61.gain_ref, bf16[512,64]{1,0:T(8,128)(2,1)} %copy.62.gate_up_t_ref, bf16[64,512]{1,0:T(8,128)(2,1)} %copy-done.6, ...), custom_call_target="tpu_custom_call" | custom-call | tf_op jit(solution)/shard_map/transition/pallas_call | solution.py:327
  (117 shorter events, 37.1 us)
Async XLA Ops:
  7.2 86.0 %all-gather.2.cloned.1.call-start = ((), (), s32[]{:S(2)}) async-start(), calls=%async_computation.2 | async-start | bytes 2359296 | tf_op jit(solution)/shard_map/all_gather | solution.py:381
  13.2 32.9 %collective-permute-start.16 = (bf16[32,64,128]{2,1,0:T(8,128)(2,1)}, bf16[32,64,128]{2,1,0:T(8,128)(2,1)}, u32[]{:S(2)}, u32[]{:S(2)}) collective-permute-start(bf16[32,64,128]{2,1,0:T(8,128)(2,1)} %mirror_logits.18), channel_id=1, source_target_pairs={{0,16},{4,20},{1,24},{5,28},{2,18},{6,22},{3,26},{7,30},{8,0},{12,... | collective-permute-start | bytes 1572872 | tf_op jit(solution)/shard_map/ppermute | solution.py:394
  19.1 33.1 %collective-permute-start.18 = (bf16[32,64,128]{2,1,0:T(8,128)(2,1)}, bf16[32,64,128]{2,1,0:T(8,128)(2,1)S(1)}, u32[]{:S(2)}, u32[]{:S(2)}) collective-permute-start(bf16[32,64,128]{2,1,0:T(8,128)(2,1)} %mirror_logits.19), channel_id=1, source_target_pairs={{0,16},{4,20},{1,24},{5,28},{2,18},{6,22},{3,26},{7,30},{8,0},{12,... | collective-permute-start | bytes 1572872 | tf_op jit(solution)/shard_map/ppermute | solution.py:394
  23.5 73.8 %collective-permute-start.12 = (bf16[32,64,128]{2,1,0:T(8,128)(2,1)}, bf16[32,64,128]{2,1,0:T(8,128)(2,1)S(1)}, u32[]{:S(2)}, u32[]{:S(2)}) collective-permute-start(bf16[32,64,128]{2,1,0:T(8,128)(2,1)} %mirror_logits.16), channel_id=1, source_target_pairs={{0,16},{4,20},{1,24},{5,28},{2,18},{6,22},{3,26},{7,30},{8,0},{12,... | collective-permute-start | bytes 1572872 | tf_op jit(solution)/shard_map/ppermute | solution.py:394
  27.9 70.8 %collective-permute-start.14 = (bf16[32,64,128]{2,1,0:T(8,128)(2,1)}, bf16[32,64,128]{2,1,0:T(8,128)(2,1)S(1)}, u32[]{:S(2)}, u32[]{:S(2)}) collective-permute-start(bf16[32,64,128]{2,1,0:T(8,128)(2,1)} %mirror_logits.17), channel_id=1, source_target_pairs={{0,16},{4,20},{1,24},{5,28},{2,18},{6,22},{3,26},{7,30},{8,0},{12,... | collective-permute-start | bytes 1572872 | tf_op jit(solution)/shard_map/ppermute | solution.py:394
  31.3 89.5 %collective-permute-start.10 = (bf16[32,64,128]{2,1,0:T(8,128)(2,1)}, bf16[32,64,128]{2,1,0:T(8,128)(2,1)S(1)}, u32[]{:S(2)}, u32[]{:S(2)}) collective-permute-start(bf16[32,64,128]{2,1,0:T(8,128)(2,1)} %mirror_logits.15), channel_id=1, source_target_pairs={{0,16},{4,20},{1,24},{5,28},{2,18},{6,22},{3,26},{7,30},{8,0},{12,... | collective-permute-start | bytes 1572872 | tf_op jit(solution)/shard_map/ppermute | solution.py:394
  46.1 54.1 %collective-permute-start.17 = (bf16[32,64,128]{2,1,0:T(8,128)(2,1)}, bf16[32,64,128]{2,1,0:T(8,128)(2,1)}, u32[]{:S(2)}, u32[]{:S(2)}) collective-permute-start(bf16[32,64,128]{2,1,0:T(8,128)(2,1)} %collective-permute-done.16), channel_id=1, source_target_pairs={{16,0},{20,4},{24,8},{28,12},{18,16},{22,20},{26,24},{30,28},{0,1}... | collective-permute-start | bytes 1572872 | tf_op jit(solution)/shard_map/ppermute | solution.py:397
  52.2 50.5 %collective-permute-start.19 = (bf16[32,64,128]{2,1,0:T(8,128)(2,1)S(1)}, bf16[32,64,128]{2,1,0:T(8,128)(2,1)}, u32[]{:S(2)}, u32[]{:S(2)}) collective-permute-start(bf16[32,64,128]{2,1,0:T(8,128)(2,1)S(1)} %collective-permute-done.18), channel_id=1, source_target_pairs={{16,4},{20,0},{24,12},{28,8},{18,20},{22,16},{26,28},{30,24},{0,5}... | collective-permute-start | bytes 1572872 | tf_op jit(solution)/shard_map/ppermute | solution.py:397
  55.6 43.1 %copy-start.16 = (bf16[16,64,128]{2,1,0:T(8,128)(2,1)S(1)}, bf16[16,64,128]{2,1,0:T(8,128)(2,1)}, u32[]{:S(2)}) copy-start(bf16[16,64,128]{2,1,0:T(8,128)(2,1)} %mirror_logits.12) | copy-start | bytes 786436
  97.4 24.1 %collective-permute-start.8 = (bf16[32,64,128]{2,1,0:T(8,128)(2,1)S(1)}, bf16[32,64,128]{2,1,0:T(8,128)(2,1)S(1)}, u32[]{:S(2)}, u32[]{:S(2)}) collective-permute-start(bf16[32,64,128]{2,1,0:T(8,128)(2,1)S(1)} %copy-done.4), channel_id=1, source_target_pairs={{0,16},{4,20},{1,24},{5,28},{2,18},{6,22},{3,26},{7,30},{8,0},{12,... | collective-permute-start | bytes 1572872 | tf_op jit(solution)/shard_map/ppermute | solution.py:394
  98.8 22.0 %collective-permute-start.4 = (bf16[16,64,128]{2,1,0:T(8,128)(2,1)S(1)}, bf16[16,64,128]{2,1,0:T(8,128)(2,1)S(1)}, u32[]{:S(2)}, u32[]{:S(2)}) collective-permute-start(bf16[16,64,128]{2,1,0:T(8,128)(2,1)S(1)} %copy-done.16), channel_id=1, source_target_pairs={{0,16},{4,20},{1,24},{5,28},{2,18},{6,22},{3,26},{7,30},{8,0},{12,... | collective-permute-start | bytes 786440 | tf_op jit(solution)/shard_map/ppermute | solution.py:394
  100.3 21.8 %collective-permute-start.13 = (bf16[32,64,128]{2,1,0:T(8,128)(2,1)S(1)}, bf16[32,64,128]{2,1,0:T(8,128)(2,1)S(1)}, u32[]{:S(2)}, u32[]{:S(2)}) collective-permute-start(bf16[32,64,128]{2,1,0:T(8,128)(2,1)S(1)} %collective-permute-done.12), channel_id=1, source_target_pairs={{16,0},{20,4},{24,8},{28,12},{18,16},{22,20},{26,24},{30,28},{0,1}... | collective-permute-start | bytes 1572872 | tf_op jit(solution)/shard_map/ppermute | solution.py:397
  102.7 22.5 %collective-permute-start.15 = (bf16[32,64,128]{2,1,0:T(8,128)(2,1)S(1)}, bf16[32,64,128]{2,1,0:T(8,128)(2,1)S(1)}, u32[]{:S(2)}, u32[]{:S(2)}) collective-permute-start(bf16[32,64,128]{2,1,0:T(8,128)(2,1)S(1)} %collective-permute-done.14), channel_id=1, source_target_pairs={{16,4},{20,0},{24,12},{28,8},{18,20},{22,16},{26,28},{30,24},{0,5}... | collective-permute-start | bytes 1572872 | tf_op jit(solution)/shard_map/ppermute | solution.py:397
  120.8 23.2 %collective-permute-start.6 = (bf16[16,64,128]{2,1,0:T(8,128)(2,1)S(1)}, bf16[16,64,128]{2,1,0:T(8,128)(2,1)S(1)}, u32[]{:S(2)}, u32[]{:S(2)}) collective-permute-start(bf16[16,64,128]{2,1,0:T(8,128)(2,1)S(1)} %copy-done.14), channel_id=1, source_target_pairs={{0,16},{4,20},{1,24},{5,28},{2,18},{6,22},{3,26},{7,30},{8,0},{12,... | collective-permute-start | bytes 786440 | tf_op jit(solution)/shard_map/ppermute | solution.py:394
  120.9 25.3 %collective-permute-start = (bf16[16,64,128]{2,1,0:T(8,128)(2,1)S(1)}, bf16[16,64,128]{2,1,0:T(8,128)(2,1)S(1)}, u32[]{:S(2)}, u32[]{:S(2)}) collective-permute-start(bf16[16,64,128]{2,1,0:T(8,128)(2,1)S(1)} %copy-done.13), channel_id=1, source_target_pairs={{0,16},{4,20},{1,24},{5,28},{2,18},{6,22},{3,26},{7,30},{8,0},{12,... | collective-permute-start | bytes 786440 | tf_op jit(solution)/shard_map/ppermute | solution.py:394
  121.5 26.2 %collective-permute-start.2 = (bf16[16,64,128]{2,1,0:T(8,128)(2,1)S(1)}, bf16[16,64,128]{2,1,0:T(8,128)(2,1)S(1)}, u32[]{:S(2)}, u32[]{:S(2)}) collective-permute-start(bf16[16,64,128]{2,1,0:T(8,128)(2,1)S(1)} %copy-done.12), channel_id=1, source_target_pairs={{0,16},{4,20},{1,24},{5,28},{2,18},{6,22},{3,26},{7,30},{8,0},{12,... | collective-permute-start | bytes 786440 | tf_op jit(solution)/shard_map/ppermute | solution.py:394
  122.0 26.0 %collective-permute-start.11 = (bf16[32,64,128]{2,1,0:T(8,128)(2,1)S(1)}, bf16[32,64,128]{2,1,0:T(8,128)(2,1)S(1)}, u32[]{:S(2)}, u32[]{:S(2)}) collective-permute-start(bf16[32,64,128]{2,1,0:T(8,128)(2,1)S(1)} %collective-permute-done.10), channel_id=1, source_target_pairs={{16,4},{20,0},{24,12},{28,8},{18,20},{22,16},{26,28},{30,24},{0,5}... | collective-permute-start | bytes 1572872 | tf_op jit(solution)/shard_map/ppermute | solution.py:397
  125.1 23.5 %collective-permute-start.9 = (bf16[32,64,128]{2,1,0:T(8,128)(2,1)S(1)}, bf16[32,64,128]{2,1,0:T(8,128)(2,1)S(1)}, u32[]{:S(2)}, u32[]{:S(2)}) collective-permute-start(bf16[32,64,128]{2,1,0:T(8,128)(2,1)S(1)} %collective-permute-done.8), channel_id=1, source_target_pairs={{16,0},{20,4},{24,8},{28,12},{18,16},{22,20},{26,24},{30,28},{0,1}... | collective-permute-start | bytes 1572872 | tf_op jit(solution)/shard_map/ppermute | solution.py:397
  144.0 22.0 %collective-permute-start.5 = (bf16[16,64,128]{2,1,0:T(8,128)(2,1)S(1)}, bf16[16,64,128]{2,1,0:T(8,128)(2,1)S(1)}, u32[]{:S(2)}, u32[]{:S(2)}) collective-permute-start(bf16[16,64,128]{2,1,0:T(8,128)(2,1)S(1)} %collective-permute-done.4), channel_id=1, source_target_pairs={{16,0},{20,4},{24,8},{28,12},{18,16},{22,20},{26,24},{30,28},{0,1}... | collective-permute-start | bytes 786440 | tf_op jit(solution)/shard_map/ppermute | solution.py:397
  146.1 19.9 %collective-permute-start.7 = (bf16[16,64,128]{2,1,0:T(8,128)(2,1)S(1)}, bf16[16,64,128]{2,1,0:T(8,128)(2,1)S(1)}, u32[]{:S(2)}, u32[]{:S(2)}) collective-permute-start(bf16[16,64,128]{2,1,0:T(8,128)(2,1)S(1)} %collective-permute-done.6), channel_id=1, source_target_pairs={{16,4},{20,0},{24,12},{28,8},{18,20},{22,16},{26,28},{30,24},{0,5}... | collective-permute-start | bytes 786440 | tf_op jit(solution)/shard_map/ppermute | solution.py:397
  147.6 33.2 %collective-permute-start.1 = (bf16[16,64,128]{2,1,0:T(8,128)(2,1)S(1)}, bf16[16,64,128]{2,1,0:T(8,128)(2,1)S(1)}, u32[]{:S(2)}, u32[]{:S(2)}) collective-permute-start(bf16[16,64,128]{2,1,0:T(8,128)(2,1)S(1)} %collective-permute-done), channel_id=1, source_target_pairs={{16,0},{20,4},{24,8},{28,12},{18,16},{22,20},{26,24},{30,28},{0,1}... | collective-permute-start | bytes 786440 | tf_op jit(solution)/shard_map/ppermute | solution.py:397
  148.0 32.9 %collective-permute-start.3 = (bf16[16,64,128]{2,1,0:T(8,128)(2,1)S(1)}, bf16[16,64,128]{2,1,0:T(8,128)(2,1)S(1)}, u32[]{:S(2)}, u32[]{:S(2)}) collective-permute-start(bf16[16,64,128]{2,1,0:T(8,128)(2,1)S(1)} %collective-permute-done.2), channel_id=1, source_target_pairs={{16,4},{20,0},{24,12},{28,8},{18,20},{22,16},{26,28},{30,24},{0,5}... | collective-permute-start | bytes 786440 | tf_op jit(solution)/shard_map/ppermute | solution.py:397
  195.8 14.2 %all-to-all-start.1 = ((bf16[32,8,256]{2,1,0:T(8,128)(2,1)}), bf16[32,8,256]{2,1,0:T(8,128)(2,1)S(1)}, u32[]{:S(2)}, u32[]{:S(2)}) async-start(bf16[32,8,256]{2,1,0:T(8,128)(2,1)} %get-tuple-element.21), calls=%async_computation.1 | async-start | bytes 262144 | tf_op jit(solution)/shard_map/all_to_all | solution.py:426
  210.1 25.0 %all-to-all-start = ((bf16[32,56,256]{2,1,0:T(8,128)(2,1)}), bf16[32,56,256]{2,1,0:T(8,128)(2,1)S(1)}, u32[]{:S(2)}, u32[]{:S(2)}) async-start(bf16[32,56,256]{2,1,0:T(8,128)(2,1)} %pad_maximum_fusion.1), calls=%async_computation | async-start | bytes 1835008 | tf_op jit(solution)/shard_map/all_to_all | solution.py:426
  (29 other events, 363.6 us)
Sparse Core Ops, SparseCore 0:
  9.9 83.2 all-gather.1

commit v3 on v2

--- a/solution.py
+++ b/solution.py
@@ -54,51 +54,105 @@
     return pairs
 
 
-def mirror_logits_kernel(part_ref, pair_ref, weight_ref, bias_ref, out_ref, widened):
+def as_column(row):
+    n = row.shape[1]
+    across = lax.broadcasted_iota(jnp.int32, (n, n), 0)
+    along = lax.broadcasted_iota(jnp.int32, (n, n), 1)
+    return jnp.sum(jnp.where(across == along, row, 0.0), axis=1, keepdims=True)
+
+
+def mirror_logits_kernel(part_ref, pair_ref, weight_ref, bias_ref, *refs):
+    out_ref, widened = refs[-2:]
     own_rows, step_cols, width = pair_ref.shape
     widened[...] = pair_ref[...].astype(F32).reshape(own_rows * step_cols, width)
     weight = weight_ref[...]
-    bias = bias_ref[...]
+    bias = as_column(bias_ref[...])
     for j in range(step_cols):
         column = widened[pl.ds(j, own_rows, stride=step_cols), :].astype(BF16)
-        out_ref[j] = (contract(weight, column, 1, 1) + bias).astype(BF16)
-
-
-def mirror_logits(part, pair_activation, weight_t, bias, first_row, chunk_rows, shift, parts):
+        out_ref[0, j] = (contract(weight, column, 1, 1) + bias).astype(BF16)
+
+
+def mirror_logits(part, pair_activation, weight_t, bias, first_row, chunk_rows, parts, ahead):
     rows, cols, width = pair_activation.shape
     bins = weight_t.shape[0]
     step = min(16, chunk_rows)
     steps = chunk_rows // step
 
     def block(s, part_ref):
-        half = lax.rem(part_ref[0] + shift, parts)
-        return (0, half * (rows // step) + first_row // step + s, 0)
+        half = lax.rem(part_ref[0] + s // steps, parts)
+        return (0, half * (rows // step) + first_row // step + lax.rem(s, steps), 0)
 
     return pl.pallas_call(
         mirror_logits_kernel,
         grid_spec=pltpu.PrefetchScalarGridSpec(
             num_scalar_prefetch=1,
-            grid=(steps,),
+            grid=(parts * steps,),
             in_specs=[
                 pl.BlockSpec((rows, step, width), block),
                 pl.BlockSpec((bins, width), lambda s, p: (0, 0)),
-                pl.BlockSpec((bins, 1), lambda s, p: (0, 0)),
-            ],
-            out_specs=pl.BlockSpec((step, bins, rows), lambda s, p: (s, 0, 0)),
+                pl.BlockSpec((1, bins), lambda s, p: (0, 0)),
+            ]
+            + [pl.BlockSpec(memory_space=pl.ANY)] * len(ahead),
+            out_specs=pl.BlockSpec(
+                (1, step, bins, rows), lambda s, p: (s // steps, lax.rem(s, steps), 0, 0)
+            ),
             scratch_shapes=[pltpu.VMEM((rows * step, width), F32)],
         ),
-        out_shape=jax.ShapeDtypeStruct((chunk_rows, bins, rows), BF16),
+        out_shape=jax.ShapeDtypeStruct((parts, chunk_rows, bins, rows), BF16),
         compiler_params=pltpu.CompilerParams(vmem_limit_bytes=VMEM_BYTES),
         cost_estimate=pl.CostEstimate(
-            flops=2 * chunk_rows * rows * bins * width * 4,
-            bytes_accessed=chunk_rows * rows * (width + bins) * 2,
+            flops=2 * parts * chunk_rows * rows * bins * width * 4,
+            bytes_accessed=parts * chunk_rows * rows * (width + bins) * 2,
             transcendentals=0,
         ),
         name="mirror_logits",
-    )(part, pair_activation, weight_t, bias)
-
-
-def pair_kernel(parts, front, tile, part_ref, pair_ref, *refs):
+    )(part, pair_activation, weight_t, bias, *ahead)
+
+
+def split_kernel(in_ref, *outs):
+    for n, out_ref in enumerate(outs):
+        out_ref[...] = in_ref[n]
+
+
+def split(array):
+    count, rows, *rest = array.shape
+    step = min(16, rows)
+    return pl.pallas_call(
+        split_kernel,
+        grid=(rows // step,),
+        in_specs=[pl.BlockSpec((count, step, *rest), lambda s: (0, s, 0, 0))],
+        out_specs=[pl.BlockSpec((step, *rest), lambda s: (s, 0, 0))] * count,
+        out_shape=[jax.ShapeDtypeStruct(array.shape[1:], array.dtype)] * count,
+        compiler_params=pltpu.CompilerParams(vmem_limit_bytes=VMEM_BYTES),
+        name="split",
+    )(array)
+
+
+def join_kernel(axis, count, *refs):
+    out_ref = refs[-1]
+    width = refs[0].shape[axis]
+    for n, ref in enumerate(refs[:count]):
+        if axis:
+            out_ref[:, n * width : (n + 1) * width] = ref[...]
+        else:
+            out_ref[n * width : (n + 1) * width] = ref[...]
+
+
+def join(arrays, axis, ahead=()):
+    shape = list(arrays[0].shape)
+    shape[axis] *= len(arrays)
+    vmem = pl.BlockSpec(memory_space=pltpu.VMEM)
+    return pl.pallas_call(
+        functools.partial(join_kernel, axis, len(arrays)),
+        in_specs=[vmem] * len(arrays) + [pl.BlockSpec(memory_space=pl.ANY)] * len(ahead),
+        out_specs=vmem,
+        out_shape=jax.ShapeDtypeStruct(shape, BF16),
+        compiler_params=pltpu.CompilerParams(vmem_limit_bytes=VMEM_BYTES),
+        name="join",
+    )(*arrays, *ahead)
+
+
+def pair_kernel(parts, slots, front, tile, part_ref, pair_ref, *refs):
     received = refs[:parts]
     target_ref, weight_t_ref, weight_wide_ref, bias_ref, factor_hbm, mix_hbm = refs[parts : parts + 6]
     grad_ref, norm_ref, slopes, factors, mix, mix_wide, mixed, total, sems = refs[-9:]
@@ -128,7 +182,7 @@
     def _():
         h = part_ref[0]
         weight_t = weight_t_ref[...]
-        bias = bias_ref[...]
+        bias = as_column(bias_ref[...])
         levels = lax.broadcasted_iota(jnp.int32, (bins, cols), 0)
         for g in range(step_groups):
             group = []
@@ -159,7 +213,7 @@
     def _():
         for copy in copies:
             copy.wait()
-        half_groups = max(1, min(groups, 256 // seqs))
+        half_groups = max(1, groups // 2)
 
         def add_tile(t, carry):
             for x in range(tile):
@@ -184,8 +238,13 @@
             return carry
 
         lax.fori_loop(0, xs // tile, add_tile, 0)
+        slot_seqs = seqs // slots
         for s in range(seqs):
-            device, k = divmod(s, device_seqs)
+            slot, rest = divmod(s, slot_seqs)
+            device, k = divmod(rest, device_seqs)
+            other, pair = divmod(slot, slots // parts)
+            block = part_ref[1] ^ pair
+            device += (block * parts + lax.rem(part_ref[0] + other, parts)) * (devices // slots)
             for c in range(total.shape[0]):
                 norm_ref[device, k * groups : (k + 1) * groups, c * 128 : (c + 1) * 128] = (
                     total[c, pl.ds(s, groups, stride=seqs), :].astype(BF16)
@@ -194,7 +253,7 @@
 
 def pair_step(
     part, pair_activation, received, targets, weight_t, weight_wide, bias, factors, mix, grad,
-    first_row, seqs, devices,
+    first_row, seqs, devices, slots, ahead,
 ):
     _, cols, width = pair_activation.shape
     bins = weight_t.shape[0]
@@ -211,7 +270,7 @@
     const2 = lambda s, p: (0, 0)
     norm_shape = (devices, seqs // devices * groups, GROUP * features)
     return pl.pallas_call(
-        functools.partial(pair_kernel, parts, front, tile),
+        functools.partial(pair_kernel, parts, slots, front, tile),
         grid_spec=pltpu.PrefetchScalarGridSpec(
             num_scalar_prefetch=1,
             grid=(front + 1,),
@@ -221,9 +280,9 @@
                 pl.BlockSpec((step_rows, cols), lambda s, p: (there(s), 0)),
                 pl.BlockSpec((bins, width), const2),
                 pl.BlockSpec((GROUP * bins, GROUP * width), const2),
-                pl.BlockSpec((bins, 1), const2),
+                pl.BlockSpec((1, bins), const2),
             ]
-            + [pl.BlockSpec(memory_space=pl.ANY)] * (2 + len(grad)),
+            + [pl.BlockSpec(memory_space=pl.ANY)] * (2 + len(grad) + len(ahead)),
             out_specs=[
                 pl.BlockSpec((step_rows, cols, width), lambda s, p: (there(s), 0, 0)),
                 pl.BlockSpec(norm_shape, lambda s, p: (0, 0, 0)),
@@ -250,7 +309,8 @@
             transcendentals=chunk_rows * cols * bins,
         ),
         name="pair_step",
-    )(part, pair_activation, *received, targets, weight_t, weight_wide, bias, factors, mix, *grad)
+    )(part, pair_activation, *received, targets, weight_t, weight_wide, bias, factors, mix, *grad,
+      *ahead)
 
 
 def norm_forward(features):
@@ -335,12 +395,8 @@
 
 
 def chunk_plan(rows):
-    sizes = []
-    while rows - sum(sizes) > 32:
-        sizes.append(32)
-    left = rows - sum(sizes)
-    sizes += [16, left - 16] if left > 16 else [left]
-    return [(sum(sizes[:n]), size) for n, size in enumerate(sizes)]
+    size = max(16, rows // 4)
+    return [(at, min(size, rows - at)) for at in range(0, rows, size)]
 
 
 def per_device(
@@ -369,35 +425,52 @@
     col_devices = lax.axis_size("col")
     parts = row_devices // col_devices
     seqs = stored_lhs_operand.shape[0] * row_devices
-    part = (lax.axis_index("row") % parts).astype(jnp.int32)[None]
+    row_index = lax.axis_index("row").astype(jnp.int32)
+    part = jnp.stack([row_index % parts, row_index // parts])
     weight_t = distogram_weight.T
-    bias = distogram_bias[:, None]
+    bias = distogram_bias[None, :]
     same = jnp.eye(GROUP, dtype=BF16)
     weight_wide = (same[:, None, :, None] * weight_t[None, :, None, :]).reshape(
         GROUP * bins, GROUP * width
     )
 
-    factors = jnp.swapaxes(jnp.concatenate([stored_rhs_operand, stored_lhs_operand], axis=1), 0, 1)
-    factors = lax.all_gather(factors, "row", axis=1, tiled=True)
-    factors = factors.reshape(2 * factor_width * seqs, cols)
+    blocks = row_devices // parts
+    own = join([stored_rhs_operand, stored_lhs_operand], 1)
+    others = []
+    for flip in range(1, blocks):
+        pairs = [((n ^ flip) * parts + h, n * parts + h) for n in range(blocks) for h in range(parts)]
+        others.append(lax.ppermute(own, "row", pairs))
 
     chunks = chunk_plan(rows)
     leg_pairs = first_leg(col_devices, parts)
-    received = []
+    logits, relayed, received = [], [], []
     for first_row, chunk_rows in chunks:
-        pieces = [
-            mirror_logits(
-                part, pair_activation, weight_t, bias, first_row, chunk_rows, shift, parts
-            )
-            for shift in range(parts)
-        ]
-        relayed = [lax.ppermute(piece, AXES, leg_pairs) for piece in pieces]
+        n = len(logits)
+        ahead = [x for arrays in logits[-1:] + relayed[: max(0, n - 1)][-1:] for x in arrays]
+        if n == 1:
+            ahead += others
+        pieces = mirror_logits(
+            part, pair_activation, weight_t, bias, first_row, chunk_rows, parts, ahead
+        )
+        logits.append([pieces])
+        relayed.append(split(lax.ppermute(pieces, AXES, leg_pairs)))
         received.append(
             [
                 lax.ppermute(piece, AXES, second_leg(col_devices, parts, shift))
-                for shift, piece in enumerate(relayed)
+                for shift, piece in enumerate(relayed[-1])
             ]
         )
+
+    across = join([own] + others, 0)
+    shifted = [across]
+    for shift in range(1, parts):
+        pairs = [
+            (n * parts + (h + shift) % parts, n * parts + h)
+            for n in range(blocks) for h in range(parts)
+        ]
+        shifted.append(lax.ppermute(across, "row", pairs))
+    factors = jnp.concatenate(shifted).reshape(seqs, 2 * factor_width, cols)
+    factors = factors.swapaxes(0, 1).reshape(2 * factor_width * seqs, cols)
 
     outer_weight = outer_pair_weight.astype(F32).reshape(factor_width, factor_width, width)
     by_bin = jnp.einsum(
@@ -415,15 +488,25 @@
     devices = row_devices * col_devices
     grad = ()
     norm_parts = []
-    for (first_row, chunk_rows), pieces in zip(chunks, received):
+    exchange = functools.partial(
+        lax.all_to_all, axis_name=AXES, split_axis=0, concat_axis=0, tiled=True
+    )
+    arrived = []
+    for n, ((first_row, chunk_rows), pieces) in enumerate(zip(chunks, received)):
+        ahead = [x for arrays in logits[n + 2 : n + 3] + relayed[n + 1 : n + 2] for x in arrays]
+        if n == len(chunks) - 1 and n > 0:
+            early = join(norm_parts, 1, pieces)
+            arrived.append(exchange(early))
+            ahead.append(early)
         *grad, norm_part = pair_step(
             part, pair_activation, pieces, target_distance_bins, weight_t, weight_wide, bias,
-            factors, mix, grad, first_row, seqs, devices,
+            factors, mix, grad, first_row, seqs, devices, row_devices, ahead,
         )
         norm_parts.append(norm_part)
-    early = jnp.concatenate(norm_parts[:-1], axis=1) if len(chunks) > 2 else norm_parts[0]
-    sent = [early] + norm_parts[1:][-1:] if len(chunks) > 1 else [early]
-    arrived = [lax.all_to_all(x, AXES, split_axis=0, concat_axis=0, tiled=True) for x in sent]
+    final = norm_parts[-1]
+    if arrived:
+        final, arrived[0] = lax.optimization_barrier((final, arrived[0]))
+    arrived.append(exchange(final))
     pieces = []
     for n, part_sums in enumerate(norm_parts):
         last = n == len(chunks) - 1 and n > 0

time: 250 us -> 207 us (0.83)
  waiting for transfers between devices: 65 us -> 39.8 us
  between operations: 14.4 us -> 1 us
  starting transfers between devices: 39.2 us -> 35.1 us
  local copies, waits for them, and re-layouts: 12.5 us -> 15 us
    all_gather x1 -> x0, waiting for transfers between devices: 37.6 us -> none  [per_device(): factors = lax.all_gather(factors, 'row', axis=1, tiled=True)]
    ppermute x10 -> x8, waiting for transfers between devices: 0.03 us -> 24.2 us  [the longest x3 24.2 us: per_device(): others.append(lax.ppermute(own, 'row', pairs))]
    all_to_all x2, waiting for transfers between devices: 26.7 us -> 9.21 us  [the longest x1 7.01 us: per_device(): arrived.append(exchange(final))]
    ppermute x10 -> x8, waiting for transfers between devices: 0.64 us -> 6.37 us  [per_device(): lax.ppermute(piece, AXES, second_leg(col_devices, parts, shift))]
    unnamed x63 -> x61, local copies, waits for them, and re-layouts: 4.88 us -> 10.3 us
    pallas_call x5 -> x11, Pallas kernels: 77.9 us -> 83.3 us  [the longest x4 69 us: pair_step(): pl.pallas_call(functools.partial(pair_kernel, parts, slots, front, tile),...]
    pallas_call x10 -> x4, Pallas kernels: 26.6 us -> 21.6 us  [mirror_logits(): pl.pallas_call(mirror_logits_kernel, grid_spec=pltpu.PrefetchScalarGridSp...]
    ppermute x10 -> x8, starting transfers between devices: 11.1 us -> 6.57 us  [the longest x3 4.46 us: per_device(): others.append(lax.ppermute(own, 'row', pairs))]
  transfers between devices with their start and end apart: 23 -> 18, of which waited for: 4 -> 6; matrix products, arithmetic and copies ran while one was open for 6% -> 6% of each run, Pallas kernels for 36% -> 49%
where the time goes in v3:
time: 207 us; the launch traced here: 206 us
  Pallas kernels  110 us (53%)
  waiting for transfers between devices  39.8 us (19%)
  starting transfers between devices  35.1 us (17%)
  local copies, waits for them, and re-layouts  15 us (7%)
  other arithmetic  2.86 us (1%)
  matrix products  2.37 us (1%)
    pallas_call x4, Pallas kernels, pair_step(): pl.pallas_call(functools.partial(pair_kernel, parts, slots, front, tile),...  69 us
    ppermute x3, waiting for transfers between devices, per_device(): others.append(lax.ppermute(own, 'row', pairs))  24.2 us
    pallas_call x4, Pallas kernels, mirror_logits(): pl.pallas_call(mirror_logits_kernel, grid_spec=pltpu.PrefetchScalarGridSp...  21.6 us
    ppermute x8, starting transfers between devices, per_device(): lax.ppermute(piece, AXES, second_leg(col_devices, parts, shift))  17.6 us
    unnamed x61, local copies, waits for them, and re-layouts  10.3 us
    pallas_call x4, Pallas kernels, split(): pl.pallas_call(split_kernel, grid=(rows // step,), in_specs=[pl.BlockSpec...  8.26 us
    all_to_all x1, waiting for transfers between devices, per_device(): arrived.append(exchange(final))  7.01 us
    ppermute x8, waiting for transfers between devices, per_device(): lax.ppermute(piece, AXES, second_leg(col_devices, parts, shift))  6.37 us
  transfers between devices with their start and end apart: 18, of which 6 were waited for; matrix products, arithmetic and copies ran while one was open for 6% of the time, Pallas kernels for 49%

profile of v3, /device:TPU:0, one launch (start us, length us, event | category | flops | bytes accessed | tf_op | source)
XLA Modules:
  0.0 206.0 jit_solution(18079525801288884346)
XLA Ops:
  2.4 2.9 %collective-permute-start = (bf16[8,64,256]{2,1,0:T(8,128)(2,1)}, bf16[8,64,256]{2,1,0:T(8,128)(2,1)S(1)}, u32[]{:S(2)}, u32[]{:S(2)}) collective-permute-start(bf16[8,64,256]{2,1,0:T(8,128)(2,1)} %join.3.refs_0_), channel_id=1, source_target_pairs={{8,0},{12,4},{0,8},{4,12},{24,16},{28,20},{16,24},{20,28},{9,1},{1... | collective-permute-start | bytes 786440 | tf_op jit(solution)/shard_map/ppermute | solution.py:442
  7.5 5.5 %mirror_logits.4.refs_0_ = bf16[2,32,64,128]{3,2,1,0:T(8,128)(2,1)} custom-call(s32[2]{0:T(128)} %pad_add_fusion.part_ref, bf16[128,256,128]{2,1,0:T(8,128)(2,1)} %pair_ref.15, bf16[64,128]{1,0:T(8,128)(2,1)} %bitcast.38, f32[1,64]{1,0:T(1,128)} %bitcast.53), custom_call_target="tpu_custom_call" | custom-call | flops 536870912 | bytes 3145728 | tf_op jit(solution)/shard_map/mirror_logits/pallas_call | solution.py:85
  15.2 4.2 %collective-permute-done.1.refs_2_ = bf16[8,64,256]{2,1,0:T(8,128)(2,1)S(1)} collective-permute-done((bf16[8,64,256]{2,1,0:T(8,128)(2,1)}, bf16[8,64,256]{2,1,0:T(8,128)(2,1)S(1)}, u32[]{:S(2)}, u32[]{:S(2)}) %collective-permute-start.1) | collective-permute-done | bytes 262176 | tf_op jit(solution)/shard_map/ppermute | solution.py:442
  19.4 20.0 %collective-permute-done.2.refs_3_ = bf16[8,64,256]{2,1,0:T(8,128)(2,1)S(1)} collective-permute-done((bf16[8,64,256]{2,1,0:T(8,128)(2,1)}, bf16[8,64,256]{2,1,0:T(8,128)(2,1)S(1)}, u32[]{:S(2)}, u32[]{:S(2)}) %collective-permute-start.2) | collective-permute-done | bytes 262176 | tf_op jit(solution)/shard_map/ppermute | solution.py:442
  40.1 5.4 %mirror_logits.5.refs_0_ = bf16[2,32,64,128]{3,2,1,0:T(8,128)(2,1)} custom-call(s32[2]{0:T(128)} %pad_add_fusion.part_ref, bf16[128,256,128]{2,1,0:T(8,128)(2,1)} %pair_ref.15, bf16[64,128]{1,0:T(8,128)(2,1)} %bitcast.39, f32[1,64]{1,0:T(1,128)} %bitcast.54, bf16[2,32,64,128]{3,2,1,0:T(8,128)(2,1)} %mirror_logits.4.refs_0_, bf16[8,64,256]{2,1,0:T(8,128)(2,1)} %copy-done.8, ...), custom_call_target="tpu_custom_call" | custom-call | flops 536870912 | bytes 3145728 | tf_op jit(solution)/shard_map/mirror_logits/pallas_call | solution.py:85
  45.5 2.3 %join.4 = bf16[32,64,256]{2,1,0:T(8,128)(2,1)} custom-call(bf16[8,64,256]{2,1,0:T(8,128)(2,1)} %join.3.refs_0_, bf16[8,64,256]{2,1,0:T(8,128)(2,1)} %copy-done.8, bf16[8,64,256]{2,1,0:T(8,128)(2,1)} %copy-done.9, bf16[8,64,256]{2,1,0:T(8,128)(2,1)} %copy-done.10), custom_call_target="tpu_custom_call" | custom-call | tf_op jit(solution)/shard_map/join/pallas_call | solution.py:145
  53.2 5.6 %collective-permute-start.14 = (bf16[32,64,128]{2,1,0:T(8,128)(2,1)}, bf16[32,64,128]{2,1,0:T(8,128)(2,1)S(1)}, u32[]{:S(2)}, u32[]{:S(2)}) collective-permute-start(bf16[32,64,128]{2,1,0:T(8,128)(2,1)} %get-tuple-element.20.refs_1_), channel_id=1, source_target_pairs={{16,0},{20,4},{24,8},{28,12},{18,16},{22,20},{26,24},{30,28},{0,1}... | collective-permute-start | bytes 1572872 | tf_op jit(solution)/shard_map/ppermute | solution.py:459
  58.9 2.4 %collective-permute-start.15 = (bf16[32,64,128]{2,1,0:T(8,128)(2,1)}, bf16[32,64,128]{2,1,0:T(8,128)(2,1)S(1)}, u32[]{:S(2)}, u32[]{:S(2)}) collective-permute-start(bf16[32,64,128]{2,1,0:T(8,128)(2,1)} %get-tuple-element.21.refs_2_), channel_id=1, source_target_pairs={{16,4},{20,0},{24,12},{28,8},{18,20},{22,16},{26,28},{30,24},{0,5}... | collective-permute-start | bytes 1572872 | tf_op jit(solution)/shard_map/ppermute | solution.py:459
  61.6 5.3 %mirror_logits.6.refs_0_.refs_8_ = bf16[2,32,64,128]{3,2,1,0:T(8,128)(2,1)} custom-call(s32[2]{0:T(128)} %pad_add_fusion.part_ref, bf16[128,256,128]{2,1,0:T(8,128)(2,1)} %pair_ref.15, bf16[64,128]{1,0:T(8,128)(2,1)} %bitcast.40, f32[1,64]{1,0:T(1,128)} %bitcast.55, bf16[2,32,64,128]{3,2,1,0:T(8,128)(2,1)} %mirror_logits.5.refs_0_, ...), custom_call_target="tpu_custom_call" | custom-call | flops 536870912 | bytes 3145728 | tf_op jit(solution)/shard_map/mirror_logits/pallas_call | solution.py:85
  69.5 2.5 %copy.21 = bf16[64,64,256]{2,1,0:T(8,128)(2,1)} copy(bf16[64,64,256]{2,0,1:T(8,128)(2,1)S(1)} %maximum_bitcast_fusion) | data formatting | bytes 4194304 | tf_op jit(solution)/shard_map/transpose | solution.py:473
  73.0 2.1 %split.5 = (bf16[32,64,128]{2,1,0:T(8,128)(2,1)}, bf16[32,64,128]{2,1,0:T(8,128)(2,1)}) custom-call(bf16[2,32,64,128]{3,2,1,0:T(8,128)(2,1)} %copy-done.4), custom_call_target="tpu_custom_call" | custom-call | tf_op jit(solution)/shard_map/split/pallas_call | solution.py:120
  75.1 5.8 %collective-permute-start.12 = (bf16[32,64,128]{2,1,0:T(8,128)(2,1)}, bf16[32,64,128]{2,1,0:T(8,128)(2,1)S(1)}, u32[]{:S(2)}, u32[]{:S(2)}) collective-permute-start(bf16[32,64,128]{2,1,0:T(8,128)(2,1)} %get-tuple-element.22.refs_1_.refs_9_), channel_id=1, source_target_pairs={{16,0},{20,4},{24,8},{28,12},{18,16},{22,20},{26,24},{30,28},{0,1}... | collective-permute-start | bytes 1572872 | tf_op jit(solution)/shard_map/ppermute | solution.py:459
  80.9 5.4 %mirror_logits.7.refs_9_ = bf16[2,32,64,128]{3,2,1,0:T(8,128)(2,1)} custom-call(s32[2]{0:T(128)} %pad_add_fusion.part_ref, bf16[128,256,128]{2,1,0:T(8,128)(2,1)} %pair_ref.15, bf16[64,128]{1,0:T(8,128)(2,1)} %bitcast.41, f32[1,64]{1,0:T(1,128)} %bitcast.56, bf16[2,32,64,128]{3,2,1,0:T(8,128)(2,1)} %mirror_logits.6.refs_0_.refs_8_, ...), custom_call_target="tpu_custom_call" | custom-call | flops 536870912 | bytes 3145728 | tf_op jit(solution)/shard_map/mirror_logits/pallas_call | solution.py:85
  87.2 17.2 %pair_step.4 = (bf16[128,256,128]{2,1,0:T(8,128)(2,1)}, bf16[32,16,256]{2,1,0:T(8,128)(2,1)}) custom-call(s32[2]{0:T(128)} %pad_add_fusion.part_ref, bf16[128,256,128]{2,1,0:T(8,128)(2,1)} %pair_ref.15, bf16[32,64,128]{2,1,0:T(8,128)(2,1)} %copy-done.23, bf16[32,64,128]{2,1,0:T(8,128)(2,1)} %copy-done.24, s32[128,256]{1,0:T(8,128)} %refs_2_.7, ...), custom_call_target="tpu_custom_call" | custom-call | flops 8589934592 | bytes 6291456 | tf_op jit(solution)/shard_map/pair_step/pallas_call | solution.py:272
  107.5 2.7 %collective-permute-start.10 = (bf16[32,64,128]{2,1,0:T(8,128)(2,1)}, bf16[32,64,128]{2,1,0:T(8,128)(2,1)S(1)}, u32[]{:S(2)}, u32[]{:S(2)}) collective-permute-start(bf16[32,64,128]{2,1,0:T(8,128)(2,1)} %get-tuple-element.26.refs_10_), channel_id=1, source_target_pairs={{16,0},{20,4},{24,8},{28,12},{18,16},{22,20},{26,24},{30,28},{0,1}... | collective-permute-start | bytes 1572872 | tf_op jit(solution)/shard_map/ppermute | solution.py:459
  111.2 17.2 %pair_step.5 = (bf16[128,256,128]{2,1,0:T(8,128)(2,1)}, bf16[32,16,256]{2,1,0:T(8,128)(2,1)}) custom-call(s32[2]{0:T(128)} %pad_add_fusion.part_ref, bf16[128,256,128]{2,1,0:T(8,128)(2,1)} %pair_ref.15, bf16[32,64,128]{2,1,0:T(8,128)(2,1)} %copy-done.25, bf16[32,64,128]{2,1,0:T(8,128)(2,1)} %copy-done.26, ...), custom_call_target="tpu_custom_call", output_to_operand_aliasing={{0}: (10, {})} | custom-call | flops 8589934592 | bytes 6291456 | tf_op jit(solution)/shard_map/pair_step/pallas_call | solution.py:272
  134.6 17.2 %pair_step.6 = (bf16[128,256,128]{2,1,0:T(8,128)(2,1)}, bf16[32,16,256]{2,1,0:T(8,128)(2,1)}) custom-call(s32[2]{0:T(128)} %pad_add_fusion.part_ref, bf16[128,256,128]{2,1,0:T(8,128)(2,1)} %pair_ref.15, bf16[32,64,128]{2,1,0:T(8,128)(2,1)} %copy-done.27, bf16[32,64,128]{2,1,0:T(8,128)(2,1)} %copy-done.28, ...), custom_call_target="tpu_custom_call", output_to_operand_aliasing={{0}: (10, {})} | custom-call | flops 8589934592 | bytes 6291456 | tf_op jit(solution)/shard_map/pair_step/pallas_call | solution.py:272
  151.8 5.1 %collective-permute-done.7.refs_4_.refs_1_ = bf16[32,64,128]{2,1,0:T(8,128)(2,1)S(1)} collective-permute-done((bf16[32,64,128]{2,1,0:T(8,128)(2,1)}, bf16[32,64,128]{2,1,0:T(8,128)(2,1)S(1)}, u32[]{:S(2)}, u32[]{:S(2)}) %collective-permute-start.7) | collective-permute-done | bytes 524320 | tf_op jit(solution)/shard_map/ppermute | solution.py:459
  159.8 6.3 %all-to-all-start = ((bf16[32,48,256]{2,1,0:T(8,128)(2,1)}), bf16[32,48,256]{2,1,0:T(8,128)(2,1)S(1)}, u32[]{:S(2)}, u32[]{:S(2)}) async-start(bf16[32,48,256]{2,1,0:T(8,128)(2,1)} %join.5.refs_9_), calls=%async_computation | async-start | bytes 1572864 | tf_op jit(solution)/shard_map/all_to_all | solution.py:499
  166.2 17.3 %pair_step.7 = (bf16[128,256,128]{2,1,0:T(8,128)(2,1)}, bf16[32,16,256]{2,1,0:T(8,128)(2,1)}) custom-call(s32[2]{0:T(128)} %pad_add_fusion.part_ref, bf16[128,256,128]{2,1,0:T(8,128)(2,1)} %pair_ref.15, bf16[32,64,128]{2,1,0:T(8,128)(2,1)} %copy-done.13, bf16[32,64,128]{2,1,0:T(8,128)(2,1)} %copy-done.14, ...), custom_call_target="tpu_custom_call", output_to_operand_aliasing={{0}: (10, {})} | custom-call | flops 8589934592 | bytes 6291456 | tf_op jit(solution)/shard_map/pair_step/pallas_call | solution.py:272
  183.5 2.2 %all-to-all-done.refs_0_ = bf16[32,48,256]{2,1,0:T(8,128)(2,1)S(1)} async-done(((bf16[32,48,256]{2,1,0:T(8,128)(2,1)}), bf16[32,48,256]{2,1,0:T(8,128)(2,1)S(1)}, u32[]{:S(2)}, u32[]{:S(2)}) %all-to-all-start) | async-done | bytes 786464 | tf_op jit(solution)/shard_map/all_to_all | solution.py:499
  185.7 4.6 %all-to-all-start.1 = ((bf16[32,16,256]{2,1,0:T(8,128)(2,1)}), bf16[32,16,256]{2,1,0:T(8,128)(2,1)S(1)}, u32[]{:S(2)}, u32[]{:S(2)}) async-start(bf16[32,16,256]{2,1,0:T(8,128)(2,1)} %get-tuple-element.37), calls=%async_computation.1 | async-start | bytes 524288 | tf_op jit(solution)/shard_map/all_to_all | solution.py:509
  193.3 7.0 %all-to-all-done.1.refs_1_ = bf16[32,16,256]{2,1,0:T(8,128)(2,1)S(1)} async-done(((bf16[32,16,256]{2,1,0:T(8,128)(2,1)}), bf16[32,16,256]{2,1,0:T(8,128)(2,1)S(1)}, u32[]{:S(2)}, u32[]{:S(2)}) %all-to-all-start.1) | async-done | bytes 262176 | tf_op jit(solution)/shard_map/all_to_all | solution.py:509
  201.0 5.0 %transition.1 = bf16[2,64,1024]{2,1,0:T(8,128)(2,1)} custom-call(bf16[2,64,1024]{2,1,0:T(8,128)(2,1)} %entry_ref.1, bf16[2,64,1024]{2,1,0:T(8,128)(2,1)} %arriving_ref.1, f32[64,1]{1,0:T(8,128)} %copy.23.mean_gain_ref, f32[64,1]{1,0:T(8,128)} %copy.24.gain_ref, bf16[512,64]{1,0:T(8,128)(2,1)} %copy.25.gate_up_t_ref, bf16[64,512]{1,0:T(8,128)(2,1)} %copy-done.15, ...), custom_call_target="tpu_custom_call" | custom-call | tf_op jit(solution)/shard_map/transition/pallas_call | solution.py:387
  (103 shorter events, 33.7 us)
Async XLA Ops:
  2.4 12.8 %collective-permute-start = (bf16[8,64,256]{2,1,0:T(8,128)(2,1)}, bf16[8,64,256]{2,1,0:T(8,128)(2,1)S(1)}, u32[]{:S(2)}, u32[]{:S(2)}) collective-permute-start(bf16[8,64,256]{2,1,0:T(8,128)(2,1)} %join.3.refs_0_), channel_id=1, source_target_pairs={{8,0},{12,4},{0,8},{4,12},{24,16},{28,20},{16,24},{20,28},{9,1},{1... | collective-permute-start | bytes 786440 | tf_op jit(solution)/shard_map/ppermute | solution.py:442
  5.3 14.1 %collective-permute-start.1 = (bf16[8,64,256]{2,1,0:T(8,128)(2,1)}, bf16[8,64,256]{2,1,0:T(8,128)(2,1)S(1)}, u32[]{:S(2)}, u32[]{:S(2)}) collective-permute-start(bf16[8,64,256]{2,1,0:T(8,128)(2,1)} %join.3.refs_0_), channel_id=1, source_target_pairs={{16,0},{20,4},{24,8},{28,12},{0,16},{4,20},{8,24},{12,28},{17,1},{... | collective-permute-start | bytes 786440 | tf_op jit(solution)/shard_map/ppermute | solution.py:442
  6.8 32.5 %collective-permute-start.2 = (bf16[8,64,256]{2,1,0:T(8,128)(2,1)}, bf16[8,64,256]{2,1,0:T(8,128)(2,1)S(1)}, u32[]{:S(2)}, u32[]{:S(2)}) collective-permute-start(bf16[8,64,256]{2,1,0:T(8,128)(2,1)} %join.3.refs_0_), channel_id=1, source_target_pairs={{24,0},{28,4},{16,8},{20,12},{8,16},{12,20},{0,24},{4,28},{25,1},{... | collective-permute-start | bytes 786440 | tf_op jit(solution)/shard_map/ppermute | solution.py:442
  12.9 37.2 %collective-permute-start.3 = (bf16[2,32,64,128]{3,2,1,0:T(8,128)(2,1)}, bf16[2,32,64,128]{3,2,1,0:T(8,128)(2,1)S(1)}, u32[]{:S(2)}, u32[]{:S(2)}) collective-permute-start(bf16[2,32,64,128]{3,2,1,0:T(8,128)(2,1)} %mirror_logits.4.refs_0_), channel_id=1, source_target_pairs={{0,16},{4,20},{1,24},{5,28},{2,18},{6,22},{3,26},{7,30},{8,0},{12,... | collective-permute-start | bytes 3145736 | tf_op jit(solution)/shard_map/ppermute | solution.py:456
  15.2 24.2 %copy-start.8 = (bf16[8,64,256]{2,1,0:T(8,128)(2,1)}, bf16[8,64,256]{2,1,0:T(8,128)(2,1)S(1)}, u32[]{:S(2)}) copy-start(bf16[8,64,256]{2,1,0:T(8,128)(2,1)S(1)} %collective-permute-done.refs_1_) | copy-start | bytes 786436
  45.4 26.6 %collective-permute-start.4 = (bf16[2,32,64,128]{3,2,1,0:T(8,128)(2,1)}, bf16[2,32,64,128]{3,2,1,0:T(8,128)(2,1)S(1)}, u32[]{:S(2)}, u32[]{:S(2)}) collective-permute-start(bf16[2,32,64,128]{3,2,1,0:T(8,128)(2,1)} %mirror_logits.5.refs_0_), channel_id=1, source_target_pairs={{0,16},{4,20},{1,24},{5,28},{2,18},{6,22},{3,26},{7,30},{8,0},{12,... | collective-permute-start | bytes 3145736 | tf_op jit(solution)/shard_map/ppermute | solution.py:456
  47.8 21.5 %collective-permute-start.8 = (bf16[32,64,256]{2,1,0:T(8,128)(2,1)}, bf16[32,64,256]{2,1,0:T(8,128)(2,1)S(1)}, u32[]{:S(2)}, u32[]{:S(2)}) collective-permute-start(bf16[32,64,256]{2,1,0:T(8,128)(2,1)} %join.4), channel_id=1, source_target_pairs={{4,0},{0,4},{12,8},{8,12},{20,16},{16,20},{28,24},{24,28},{5,1},{1... | collective-permute-start | bytes 3145736 | tf_op jit(solution)/shard_map/ppermute | solution.py:471
  53.2 33.0 %collective-permute-start.14 = (bf16[32,64,128]{2,1,0:T(8,128)(2,1)}, bf16[32,64,128]{2,1,0:T(8,128)(2,1)S(1)}, u32[]{:S(2)}, u32[]{:S(2)}) collective-permute-start(bf16[32,64,128]{2,1,0:T(8,128)(2,1)} %get-tuple-element.20.refs_1_), channel_id=1, source_target_pairs={{16,0},{20,4},{24,8},{28,12},{18,16},{22,20},{26,24},{30,28},{0,1}... | collective-permute-start | bytes 1572872 | tf_op jit(solution)/shard_map/ppermute | solution.py:459
  58.9 27.4 %collective-permute-start.15 = (bf16[32,64,128]{2,1,0:T(8,128)(2,1)}, bf16[32,64,128]{2,1,0:T(8,128)(2,1)S(1)}, u32[]{:S(2)}, u32[]{:S(2)}) collective-permute-start(bf16[32,64,128]{2,1,0:T(8,128)(2,1)} %get-tuple-element.21.refs_2_), channel_id=1, source_target_pairs={{16,4},{20,0},{24,12},{28,8},{18,20},{22,16},{26,28},{30,24},{0,5}... | collective-permute-start | bytes 1572872 | tf_op jit(solution)/shard_map/ppermute | solution.py:459
  67.0 37.5 %collective-permute-start.9 = (bf16[2,32,64,128]{3,2,1,0:T(8,128)(2,1)}, bf16[2,32,64,128]{3,2,1,0:T(8,128)(2,1)S(1)}, u32[]{:S(2)}, u32[]{:S(2)}) collective-permute-start(bf16[2,32,64,128]{3,2,1,0:T(8,128)(2,1)} %mirror_logits.6.refs_0_.refs_8_), channel_id=1, source_target_pairs={{0,16},{4,20},{1,24},{5,28},{2,18},{6,22},{3,26},{7,30},{8,0},{12,... | collective-permute-start | bytes 3145736 | tf_op jit(solution)/shard_map/ppermute | solution.py:456
  75.1 35.2 %collective-permute-start.12 = (bf16[32,64,128]{2,1,0:T(8,128)(2,1)}, bf16[32,64,128]{2,1,0:T(8,128)(2,1)S(1)}, u32[]{:S(2)}, u32[]{:S(2)}) collective-permute-start(bf16[32,64,128]{2,1,0:T(8,128)(2,1)} %get-tuple-element.22.refs_1_.refs_9_), channel_id=1, source_target_pairs={{16,0},{20,4},{24,8},{28,12},{18,16},{22,20},{26,24},{30,28},{0,1}... | collective-permute-start | bytes 1572872 | tf_op jit(solution)/shard_map/ppermute | solution.py:459
  80.9 29.4 %collective-permute-start.13 = (bf16[32,64,128]{2,1,0:T(8,128)(2,1)}, bf16[32,64,128]{2,1,0:T(8,128)(2,1)S(1)}, u32[]{:S(2)}, u32[]{:S(2)}) collective-permute-start(bf16[32,64,128]{2,1,0:T(8,128)(2,1)} %get-tuple-element.23.refs_2_.refs_10_), channel_id=1, source_target_pairs={{16,4},{20,0},{24,12},{28,8},{18,20},{22,16},{26,28},{30,24},{0,5}... | collective-permute-start | bytes 1572872 | tf_op jit(solution)/shard_map/ppermute | solution.py:459
  86.2 42.2 %collective-permute-start.5 = (bf16[2,32,64,128]{3,2,1,0:T(8,128)(2,1)}, bf16[2,32,64,128]{3,2,1,0:T(8,128)(2,1)S(1)}, u32[]{:S(2)}, u32[]{:S(2)}) collective-permute-start(bf16[2,32,64,128]{3,2,1,0:T(8,128)(2,1)} %mirror_logits.7.refs_9_), channel_id=1, source_target_pairs={{0,16},{4,20},{1,24},{5,28},{2,18},{6,22},{3,26},{7,30},{8,0},{12,... | collective-permute-start | bytes 3145736 | tf_op jit(solution)/shard_map/ppermute | solution.py:456
  107.5 25.0 %collective-permute-start.10 = (bf16[32,64,128]{2,1,0:T(8,128)(2,1)}, bf16[32,64,128]{2,1,0:T(8,128)(2,1)S(1)}, u32[]{:S(2)}, u32[]{:S(2)}) collective-permute-start(bf16[32,64,128]{2,1,0:T(8,128)(2,1)} %get-tuple-element.26.refs_10_), channel_id=1, source_target_pairs={{16,0},{20,4},{24,8},{28,12},{18,16},{22,20},{26,24},{30,28},{0,1}... | collective-permute-start | bytes 1572872 | tf_op jit(solution)/shard_map/ppermute | solution.py:459
  110.2 23.6 %collective-permute-start.11 = (bf16[32,64,128]{2,1,0:T(8,128)(2,1)}, bf16[32,64,128]{2,1,0:T(8,128)(2,1)S(1)}, u32[]{:S(2)}, u32[]{:S(2)}) collective-permute-start(bf16[32,64,128]{2,1,0:T(8,128)(2,1)} %get-tuple-element.27.refs_11_), channel_id=1, source_target_pairs={{16,4},{20,0},{24,12},{28,8},{18,20},{22,16},{26,28},{30,24},{0,5}... | collective-permute-start | bytes 1572872 | tf_op jit(solution)/shard_map/ppermute | solution.py:459
  131.4 20.3 %collective-permute-start.6 = (bf16[32,64,128]{2,1,0:T(8,128)(2,1)}, bf16[32,64,128]{2,1,0:T(8,128)(2,1)S(1)}, u32[]{:S(2)}, u32[]{:S(2)}) collective-permute-start(bf16[32,64,128]{2,1,0:T(8,128)(2,1)} %get-tuple-element.24.refs_9_), channel_id=1, source_target_pairs={{16,0},{20,4},{24,8},{28,12},{18,16},{22,20},{26,24},{30,28},{0,1}... | collective-permute-start | bytes 1572872 | tf_op jit(solution)/shard_map/ppermute | solution.py:459
  132.1 24.8 %collective-permute-start.7 = (bf16[32,64,128]{2,1,0:T(8,128)(2,1)}, bf16[32,64,128]{2,1,0:T(8,128)(2,1)S(1)}, u32[]{:S(2)}, u32[]{:S(2)}) collective-permute-start(bf16[32,64,128]{2,1,0:T(8,128)(2,1)} %get-tuple-element.25.refs_10_), channel_id=1, source_target_pairs={{16,4},{20,0},{24,12},{28,8},{18,20},{22,16},{26,28},{30,24},{0,5}... | collective-permute-start | bytes 1572872 | tf_op jit(solution)/shard_map/ppermute | solution.py:459
  159.8 25.9 %all-to-all-start = ((bf16[32,48,256]{2,1,0:T(8,128)(2,1)}), bf16[32,48,256]{2,1,0:T(8,128)(2,1)S(1)}, u32[]{:S(2)}, u32[]{:S(2)}) async-start(bf16[32,48,256]{2,1,0:T(8,128)(2,1)} %join.5.refs_9_), calls=%async_computation | async-start | bytes 1572864 | tf_op jit(solution)/shard_map/all_to_all | solution.py:499
  166.1 24.2 %copy-start.17 = (bf16[64,256]{1,0:T(8,128)(2,1)S(1)}, bf16[64,256]{1,0:T(8,128)(2,1)}, u32[]{:S(2)}) copy-start(bf16[64,256]{1,0:T(8,128)(2,1)} %param.27) | copy-start | bytes 98308
  166.1 24.2 %copy-start.18 = (bf16[64,256]{1,0:T(8,128)(2,1)S(1)}, bf16[64,256]{1,0:T(8,128)(2,1)}, u32[]{:S(2)}) copy-start(bf16[64,256]{1,0:T(8,128)(2,1)} %param.28) | copy-start | bytes 98308
  166.1 25.0 %copy-start.16 = (bf16[256,64]{0,1:T(8,128)(2,1)S(1)}, bf16[256,64]{0,1:T(8,128)(2,1)}, u32[]{:S(2)}) copy-start(bf16[256,64]{0,1:T(8,128)(2,1)} %param.29) | copy-start | bytes 98308
  166.2 25.7 %copy-start.21 = (f32[64]{0:T(128)S(1)}, f32[64]{0:T(128)}, u32[]{:S(2)}) copy-start(f32[64]{0:T(128)} %param.25) | copy-start | bytes 772
  166.2 26.4 %copy-start.22 = (f32[64]{0:T(128)S(1)}, f32[64]{0:T(128)}, u32[]{:S(2)}) copy-start(f32[64]{0:T(128)} %param.26) | copy-start | bytes 772
  185.7 14.6 %all-to-all-start.1 = ((bf16[32,16,256]{2,1,0:T(8,128)(2,1)}), bf16[32,16,256]{2,1,0:T(8,128)(2,1)S(1)}, u32[]{:S(2)}, u32[]{:S(2)}) async-start(bf16[32,16,256]{2,1,0:T(8,128)(2,1)} %get-tuple-element.37), calls=%async_computation.1 | async-start | bytes 524288 | tf_op jit(solution)/shard_map/all_to_all | solution.py:509
  (23 other events, 93.7 us)

commit v4 on v3

--- a/solution.py
+++ b/solution.py
@@ -9,8 +9,10 @@
 
 BF16, F32 = jnp.bfloat16, jnp.float32
 VMEM_BYTES = 56 * 1024 * 1024
+LEAN_BYTES = 32 * 1024 * 1024
 AXES = ("row", "col")
 GROUP = 4
+SHORT = pl.CostEstimate(flops=0, bytes_accessed=0, transcendentals=0)
 
 
 def contract(lhs, rhs, lhs_dim, rhs_dim):
@@ -100,62 +102,87 @@
         ),
         out_shape=jax.ShapeDtypeStruct((parts, chunk_rows, bins, rows), BF16),
         compiler_params=pltpu.CompilerParams(vmem_limit_bytes=VMEM_BYTES),
-        cost_estimate=pl.CostEstimate(
-            flops=2 * parts * chunk_rows * rows * bins * width * 4,
-            bytes_accessed=parts * chunk_rows * rows * (width + bins) * 2,
-            transcendentals=0,
-        ),
+        cost_estimate=SHORT,
         name="mirror_logits",
     )(part, pair_activation, weight_t, bias, *ahead)
 
 
-def split_kernel(in_ref, *outs):
-    for n, out_ref in enumerate(outs):
+def tie_kernel(*refs):
+    pass
+
+
+def tie(array, ahead):
+    anywhere = pl.BlockSpec(memory_space=pl.ANY)
+    return pl.pallas_call(
+        tie_kernel,
+        in_specs=[anywhere] * (1 + len(ahead)),
+        out_specs=anywhere,
+        out_shape=jax.ShapeDtypeStruct(array.shape, array.dtype),
+        input_output_aliases={0: 0},
+        compiler_params=pltpu.CompilerParams(vmem_limit_bytes=LEAN_BYTES),
+        name="tie",
+    )(array, *ahead)
+
+
+def split_kernel(in_ref, *refs):
+    for n, out_ref in enumerate(refs[-in_ref.shape[0] :]):
         out_ref[...] = in_ref[n]
 
 
-def split(array):
+def split(array, ahead):
     count, rows, *rest = array.shape
     step = min(16, rows)
     return pl.pallas_call(
         split_kernel,
         grid=(rows // step,),
-        in_specs=[pl.BlockSpec((count, step, *rest), lambda s: (0, s, 0, 0))],
+        in_specs=[pl.BlockSpec((count, step, *rest), lambda s: (0, s, 0, 0))]
+        + [pl.BlockSpec(memory_space=pl.ANY)] * len(ahead),
         out_specs=[pl.BlockSpec((step, *rest), lambda s: (s, 0, 0))] * count,
         out_shape=[jax.ShapeDtypeStruct(array.shape[1:], array.dtype)] * count,
-        compiler_params=pltpu.CompilerParams(vmem_limit_bytes=VMEM_BYTES),
+        compiler_params=pltpu.CompilerParams(vmem_limit_bytes=LEAN_BYTES),
         name="split",
-    )(array)
+    )(array, *ahead)
 
 
 def join_kernel(axis, count, *refs):
     out_ref = refs[-1]
-    width = refs[0].shape[axis]
-    for n, ref in enumerate(refs[:count]):
+    at = 0
+    for ref in refs[:count]:
+        end = at + ref.shape[axis]
         if axis:
-            out_ref[:, n * width : (n + 1) * width] = ref[...]
+            out_ref[:, at:end] = ref[...]
         else:
-            out_ref[n * width : (n + 1) * width] = ref[...]
+            out_ref[at:end] = ref[...]
+        at = end
 
 
 def join(arrays, axis, ahead=()):
     shape = list(arrays[0].shape)
-    shape[axis] *= len(arrays)
+    shape[axis] = sum(array.shape[axis] for array in arrays)
     vmem = pl.BlockSpec(memory_space=pltpu.VMEM)
     return pl.pallas_call(
         functools.partial(join_kernel, axis, len(arrays)),
         in_specs=[vmem] * len(arrays) + [pl.BlockSpec(memory_space=pl.ANY)] * len(ahead),
         out_specs=vmem,
         out_shape=jax.ShapeDtypeStruct(shape, BF16),
-        compiler_params=pltpu.CompilerParams(vmem_limit_bytes=VMEM_BYTES),
+        compiler_params=pltpu.CompilerParams(vmem_limit_bytes=LEAN_BYTES),
         name="join",
     )(*arrays, *ahead)
 
 
-def pair_kernel(parts, slots, front, tile, part_ref, pair_ref, *refs):
+def pair_kernel(parts, slots, front, tile, resident, part_ref, pair_ref, *refs):
     received = refs[:parts]
-    target_ref, weight_t_ref, weight_wide_ref, bias_ref, factor_hbm, mix_hbm = refs[parts : parts + 6]
-    grad_ref, norm_ref, slopes, factors, mix, mix_wide, mixed, total, sems = refs[-9:]
+    target_ref, weight_t_ref, weight_wide_ref, bias_ref, factors, mix = refs[parts : parts + 6]
+    if resident:
+        grad_ref, norm_ref, slopes, mix_wide, mixed, total = refs[-6:]
+        copies = []
+    else:
+        grad_ref, norm_ref, slopes, mix_wide, mixed, total, factor_copy, mix_copy, sems = refs[-9:]
+        copies = [
+            pltpu.make_async_copy(factors, factor_copy, sems.at[0]),
+            pltpu.make_async_copy(mix, mix_copy, sems.at[1]),
+        ]
+        factors, mix = factor_copy, mix_copy
     step = pl.program_id(0)
     step_rows, cols, width = pair_ref.shape
     bins = weight_t_ref.shape[0]
@@ -166,10 +193,7 @@
     device_seqs = device_rows // groups
     seqs = devices * device_seqs
     xs = mix.shape[0]
-    copies = [
-        pltpu.make_async_copy(factor_hbm, factors, sems.at[0]),
-        pltpu.make_async_copy(mix_hbm, mix, sems.at[1]),
-    ]
+    base = step * step_rows if resident else 0
 
     @pl.when(step == 0)
     def _():
@@ -191,10 +215,10 @@
                 own = (contract(weight_t, pair_ref[i], 1, 1) + bias).astype(BF16).astype(F32)
                 halves = []
                 for u in range(parts):
-                    half = received[0][i]
+                    half = received[0][base + i]
                     for shift in range(1, parts):
                         half = jnp.where(
-                            lax.rem(h + parts - u, parts) == shift, received[shift][i], half
+                            lax.rem(h + parts - u, parts) == shift, received[shift][base + i], half
                         )
                     halves.append(half)
                 symmetric = own + jnp.concatenate(halves, axis=1).astype(F32)
@@ -253,7 +277,7 @@
 
 def pair_step(
     part, pair_activation, received, targets, weight_t, weight_wide, bias, factors, mix, grad,
-    first_row, seqs, devices, slots, ahead,
+    first_row, seqs, devices, slots, ahead, resident,
 ):
     _, cols, width = pair_activation.shape
     bins = weight_t.shape[0]
@@ -266,48 +290,54 @@
     tile = max(1, min(8, 512 // seqs))
     front = chunk_rows // step_rows
     near = lambda s: jnp.minimum(s, front - 1)
+    anywhere = pl.BlockSpec(memory_space=pl.ANY)
+    if resident:
+        held = moved = pl.BlockSpec(memory_space=pltpu.VMEM)
+    else:
+        held = pl.BlockSpec((step_rows, bins, cols // parts), lambda s, p: (near(s), 0, 0))
+        moved = anywhere
     there = lambda s: first_row // step_rows + jnp.minimum(s, front - 1)
     const2 = lambda s, p: (0, 0)
     norm_shape = (devices, seqs // devices * groups, GROUP * features)
     return pl.pallas_call(
-        functools.partial(pair_kernel, parts, slots, front, tile),
+        functools.partial(pair_kernel, parts, slots, front, tile, resident),
         grid_spec=pltpu.PrefetchScalarGridSpec(
             num_scalar_prefetch=1,
             grid=(front + 1,),
             in_specs=[pl.BlockSpec((step_rows, cols, width), lambda s, p: (there(s), 0, 0))]
-            + [pl.BlockSpec((step_rows, bins, cols // parts), lambda s, p: (near(s), 0, 0))] * parts
+            + [held] * parts
             + [
                 pl.BlockSpec((step_rows, cols), lambda s, p: (there(s), 0)),
                 pl.BlockSpec((bins, width), const2),
                 pl.BlockSpec((GROUP * bins, GROUP * width), const2),
                 pl.BlockSpec((1, bins), const2),
             ]
-            + [pl.BlockSpec(memory_space=pl.ANY)] * (2 + len(grad) + len(ahead)),
+            + [moved] * 2
+            + [pl.BlockSpec(memory_space=pltpu.HBM)] * len(grad)
+            + [anywhere] * len(ahead),
             out_specs=[
                 pl.BlockSpec((step_rows, cols, width), lambda s, p: (there(s), 0, 0)),
                 pl.BlockSpec(norm_shape, lambda s, p: (0, 0, 0)),
             ],
             scratch_shapes=[
                 pltpu.VMEM((groups, cols, GROUP * bins), BF16),
-                pltpu.VMEM(factors.shape, BF16),
-                pltpu.VMEM(mix.shape, BF16),
                 pltpu.VMEM((tile * GROUP * bins, GROUP * features), BF16),
                 pltpu.VMEM((groups * seqs, tile * GROUP * bins), BF16),
                 pltpu.VMEM((GROUP * features // 128, groups * seqs, 128), F32),
+            ]
+            + ([] if resident else [
+                pltpu.VMEM(factors.shape, BF16),
+                pltpu.VMEM(mix.shape, BF16),
                 pltpu.SemaphoreType.DMA((2,)),
-            ],
+            ]),
         ),
         out_shape=[
             jax.ShapeDtypeStruct(pair_activation.shape, BF16),
             jax.ShapeDtypeStruct(norm_shape, BF16),
         ],
         input_output_aliases={parts + 8: 0} if grad else {},
-        compiler_params=pltpu.CompilerParams(vmem_limit_bytes=VMEM_BYTES),
-        cost_estimate=pl.CostEstimate(
-            flops=4 * xs * seqs * cols * chunk_rows * bins,
-            bytes_accessed=chunk_rows * cols * width * 6,
-            transcendentals=chunk_rows * cols * bins,
-        ),
+        compiler_params=pltpu.CompilerParams(vmem_limit_bytes=LEAN_BYTES if resident else VMEM_BYTES),
+        cost_estimate=SHORT,
         name="pair_step",
     )(part, pair_activation, *received, targets, weight_t, weight_wide, bias, factors, mix, *grad,
       *ahead)
@@ -441,26 +471,6 @@
         pairs = [((n ^ flip) * parts + h, n * parts + h) for n in range(blocks) for h in range(parts)]
         others.append(lax.ppermute(own, "row", pairs))
 
-    chunks = chunk_plan(rows)
-    leg_pairs = first_leg(col_devices, parts)
-    logits, relayed, received = [], [], []
-    for first_row, chunk_rows in chunks:
-        n = len(logits)
-        ahead = [x for arrays in logits[-1:] + relayed[: max(0, n - 1)][-1:] for x in arrays]
-        if n == 1:
-            ahead += others
-        pieces = mirror_logits(
-            part, pair_activation, weight_t, bias, first_row, chunk_rows, parts, ahead
-        )
-        logits.append([pieces])
-        relayed.append(split(lax.ppermute(pieces, AXES, leg_pairs)))
-        received.append(
-            [
-                lax.ppermute(piece, AXES, second_leg(col_devices, parts, shift))
-                for shift, piece in enumerate(relayed[-1])
-            ]
-        )
-
     across = join([own] + others, 0)
     shifted = [across]
     for shift in range(1, parts):
@@ -486,23 +496,56 @@
     mix = jnp.concatenate([mix, mix], axis=2)
 
     devices = row_devices * col_devices
-    grad = ()
-    norm_parts = []
     exchange = functools.partial(
         lax.all_to_all, axis_name=AXES, split_axis=0, concat_axis=0, tiled=True
     )
-    arrived = []
-    for n, ((first_row, chunk_rows), pieces) in enumerate(zip(chunks, received)):
-        ahead = [x for arrays in logits[n + 2 : n + 3] + relayed[n + 1 : n + 2] for x in arrays]
-        if n == len(chunks) - 1 and n > 0:
-            early = join(norm_parts, 1, pieces)
-            arrived.append(exchange(early))
-            ahead.append(early)
-        *grad, norm_part = pair_step(
-            part, pair_activation, pieces, target_distance_bins, weight_t, weight_wide, bias,
-            factors, mix, grad, first_row, seqs, devices, row_devices, ahead,
-        )
-        norm_parts.append(norm_part)
+    chunks = chunk_plan(rows)
+    count = len(chunks)
+    leg_pairs = first_leg(col_devices, parts)
+    first, logits, sent, relayed, received = [], [], [], [], []
+    norm_parts, arrived, grad = [], [], []
+    for n in range(count + 2):
+        while len(first) < min(2, count):
+            first.append(
+                mirror_logits(
+                    part, pair_activation, weight_t, bias, *chunks[len(first)], parts, first[-1:]
+                )
+            )
+        for m in range(len(logits), min(count, n + 2)):
+            before = others if m < 2 else relayed[m - 2] + sum(received[: m - 2][-1:], [])
+            logits.append(tie(first[m], before))
+            sent.append(lax.ppermute(logits[m], AXES, leg_pairs))
+        while len(first) < count:
+            first.append(
+                mirror_logits(
+                    part, pair_activation, weight_t, bias, *chunks[len(first)], parts,
+                    logits[-1:] if len(first) == 2 else first[-1:],
+                )
+            )
+        if n >= min(2, count):
+            now = n - min(2, count)
+            if now < count:
+                ahead = logits[n : n + 1] + [x for arrays in relayed[now + 1 :] for x in arrays]
+                if now == count - 1 and now > 0:
+                    early = join(norm_parts, 1, received[now])
+                    arrived.append(exchange(early))
+                    ahead = [early]
+                *grad, norm_part = pair_step(
+                    part, pair_activation, received[now], target_distance_bins, weight_t,
+                    weight_wide, bias, factors, mix, grad, chunks[now][0], seqs, devices,
+                    row_devices, ahead, now < count - 1,
+                )
+                norm_parts.append(norm_part)
+        if n < count:
+            before = [[across, mix, weight_wide], [factors]][n] if n < 2 else [norm_parts[n - 2]]
+            before = before + (first[2:] if n == 0 else logits[n + 1 : n + 2])
+            relayed.append(list(split(sent[n], before)))
+            received.append(
+                [
+                    lax.ppermute(piece, AXES, second_leg(col_devices, parts, shift))
+                    for shift, piece in enumerate(relayed[n])
+                ]
+            )
     final = norm_parts[-1]
     if arrived:
         final, arrived[0] = lax.optimization_barrier((final, arrived[0]))

time: 207 us -> 191 us (0.923)
  Pallas kernels: 110 us -> 92.4 us
  local copies, waits for them, and re-layouts: 15 us -> 9.67 us
  waiting for transfers between devices: 39.8 us -> 44.9 us
    ppermute x3, waiting for transfers between devices: 24.2 us -> 0.08 us  [per_device(): others.append(lax.ppermute(own, 'row', pairs))]
    ppermute x4, waiting for transfers between devices: 0.01 us -> 22.5 us  [per_device(): sent.append(lax.ppermute(logits[m], AXES, leg_pairs))]
    pallas_call x4, Pallas kernels: 8.26 us -> 0.78 us  [split(): pl.pallas_call(split_kernel, grid=(rows // step,), in_specs=[pl.BlockSpec...]
    ppermute x8, waiting for transfers between devices: 6.37 us -> 13.1 us  [per_device(): lax.ppermute(piece, AXES, second_leg(col_devices, parts, shift))]
    pallas_call x4 -> x8, Pallas kernels: 69 us -> 63.8 us  [the longest x4 63.8 us: pair_step(): pl.pallas_call(functools.partial(pair_kernel, parts, slots, front, tile,...]
    pallas_call x3, Pallas kernels: 6.06 us -> 1.02 us  [join(): pl.pallas_call(functools.partial(join_kernel, axis, len(arrays)), in_spec...]
    unnamed x61 -> x65, local copies, waits for them, and re-layouts: 10.3 us -> 6.31 us
    ppermute x4, starting transfers between devices: 2.1 us -> 4.44 us  [per_device(): sent.append(lax.ppermute(logits[m], AXES, leg_pairs))]
  transfers between devices with their start and end apart: 18 -> 18, of which waited for: 6 -> 9; matrix products, arithmetic and copies ran while one was open for 6% -> 5% of each run, Pallas kernels for 49% -> 45%
where the time goes in v4:
time: 191 us; the launch traced here: 190 us
  Pallas kernels  92.4 us (48%)
  waiting for transfers between devices  44.9 us (24%)
  starting transfers between devices  36.3 us (19%)
  local copies, waits for them, and re-layouts  9.67 us (5%)
  other arithmetic  3.28 us (2%)
  matrix products  2.38 us (1%)
    pallas_call x4, Pallas kernels, pair_step(): pl.pallas_call(functools.partial(pair_kernel, parts, slots, front, tile,...  63.8 us
    ppermute x4, waiting for transfers between devices, per_device(): sent.append(lax.ppermute(logits[m], AXES, leg_pairs))  22.5 us
    pallas_call x4, Pallas kernels, mirror_logits(): pl.pallas_call(mirror_logits_kernel, grid_spec=pltpu.PrefetchScalarGridSp...  21.7 us
    ppermute x8, starting transfers between devices, per_device(): lax.ppermute(piece, AXES, second_leg(col_devices, parts, shift))  17.1 us
    ppermute x8, waiting for transfers between devices, per_device(): lax.ppermute(piece, AXES, second_leg(col_devices, parts, shift))  13.1 us
    all_to_all x1, waiting for transfers between devices, per_device(): arrived.append(exchange(final))  7.01 us
    unnamed x65, local copies, waits for them, and re-layouts  6.31 us
    all_to_all x1, starting transfers between devices, per_device(): arrived.append(exchange(early))  5.64 us
  transfers between devices with their start and end apart: 18, of which 9 were waited for; matrix products, arithmetic and copies ran while one was open for 5% of the time, Pallas kernels for 45%

profile of v4, /device:TPU:0, one launch (start us, length us, event | category | flops | bytes accessed | tf_op | source)
XLA Modules:
  0.0 190.1 jit_solution(15480454889950534497)
XLA Ops:
  2.5 3.0 %collective-permute-start = (bf16[8,64,256]{2,1,0:T(8,128)(2,1)S(1)}, bf16[8,64,256]{2,1,0:T(8,128)(2,1)S(1)}, u32[]{:S(2)}, u32[]{:S(2)}) collective-permute-start(bf16[8,64,256]{2,1,0:T(8,128)(2,1)S(1)} %join.3.refs_0_), channel_id=1, source_target_pairs={{8,0},{12,4},{0,8},{4,12},{24,16},{28,20},{16,24},{20,28},{9,1},{1... | collective-permute-start | bytes 786440 | tf_op jit(solution)/shard_map/ppermute | solution.py:472
  7.7 5.3 %mirror_logits.4.refs_0_ = bf16[2,32,64,128]{3,2,1,0:T(8,128)(2,1)} custom-call(s32[2]{0:T(128)} %pad_add_fusion.part_ref, bf16[128,256,128]{2,1,0:T(8,128)(2,1)} %pair_ref.15, bf16[64,128]{1,0:T(8,128)(2,1)} %bitcast.45, f32[1,64]{1,0:T(1,128)} %bitcast.54), custom_call_target="tpu_custom_call" | custom-call | tf_op jit(solution)/shard_map/mirror_logits/pallas_call | solution.py:87
  13.1 5.5 %mirror_logits.5.refs_0_ = bf16[2,32,64,128]{3,2,1,0:T(8,128)(2,1)} custom-call(s32[2]{0:T(128)} %pad_add_fusion.part_ref, bf16[128,256,128]{2,1,0:T(8,128)(2,1)} %pair_ref.15, bf16[64,128]{1,0:T(8,128)(2,1)} %bitcast.46, f32[1,64]{1,0:T(1,128)} %bitcast.55, bf16[2,32,64,128]{3,2,1,0:T(8,128)(2,1)} %mirror_logits.4.refs_0_), custom_call_target="tpu_custom_call" | custom-call | tf_op jit(solution)/shard_map/mirror_logits/pallas_call | solution.py:87
  26.1 5.4 %mirror_logits.6.refs_0_.refs_3_ = bf16[2,32,64,128]{3,2,1,0:T(8,128)(2,1)} custom-call(s32[2]{0:T(128)} %pad_add_fusion.part_ref, bf16[128,256,128]{2,1,0:T(8,128)(2,1)} %pair_ref.15, bf16[64,128]{1,0:T(8,128)(2,1)} %bitcast.47, f32[1,64]{1,0:T(1,128)} %bitcast.56, bf16[2,32,64,128]{3,2,1,0:T(8,128)(2,1)} %copy-done.9), custom_call_target="tpu_custom_call" | custom-call | tf_op jit(solution)/shard_map/mirror_logits/pallas_call | solution.py:87
  31.5 5.5 %mirror_logits.7.refs_4_.refs_0_ = bf16[2,32,64,128]{3,2,1,0:T(8,128)(2,1)} custom-call(s32[2]{0:T(128)} %pad_add_fusion.part_ref, bf16[128,256,128]{2,1,0:T(8,128)(2,1)} %pair_ref.15, bf16[64,128]{1,0:T(8,128)(2,1)} %bitcast.48, f32[1,64]{1,0:T(1,128)} %bitcast.57, bf16[2,32,64,128]{3,2,1,0:T(8,128)(2,1)} %mirror_logits.6.refs_0_.refs_3_), custom_call_target="tpu_custom_call" | custom-call | tf_op jit(solution)/shard_map/mirror_logits/pallas_call | solution.py:87
  37.0 8.1 %collective-permute-done.5.in_ref = bf16[2,32,64,128]{3,2,1,0:T(8,128)(2,1)S(1)} collective-permute-done((bf16[2,32,64,128]{3,2,1,0:T(8,128)(2,1)S(1)}, bf16[2,32,64,128]{3,2,1,0:T(8,128)(2,1)S(1)}, u32[]{:S(2)}, u32[]{:S(2)}) %collective-permute-start.5) | collective-permute-done | bytes 1048608 | tf_op jit(solution)/shard_map/ppermute | solution.py:517
  46.5 3.8 %collective-permute-start.6 = (bf16[32,64,128]{2,1,0:T(8,128)(2,1)S(1)}, bf16[32,64,128]{2,1,0:T(8,128)(2,1)S(1)}, u32[]{:S(2)}, u32[]{:S(2)}) collective-permute-start(bf16[32,64,128]{2,1,0:T(8,128)(2,1)S(1)} %get-tuple-element.20.refs_1_), channel_id=1, source_target_pairs={{16,0},{20,4},{24,8},{28,12},{18,16},{22,20},{26,24},{30,28},{0,1}... | collective-permute-start | bytes 1572872 | tf_op jit(solution)/shard_map/ppermute | solution.py:545
  53.1 14.4 %collective-permute-done.3.in_ref = bf16[2,32,64,128]{3,2,1,0:T(8,128)(2,1)S(1)} collective-permute-done((bf16[2,32,64,128]{3,2,1,0:T(8,128)(2,1)S(1)}, bf16[2,32,64,128]{3,2,1,0:T(8,128)(2,1)S(1)}, u32[]{:S(2)}, u32[]{:S(2)}) %collective-permute-start.3) | collective-permute-done | bytes 1048608 | tf_op jit(solution)/shard_map/ppermute | solution.py:517
  69.8 4.4 %collective-permute-start.10 = (bf16[32,64,128]{2,1,0:T(8,128)(2,1)S(1)}, bf16[32,64,128]{2,1,0:T(8,128)(2,1)S(1)}, u32[]{:S(2)}, u32[]{:S(2)}) collective-permute-start(bf16[32,64,128]{2,1,0:T(8,128)(2,1)S(1)} %get-tuple-element.23.refs_2_.refs_10_), channel_id=1, source_target_pairs={{16,4},{20,0},{24,12},{28,8},{18,20},{22,16},{26,28},{30,24},{0,5}... | collective-permute-start | bytes 1572872 | tf_op jit(solution)/shard_map/ppermute | solution.py:545
  75.9 15.5 %pair_step.4 = (bf16[128,256,128]{2,1,0:T(8,128)(2,1)}, bf16[32,16,256]{2,1,0:T(8,128)(2,1)S(1)}) custom-call(s32[2]{0:T(128)S(1)} %copy-done.18, bf16[128,256,128]{2,1,0:T(8,128)(2,1)S(1)} %bitcast.34, bf16[32,64,128]{2,1,0:T(8,128)(2,1)S(1)} %collective-permute-done.6.refs_3_.refs_0_, bf16[32,64,128]{2,1,0:T(8,128)(2,1)S(1)} %collective-permute-done.7.refs_4_.refs_1_, ...), custom_call_target="tpu_custom_call" | custom-call | tf_op jit(solution)/shard_map/pair_step/pallas_call | solution.py:302
  91.6 2.4 %collective-permute-start.14 = (bf16[32,64,128]{2,1,0:T(8,128)(2,1)S(1)}, bf16[32,64,128]{2,1,0:T(8,128)(2,1)S(1)}, u32[]{:S(2)}, u32[]{:S(2)}) collective-permute-start(bf16[32,64,128]{2,1,0:T(8,128)(2,1)S(1)} %get-tuple-element.26.refs_10_), channel_id=1, source_target_pairs={{16,0},{20,4},{24,8},{28,12},{18,16},{22,20},{26,24},{30,28},{0,1}... | collective-permute-start | bytes 1572872 | tf_op jit(solution)/shard_map/ppermute | solution.py:545
  94.1 3.7 %collective-permute-done.9.refs_0_ = bf16[32,64,128]{2,1,0:T(8,128)(2,1)S(1)} collective-permute-done((bf16[32,64,128]{2,1,0:T(8,128)(2,1)S(1)}, bf16[32,64,128]{2,1,0:T(8,128)(2,1)S(1)}, u32[]{:S(2)}, u32[]{:S(2)}) %collective-permute-start.9) | collective-permute-done | bytes 524320 | tf_op jit(solution)/shard_map/ppermute | solution.py:545
  97.7 15.5 %pair_step.5 = (bf16[128,256,128]{2,1,0:T(8,128)(2,1)}, bf16[32,16,256]{2,1,0:T(8,128)(2,1)S(1)}) custom-call(s32[2]{0:T(128)S(1)} %copy-done.18, bf16[128,256,128]{2,1,0:T(8,128)(2,1)S(1)} %bitcast.34, bf16[32,64,128]{2,1,0:T(8,128)(2,1)S(1)} %collective-permute-done.9.refs_0_, ...), custom_call_target="tpu_custom_call", output_to_operand_aliasing={{0}: (10, {})} | custom-call | tf_op jit(solution)/shard_map/pair_step/pallas_call | solution.py:302
  113.4 2.5 %collective-permute-start.12 = (bf16[32,64,128]{2,1,0:T(8,128)(2,1)S(1)}, bf16[32,64,128]{2,1,0:T(8,128)(2,1)S(1)}, u32[]{:S(2)}, u32[]{:S(2)}) collective-permute-start(bf16[32,64,128]{2,1,0:T(8,128)(2,1)S(1)} %get-tuple-element.29.refs_9_), channel_id=1, source_target_pairs={{16,0},{20,4},{24,8},{28,12},{18,16},{22,20},{26,24},{30,28},{0,1}... | collective-permute-start | bytes 1572872 | tf_op jit(solution)/shard_map/ppermute | solution.py:545
  116.0 2.2 %collective-permute-start.13 = (bf16[32,64,128]{2,1,0:T(8,128)(2,1)S(1)}, bf16[32,64,128]{2,1,0:T(8,128)(2,1)S(1)}, u32[]{:S(2)}, u32[]{:S(2)}) collective-permute-start(bf16[32,64,128]{2,1,0:T(8,128)(2,1)S(1)} %get-tuple-element.30.refs_10_), channel_id=1, source_target_pairs={{16,4},{20,0},{24,12},{28,8},{18,20},{22,16},{26,28},{30,24},{0,5}... | collective-permute-start | bytes 1572872 | tf_op jit(solution)/shard_map/ppermute | solution.py:545
  118.2 2.0 %collective-permute-done.15.refs_1_ = bf16[32,64,128]{2,1,0:T(8,128)(2,1)S(1)} collective-permute-done((bf16[32,64,128]{2,1,0:T(8,128)(2,1)S(1)}, bf16[32,64,128]{2,1,0:T(8,128)(2,1)S(1)}, u32[]{:S(2)}, u32[]{:S(2)}) %collective-permute-start.15) | collective-permute-done | bytes 524320 | tf_op jit(solution)/shard_map/ppermute | solution.py:545
  120.2 15.5 %pair_step.6 = (bf16[128,256,128]{2,1,0:T(8,128)(2,1)}, bf16[32,16,256]{2,1,0:T(8,128)(2,1)S(1)}) custom-call(s32[2]{0:T(128)S(1)} %copy-done.18, bf16[128,256,128]{2,1,0:T(8,128)(2,1)S(1)} %bitcast.34, bf16[32,64,128]{2,1,0:T(8,128)(2,1)S(1)} %collective-permute-done.14.refs_0_, ...), custom_call_target="tpu_custom_call", output_to_operand_aliasing={{0}: (10, {})} | custom-call | tf_op jit(solution)/shard_map/pair_step/pallas_call | solution.py:302
  135.7 6.2 %collective-permute-done.13.refs_4_.refs_1_ = bf16[32,64,128]{2,1,0:T(8,128)(2,1)S(1)} collective-permute-done((bf16[32,64,128]{2,1,0:T(8,128)(2,1)S(1)}, bf16[32,64,128]{2,1,0:T(8,128)(2,1)S(1)}, u32[]{:S(2)}, u32[]{:S(2)}) %collective-permute-start.13) | collective-permute-done | bytes 524320 | tf_op jit(solution)/shard_map/ppermute | solution.py:545
  144.5 5.6 %all-to-all-start = ((bf16[32,48,256]{2,1,0:T(8,128)(2,1)}), bf16[32,48,256]{2,1,0:T(8,128)(2,1)S(1)}, u32[]{:S(2)}, u32[]{:S(2)}) async-start(bf16[32,48,256]{2,1,0:T(8,128)(2,1)} %join.5.refs_9_), calls=%async_computation | async-start | bytes 1572864 | tf_op jit(solution)/shard_map/all_to_all | solution.py:531
  150.2 17.4 %pair_step.7 = (bf16[128,256,128]{2,1,0:T(8,128)(2,1)}, bf16[32,16,256]{2,1,0:T(8,128)(2,1)}) custom-call(s32[2]{0:T(128)} %pad_add_fusion.part_ref, bf16[128,256,128]{2,1,0:T(8,128)(2,1)} %pair_ref.15, bf16[32,64,128]{2,1,0:T(8,128)(2,1)} %copy-done.11, bf16[32,64,128]{2,1,0:T(8,128)(2,1)} %copy-done.12, ...), custom_call_target="tpu_custom_call", output_to_operand_aliasing={{0}: (10, {})} | custom-call | tf_op jit(solution)/shard_map/pair_step/pallas_call | solution.py:302
  167.6 2.2 %all-to-all-done.refs_0_ = bf16[32,48,256]{2,1,0:T(8,128)(2,1)S(1)} async-done(((bf16[32,48,256]{2,1,0:T(8,128)(2,1)}), bf16[32,48,256]{2,1,0:T(8,128)(2,1)S(1)}, u32[]{:S(2)}, u32[]{:S(2)}) %all-to-all-start) | async-done | bytes 786464 | tf_op jit(solution)/shard_map/all_to_all | solution.py:531
  169.8 4.6 %all-to-all-start.1 = ((bf16[32,16,256]{2,1,0:T(8,128)(2,1)}), bf16[32,16,256]{2,1,0:T(8,128)(2,1)S(1)}, u32[]{:S(2)}, u32[]{:S(2)}) async-start(bf16[32,16,256]{2,1,0:T(8,128)(2,1)} %get-tuple-element.37), calls=%async_computation.1 | async-start | bytes 524288 | tf_op jit(solution)/shard_map/all_to_all | solution.py:552
  177.3 7.0 %all-to-all-done.1.refs_1_ = bf16[32,16,256]{2,1,0:T(8,128)(2,1)S(1)} async-done(((bf16[32,16,256]{2,1,0:T(8,128)(2,1)}), bf16[32,16,256]{2,1,0:T(8,128)(2,1)S(1)}, u32[]{:S(2)}, u32[]{:S(2)}) %all-to-all-start.1) | async-done | bytes 262176 | tf_op jit(solution)/shard_map/all_to_all | solution.py:552
  185.0 5.0 %transition.1 = bf16[2,64,1024]{2,1,0:T(8,128)(2,1)} custom-call(bf16[2,64,1024]{2,1,0:T(8,128)(2,1)} %entry_ref.1, bf16[2,64,1024]{2,1,0:T(8,128)(2,1)} %arriving_ref.1, f32[64,1]{1,0:T(8,128)} %copy.27.mean_gain_ref, f32[64,1]{1,0:T(8,128)} %copy.28.gain_ref, bf16[512,64]{1,0:T(8,128)(2,1)} %copy.29.gate_up_t_ref, bf16[64,512]{1,0:T(8,128)(2,1)} %copy-done.21, ...), custom_call_target="tpu_custom_call" | custom-call | tf_op jit(solution)/shard_map/transition/pallas_call | solution.py:417
  (112 shorter events, 26.2 us)
Async XLA Ops:
  2.5 16.3 %collective-permute-start = (bf16[8,64,256]{2,1,0:T(8,128)(2,1)S(1)}, bf16[8,64,256]{2,1,0:T(8,128)(2,1)S(1)}, u32[]{:S(2)}, u32[]{:S(2)}) collective-permute-start(bf16[8,64,256]{2,1,0:T(8,128)(2,1)S(1)} %join.3.refs_0_), channel_id=1, source_target_pairs={{8,0},{12,4},{0,8},{4,12},{24,16},{28,20},{16,24},{20,28},{9,1},{1... | collective-permute-start | bytes 786440 | tf_op jit(solution)/shard_map/ppermute | solution.py:472
  5.5 13.4 %collective-permute-start.1 = (bf16[8,64,256]{2,1,0:T(8,128)(2,1)S(1)}, bf16[8,64,256]{2,1,0:T(8,128)(2,1)S(1)}, u32[]{:S(2)}, u32[]{:S(2)}) collective-permute-start(bf16[8,64,256]{2,1,0:T(8,128)(2,1)S(1)} %join.3.refs_0_), channel_id=1, source_target_pairs={{16,0},{20,4},{24,8},{28,12},{0,16},{4,20},{8,24},{12,28},{17,1},{... | collective-permute-start | bytes 786440 | tf_op jit(solution)/shard_map/ppermute | solution.py:472
  7.0 11.9 %collective-permute-start.2 = (bf16[8,64,256]{2,1,0:T(8,128)(2,1)S(1)}, bf16[8,64,256]{2,1,0:T(8,128)(2,1)S(1)}, u32[]{:S(2)}, u32[]{:S(2)}) collective-permute-start(bf16[8,64,256]{2,1,0:T(8,128)(2,1)S(1)} %join.3.refs_0_), channel_id=1, source_target_pairs={{24,0},{28,4},{16,8},{20,12},{8,16},{12,20},{0,24},{4,28},{25,1},{... | collective-permute-start | bytes 786440 | tf_op jit(solution)/shard_map/ppermute | solution.py:472
  18.8 101.4 %copy-start.6 = (bf16[32,8,4,128]{3,1,2,0:T(8,128)(2,1)}, bf16[32,8,4,128]{3,1,2,0:T(8,128)(2,1)S(1)}, u32[]{:S(2)}) copy-start(bf16[32,8,4,128]{3,1,2,0:T(8,128)(2,1)S(1)} %copy.35) | copy-start | bytes 786436
  18.9 26.1 %collective-permute-start.5 = (bf16[2,32,64,128]{3,2,1,0:T(8,128)(2,1)S(1)}, bf16[2,32,64,128]{3,2,1,0:T(8,128)(2,1)S(1)}, u32[]{:S(2)}, u32[]{:S(2)}) collective-permute-start(bf16[2,32,64,128]{3,2,1,0:T(8,128)(2,1)S(1)} %tie.5), channel_id=1, source_target_pairs={{0,16},{4,20},{1,24},{5,28},{2,18},{6,22},{3,26},{7,30},{8,0},{12,... | collective-permute-start | bytes 3145736 | tf_op jit(solution)/shard_map/ppermute | solution.py:517
  21.2 29.1 %collective-permute-start.4 = (bf16[32,64,256]{2,1,0:T(8,128)(2,1)S(1)}, bf16[32,64,256]{2,1,0:T(8,128)(2,1)}, u32[]{:S(2)}, u32[]{:S(2)}) collective-permute-start(bf16[32,64,256]{2,1,0:T(8,128)(2,1)S(1)} %join.4.refs_0_), channel_id=1, source_target_pairs={{4,0},{0,4},{12,8},{8,12},{20,16},{16,20},{28,24},{24,28},{5,1},{1... | collective-permute-start | bytes 3145736 | tf_op jit(solution)/shard_map/ppermute | solution.py:481
  22.4 45.2 %collective-permute-start.3 = (bf16[2,32,64,128]{3,2,1,0:T(8,128)(2,1)S(1)}, bf16[2,32,64,128]{3,2,1,0:T(8,128)(2,1)S(1)}, u32[]{:S(2)}, u32[]{:S(2)}) collective-permute-start(bf16[2,32,64,128]{3,2,1,0:T(8,128)(2,1)S(1)} %tie.4.refs_0_), channel_id=1, source_target_pairs={{0,16},{4,20},{1,24},{5,28},{2,18},{6,22},{3,26},{7,30},{8,0},{12,... | collective-permute-start | bytes 3145736 | tf_op jit(solution)/shard_map/ppermute | solution.py:517
  26.1 94.1 %copy-start.2 = (bf16[64,64,128]{2,1,0:T(8,128)(2,1)}, bf16[64,64,128]{2,1,0:T(8,128)(2,1)S(1)}, u32[]{:S(2)}) copy-start(bf16[64,64,128]{2,1,0:T(8,128)(2,1)S(1)} %pad_maximum_fusion.refs_1_.refs_7_) | copy-start | bytes 3145732
  46.5 21.2 %collective-permute-start.6 = (bf16[32,64,128]{2,1,0:T(8,128)(2,1)S(1)}, bf16[32,64,128]{2,1,0:T(8,128)(2,1)S(1)}, u32[]{:S(2)}, u32[]{:S(2)}) collective-permute-start(bf16[32,64,128]{2,1,0:T(8,128)(2,1)S(1)} %get-tuple-element.20.refs_1_), channel_id=1, source_target_pairs={{16,0},{20,4},{24,8},{28,12},{18,16},{22,20},{26,24},{30,28},{0,1}... | collective-permute-start | bytes 1572872 | tf_op jit(solution)/shard_map/ppermute | solution.py:545
  50.3 18.6 %collective-permute-start.7 = (bf16[32,64,128]{2,1,0:T(8,128)(2,1)S(1)}, bf16[32,64,128]{2,1,0:T(8,128)(2,1)S(1)}, u32[]{:S(2)}, u32[]{:S(2)}) collective-permute-start(bf16[32,64,128]{2,1,0:T(8,128)(2,1)S(1)} %get-tuple-element.21.refs_2_), channel_id=1, source_target_pairs={{16,4},{20,0},{24,12},{28,8},{18,20},{22,16},{26,28},{30,24},{0,5}... | collective-permute-start | bytes 1572872 | tf_op jit(solution)/shard_map/ppermute | solution.py:545
  50.3 41.1 %collective-permute-start.11 = (bf16[2,32,64,128]{3,2,1,0:T(8,128)(2,1)S(1)}, bf16[2,32,64,128]{3,2,1,0:T(8,128)(2,1)S(1)}, u32[]{:S(2)}, u32[]{:S(2)}) collective-permute-start(bf16[2,32,64,128]{3,2,1,0:T(8,128)(2,1)S(1)} %tie.6.refs_1_.refs_8_), channel_id=1, source_target_pairs={{0,16},{4,20},{1,24},{5,28},{2,18},{6,22},{3,26},{7,30},{8,0},{12,... | collective-permute-start | bytes 3145736 | tf_op jit(solution)/shard_map/ppermute | solution.py:517
  50.4 25.5 %slice-start = ((s8[8388608]{0:T(1024)(128)(4,1)}), s8[4194304]{0:T(1024)(128)(4,1)S(1)}, s32[]{:S(2)}) async-start(s8[8388608]{0:T(1024)(128)(4,1)} %bitcast.33), calls=%async_computation.2 | async-start | bytes 8388608
  53.1 67.1 %copy-start.1 = (bf16[64,64,256]{2,1,0:T(8,128)(2,1)}, bf16[64,64,256]{2,1,0:T(8,128)(2,1)S(1)}, u32[]{:S(2)}) copy-start(bf16[64,64,256]{2,1,0:T(8,128)(2,1)S(1)} %copy.25) | copy-start | bytes 6291460
  69.0 44.2 %collective-permute-start.8 = (bf16[2,32,64,128]{3,2,1,0:T(8,128)(2,1)S(1)}, bf16[2,32,64,128]{3,2,1,0:T(8,128)(2,1)S(1)}, u32[]{:S(2)}, u32[]{:S(2)}) collective-permute-start(bf16[2,32,64,128]{3,2,1,0:T(8,128)(2,1)S(1)} %tie.7.refs_1_.refs_9_), channel_id=1, source_target_pairs={{0,16},{4,20},{1,24},{5,28},{2,18},{6,22},{3,26},{7,30},{8,0},{12,... | collective-permute-start | bytes 3145736 | tf_op jit(solution)/shard_map/ppermute | solution.py:517
  69.8 24.2 %collective-permute-start.10 = (bf16[32,64,128]{2,1,0:T(8,128)(2,1)S(1)}, bf16[32,64,128]{2,1,0:T(8,128)(2,1)S(1)}, u32[]{:S(2)}, u32[]{:S(2)}) collective-permute-start(bf16[32,64,128]{2,1,0:T(8,128)(2,1)S(1)} %get-tuple-element.23.refs_2_.refs_10_), channel_id=1, source_target_pairs={{16,4},{20,0},{24,12},{28,8},{18,20},{22,16},{26,28},{30,24},{0,5}... | collective-permute-start | bytes 1572872 | tf_op jit(solution)/shard_map/ppermute | solution.py:545
  74.2 23.5 %collective-permute-start.9 = (bf16[32,64,128]{2,1,0:T(8,128)(2,1)S(1)}, bf16[32,64,128]{2,1,0:T(8,128)(2,1)S(1)}, u32[]{:S(2)}, u32[]{:S(2)}) collective-permute-start(bf16[32,64,128]{2,1,0:T(8,128)(2,1)S(1)} %get-tuple-element.22.refs_1_.refs_9_), channel_id=1, source_target_pairs={{16,0},{20,4},{24,8},{28,12},{18,16},{22,20},{26,24},{30,28},{0,1}... | collective-permute-start | bytes 1572872 | tf_op jit(solution)/shard_map/ppermute | solution.py:545
  91.6 26.5 %collective-permute-start.14 = (bf16[32,64,128]{2,1,0:T(8,128)(2,1)S(1)}, bf16[32,64,128]{2,1,0:T(8,128)(2,1)S(1)}, u32[]{:S(2)}, u32[]{:S(2)}) collective-permute-start(bf16[32,64,128]{2,1,0:T(8,128)(2,1)S(1)} %get-tuple-element.26.refs_10_), channel_id=1, source_target_pairs={{16,0},{20,4},{24,8},{28,12},{18,16},{22,20},{26,24},{30,28},{0,1}... | collective-permute-start | bytes 1572872 | tf_op jit(solution)/shard_map/ppermute | solution.py:545
  94.1 26.1 %collective-permute-start.15 = (bf16[32,64,128]{2,1,0:T(8,128)(2,1)S(1)}, bf16[32,64,128]{2,1,0:T(8,128)(2,1)S(1)}, u32[]{:S(2)}, u32[]{:S(2)}) collective-permute-start(bf16[32,64,128]{2,1,0:T(8,128)(2,1)S(1)} %get-tuple-element.27.refs_11_), channel_id=1, source_target_pairs={{16,4},{20,0},{24,12},{28,8},{18,20},{22,16},{26,28},{30,24},{0,5}... | collective-permute-start | bytes 1572872 | tf_op jit(solution)/shard_map/ppermute | solution.py:545
  113.4 22.3 %collective-permute-start.12 = (bf16[32,64,128]{2,1,0:T(8,128)(2,1)S(1)}, bf16[32,64,128]{2,1,0:T(8,128)(2,1)S(1)}, u32[]{:S(2)}, u32[]{:S(2)}) collective-permute-start(bf16[32,64,128]{2,1,0:T(8,128)(2,1)S(1)} %get-tuple-element.29.refs_9_), channel_id=1, source_target_pairs={{16,0},{20,4},{24,8},{28,12},{18,16},{22,20},{26,24},{30,28},{0,1}... | collective-permute-start | bytes 1572872 | tf_op jit(solution)/shard_map/ppermute | solution.py:545
  116.0 26.0 %collective-permute-start.13 = (bf16[32,64,128]{2,1,0:T(8,128)(2,1)S(1)}, bf16[32,64,128]{2,1,0:T(8,128)(2,1)S(1)}, u32[]{:S(2)}, u32[]{:S(2)}) collective-permute-start(bf16[32,64,128]{2,1,0:T(8,128)(2,1)S(1)} %get-tuple-element.30.refs_10_), channel_id=1, source_target_pairs={{16,4},{20,0},{24,12},{28,8},{18,20},{22,16},{26,28},{30,24},{0,5}... | collective-permute-start | bytes 1572872 | tf_op jit(solution)/shard_map/ppermute | solution.py:545
  144.5 25.3 %all-to-all-start = ((bf16[32,48,256]{2,1,0:T(8,128)(2,1)}), bf16[32,48,256]{2,1,0:T(8,128)(2,1)S(1)}, u32[]{:S(2)}, u32[]{:S(2)}) async-start(bf16[32,48,256]{2,1,0:T(8,128)(2,1)} %join.5.refs_9_), calls=%async_computation | async-start | bytes 1572864 | tf_op jit(solution)/shard_map/all_to_all | solution.py:531
  150.2 25.7 %copy-start.27 = (f32[64]{0:T(128)S(1)}, f32[64]{0:T(128)}, u32[]{:S(2)}) copy-start(f32[64]{0:T(128)} %param.25) | copy-start | bytes 772
  150.2 26.4 %copy-start.28 = (f32[64]{0:T(128)S(1)}, f32[64]{0:T(128)}, u32[]{:S(2)}) copy-start(f32[64]{0:T(128)} %param.26) | copy-start | bytes 772
  169.8 14.6 %all-to-all-start.1 = ((bf16[32,16,256]{2,1,0:T(8,128)(2,1)}), bf16[32,16,256]{2,1,0:T(8,128)(2,1)S(1)}, u32[]{:S(2)}, u32[]{:S(2)}) async-start(bf16[32,16,256]{2,1,0:T(8,128)(2,1)} %get-tuple-element.37), calls=%async_computation.1 | async-start | bytes 524288 | tf_op jit(solution)/shard_map/all_to_all | solution.py:552
  (25 other events, 211.5 us)

commit v5 on v4

--- a/solution.py
+++ b/solution.py
@@ -13,6 +13,7 @@
 AXES = ("row", "col")
 GROUP = 4
 SHORT = pl.CostEstimate(flops=0, bytes_accessed=0, transcendentals=0)
+LONG = pl.CostEstimate(flops=16 * 10**9, bytes_accessed=40 * 10**6, transcendentals=0)
 
 
 def contract(lhs, rhs, lhs_dim, rhs_dim):
@@ -107,6 +108,35 @@
     )(part, pair_activation, weight_t, bias, *ahead)
 
 
+def own_logits_kernel(pair_ref, weight_ref, bias_ref, *refs):
+    out_ref = refs[-1]
+    weight = weight_ref[...]
+    bias = as_column(bias_ref[...])
+    for i in range(pair_ref.shape[0]):
+        out_ref[i] = (contract(weight, pair_ref[i], 1, 1) + bias).astype(BF16)
+
+
+def own_logits(pair_activation, weight_t, bias, first_row, chunk_rows, ahead):
+    rows, cols, width = pair_activation.shape
+    bins = weight_t.shape[0]
+    step = min(8, chunk_rows)
+    return pl.pallas_call(
+        own_logits_kernel,
+        grid=(chunk_rows // step,),
+        in_specs=[
+            pl.BlockSpec((step, cols, width), lambda s: (first_row // step + s, 0, 0)),
+            pl.BlockSpec((bins, width), lambda s: (0, 0)),
+            pl.BlockSpec((1, bins), lambda s: (0, 0)),
+        ]
+        + [pl.BlockSpec(memory_space=pl.ANY)] * len(ahead),
+        out_specs=pl.BlockSpec((step, bins, cols), lambda s: (s, 0, 0)),
+        out_shape=jax.ShapeDtypeStruct((chunk_rows, bins, cols), BF16),
+        compiler_params=pltpu.CompilerParams(vmem_limit_bytes=LEAN_BYTES),
+        cost_estimate=SHORT,
+        name="own_logits",
+    )(pair_activation, weight_t, bias, *ahead)
+
+
 def tie_kernel(*refs):
     pass
 
@@ -170,9 +200,9 @@
     )(*arrays, *ahead)
 
 
-def pair_kernel(parts, slots, front, tile, resident, part_ref, pair_ref, *refs):
+def pair_kernel(parts, slots, front, tile, resident, part_ref, own_ref, *refs):
     received = refs[:parts]
-    target_ref, weight_t_ref, weight_wide_ref, bias_ref, factors, mix = refs[parts : parts + 6]
+    target_ref, weight_wide_ref, factors, mix = refs[parts : parts + 4]
     if resident:
         grad_ref, norm_ref, slopes, mix_wide, mixed, total = refs[-6:]
         copies = []
@@ -184,8 +214,8 @@
         ]
         factors, mix = factor_copy, mix_copy
     step = pl.program_id(0)
-    step_rows, cols, width = pair_ref.shape
-    bins = weight_t_ref.shape[0]
+    step_rows, cols, width = grad_ref.shape
+    bins = own_ref.shape[1]
     groups = slopes.shape[0]
     step_groups = step_rows // GROUP
     features = total.shape[0] * total.shape[2] // GROUP
@@ -205,14 +235,12 @@
     @pl.when(step < front)
     def _():
         h = part_ref[0]
-        weight_t = weight_t_ref[...]
-        bias = as_column(bias_ref[...])
         levels = lax.broadcasted_iota(jnp.int32, (bins, cols), 0)
         for g in range(step_groups):
             group = []
             for r in range(GROUP):
                 i = g * GROUP + r
-                own = (contract(weight_t, pair_ref[i], 1, 1) + bias).astype(BF16).astype(F32)
+                own = own_ref[base + i].astype(F32)
                 halves = []
                 for u in range(parts):
                     half = received[0][base + i]
@@ -276,11 +304,11 @@
 
 
 def pair_step(
-    part, pair_activation, received, targets, weight_t, weight_wide, bias, factors, mix, grad,
+    part, shape, own, received, targets, weight_wide, factors, mix, grad,
     first_row, seqs, devices, slots, ahead, resident,
 ):
-    _, cols, width = pair_activation.shape
-    bins = weight_t.shape[0]
+    _, cols, width = shape
+    bins = own.shape[1]
     features = mix.shape[2] // 2
     parts = len(received)
     chunk_rows = received[0].shape[0]
@@ -292,9 +320,10 @@
     near = lambda s: jnp.minimum(s, front - 1)
     anywhere = pl.BlockSpec(memory_space=pl.ANY)
     if resident:
-        held = moved = pl.BlockSpec(memory_space=pltpu.VMEM)
+        mine = held = moved = pl.BlockSpec(memory_space=pltpu.VMEM)
     else:
         held = pl.BlockSpec((step_rows, bins, cols // parts), lambda s, p: (near(s), 0, 0))
+        mine = pl.BlockSpec((step_rows, bins, cols), lambda s, p: (near(s), 0, 0))
         moved = anywhere
     there = lambda s: first_row // step_rows + jnp.minimum(s, front - 1)
     const2 = lambda s, p: (0, 0)
@@ -304,13 +333,11 @@
         grid_spec=pltpu.PrefetchScalarGridSpec(
             num_scalar_prefetch=1,
             grid=(front + 1,),
-            in_specs=[pl.BlockSpec((step_rows, cols, width), lambda s, p: (there(s), 0, 0))]
+            in_specs=[mine]
             + [held] * parts
             + [
                 pl.BlockSpec((step_rows, cols), lambda s, p: (there(s), 0)),
-                pl.BlockSpec((bins, width), const2),
                 pl.BlockSpec((GROUP * bins, GROUP * width), const2),
-                pl.BlockSpec((1, bins), const2),
             ]
             + [moved] * 2
             + [pl.BlockSpec(memory_space=pltpu.HBM)] * len(grad)
@@ -332,15 +359,14 @@
             ]),
         ),
         out_shape=[
-            jax.ShapeDtypeStruct(pair_activation.shape, BF16),
+            jax.ShapeDtypeStruct(shape, BF16),
             jax.ShapeDtypeStruct(norm_shape, BF16),
         ],
-        input_output_aliases={parts + 8: 0} if grad else {},
+        input_output_aliases={parts + 6: 0} if grad else {},
         compiler_params=pltpu.CompilerParams(vmem_limit_bytes=LEAN_BYTES if resident else VMEM_BYTES),
-        cost_estimate=SHORT,
+        cost_estimate=LONG,
         name="pair_step",
-    )(part, pair_activation, *received, targets, weight_t, weight_wide, bias, factors, mix, *grad,
-      *ahead)
+    )(part, own, *received, targets, weight_wide, factors, mix, *grad, *ahead)
 
 
 def norm_forward(features):
@@ -503,7 +529,7 @@
     count = len(chunks)
     leg_pairs = first_leg(col_devices, parts)
     first, logits, sent, relayed, received = [], [], [], [], []
-    norm_parts, arrived, grad = [], [], []
+    owns, norm_parts, arrived, grad = [], [], [], []
     for n in range(count + 2):
         while len(first) < min(2, count):
             first.append(
@@ -531,14 +557,24 @@
                     arrived.append(exchange(early))
                     ahead = [early]
                 *grad, norm_part = pair_step(
-                    part, pair_activation, received[now], target_distance_bins, weight_t,
-                    weight_wide, bias, factors, mix, grad, chunks[now][0], seqs, devices,
-                    row_devices, ahead, now < count - 1,
+                    part, pair_activation.shape, owns[now], received[now], target_distance_bins,
+                    weight_wide, factors, mix, grad, chunks[now][0], seqs, devices, row_devices,
+                    ahead, now < count - 1,
                 )
                 norm_parts.append(norm_part)
         if n < count:
             before = [[across, mix, weight_wide], [factors]][n] if n < 2 else [norm_parts[n - 2]]
-            before = before + (first[2:] if n == 0 else logits[n + 1 : n + 2])
+            if n == 0:
+                before = before + first[2:]
+            if n < 2:
+                for chunk in chunks[2 * n :][: 2 if n == 0 else count]:
+                    owns.append(
+                        own_logits(
+                            pair_activation, weight_t, bias, *chunk,
+                            owns[-1:] + (first[-1:] if n == 0 else relayed[0]),
+                        )
+                    )
+                before = before + owns[2 * n :]
             relayed.append(list(split(sent[n], before)))
             received.append(
                 [

time: 191 us -> 188 us (0.984)
  waiting for transfers between devices: 44.9 us -> 41.1 us
  local copies, waits for them, and re-layouts: 9.67 us -> 13.1 us
  starting transfers between devices: 36.3 us -> 33.8 us
    pallas_call x4, Pallas kernels: 63.8 us -> 57.8 us  [pair_step(): pl.pallas_call(functools.partial(pair_kernel, parts, slots, front, tile,...]
    pallas_call x0 -> x4, Pallas kernels: none -> 5.05 us  [own_logits(): pl.pallas_call(own_logits_kernel, grid=(chunk_rows // step,), in_specs=[p...]
    ppermute x4, waiting for transfers between devices: 22.5 us -> 18.7 us  [per_device(): sent.append(lax.ppermute(logits[m], AXES, leg_pairs))]
    unnamed x65 -> x73, local copies, waits for them, and re-layouts: 6.31 us -> 9.69 us
    ppermute x8, starting transfers between devices: 17.1 us -> 15.1 us  [per_device(): lax.ppermute(piece, AXES, second_leg(col_devices, parts, shift))]
  transfers between devices with their start and end apart: 18 -> 18, of which waited for: 9 -> 10; matrix products, arithmetic and copies ran while one was open for 5% -> 5% of each run, Pallas kernels for 45% -> 46%
where the time goes in v5:
time: 188 us
  Pallas kernels  92.6 us (49%)
  waiting for transfers between devices  41.1 us (22%)
  starting transfers between devices  33.8 us (18%)
  local copies, waits for them, and re-layouts  13.1 us (7%)
  other arithmetic  3.45 us (2%)
  matrix products  2.37 us (1%)
    pallas_call x4, Pallas kernels, pair_step(): pl.pallas_call(functools.partial(pair_kernel, parts, slots, front, tile,...  57.8 us
    pallas_call x4, Pallas kernels, mirror_logits(): pl.pallas_call(mirror_logits_kernel, grid_spec=pltpu.PrefetchScalarGridSp...  21.8 us
    ppermute x4, waiting for transfers between devices, per_device(): sent.append(lax.ppermute(logits[m], AXES, leg_pairs))  18.7 us
    ppermute x8, starting transfers between devices, per_device(): lax.ppermute(piece, AXES, second_leg(col_devices, parts, shift))  15.1 us
    ppermute x8, waiting for transfers between devices, per_device(): lax.ppermute(piece, AXES, second_leg(col_devices, parts, shift))  11.2 us
    unnamed x73, local copies, waits for them, and re-layouts  9.69 us
    all_to_all x1, waiting for transfers between devices, per_device(): arrived.append(exchange(final))  7.23 us
    all_to_all x1, starting transfers between devices, per_device(): arrived.append(exchange(early))  6.04 us
  transfers between devices with their start and end apart: 18, of which 10 were waited for; matrix products, arithmetic and copies ran while one was open for 5% of the time, Pallas kernels for 46%

profile of v5, /device:TPU:0, one launch (start us, length us, event | category | flops | bytes accessed | tf_op | source)
XLA Modules:
  0.0 187.5 jit_solution(18300497693816006992)
XLA Ops:
  2.5 3.0 %collective-permute-start = (bf16[8,64,256]{2,1,0:T(8,128)(2,1)S(1)}, bf16[8,64,256]{2,1,0:T(8,128)(2,1)S(1)}, u32[]{:S(2)}, u32[]{:S(2)}) collective-permute-start(bf16[8,64,256]{2,1,0:T(8,128)(2,1)S(1)} %join.3.refs_0_), channel_id=1, source_target_pairs={{8,0},{12,4},{0,8},{4,12},{24,16},{28,20},{16,24},{20,28},{9,1},{1... | collective-permute-start | bytes 786440 | tf_op jit(solution)/shard_map/ppermute | solution.py:498
  7.7 5.3 %mirror_logits.4.refs_0_ = bf16[2,32,64,128]{3,2,1,0:T(8,128)(2,1)} custom-call(s32[2]{0:T(128)} %pad_add_fusion.part_ref, bf16[128,256,128]{2,1,0:T(8,128)(2,1)} %pair_ref.15, bf16[64,128]{1,0:T(8,128)(2,1)} %bitcast.40, f32[1,64]{1,0:T(1,128)} %bitcast.54), custom_call_target="tpu_custom_call" | custom-call | tf_op jit(solution)/shard_map/mirror_logits/pallas_call | solution.py:88
  13.0 5.5 %mirror_logits.5.refs_0_ = bf16[2,32,64,128]{3,2,1,0:T(8,128)(2,1)} custom-call(s32[2]{0:T(128)} %pad_add_fusion.part_ref, bf16[128,256,128]{2,1,0:T(8,128)(2,1)} %pair_ref.15, bf16[64,128]{1,0:T(8,128)(2,1)} %bitcast.41, f32[1,64]{1,0:T(1,128)} %bitcast.55, bf16[2,32,64,128]{3,2,1,0:T(8,128)(2,1)} %mirror_logits.4.refs_0_), custom_call_target="tpu_custom_call" | custom-call | tf_op jit(solution)/shard_map/mirror_logits/pallas_call | solution.py:88
  18.9 2.0 %collective-permute-start.3 = (bf16[2,32,64,128]{3,2,1,0:T(8,128)(2,1)S(1)}, bf16[2,32,64,128]{3,2,1,0:T(8,128)(2,1)S(1)}, u32[]{:S(2)}, u32[]{:S(2)}) collective-permute-start(bf16[2,32,64,128]{3,2,1,0:T(8,128)(2,1)S(1)} %tie.5), channel_id=1, source_target_pairs={{0,16},{4,20},{1,24},{5,28},{2,18},{6,22},{3,26},{7,30},{8,0},{12,... | collective-permute-start | bytes 3145736 | tf_op jit(solution)/shard_map/ppermute | solution.py:543
  26.1 5.4 %mirror_logits.6.refs_0_.refs_3_ = bf16[2,32,64,128]{3,2,1,0:T(8,128)(2,1)} custom-call(s32[2]{0:T(128)} %pad_add_fusion.part_ref, bf16[128,256,128]{2,1,0:T(8,128)(2,1)} %pair_ref.15, bf16[64,128]{1,0:T(8,128)(2,1)} %bitcast.42, f32[1,64]{1,0:T(1,128)} %bitcast.56, bf16[2,32,64,128]{3,2,1,0:T(8,128)(2,1)} %copy-done.7), custom_call_target="tpu_custom_call" | custom-call | tf_op jit(solution)/shard_map/mirror_logits/pallas_call | solution.py:88
  31.5 5.5 %mirror_logits.7.refs_0_.refs_1_.refs_4_ = bf16[2,32,64,128]{3,2,1,0:T(8,128)(2,1)} custom-call(s32[2]{0:T(128)} %pad_add_fusion.part_ref, bf16[128,256,128]{2,1,0:T(8,128)(2,1)} %pair_ref.15, bf16[64,128]{1,0:T(8,128)(2,1)} %bitcast.43, f32[1,64]{1,0:T(1,128)} %bitcast.57, bf16[2,32,64,128]{3,2,1,0:T(8,128)(2,1)} %mirror_logits.6.refs_0_.refs_3_), custom_call_target="tpu_custom_call" | custom-call | tf_op jit(solution)/shard_map/mirror_logits/pallas_call | solution.py:88
  37.0 3.4 %copy-done.1 = bf16[128,256,128]{2,1,0:T(8,128)(2,1)S(1)} copy-done((bf16[128,256,128]{2,1,0:T(8,128)(2,1)S(1)}, bf16[128,256,128]{2,1,0:T(8,128)(2,1)}, u32[]{:S(2)}) %copy-start.1) | copy-done | bytes 8388632
  45.3 3.8 %collective-permute-start.6 = (bf16[32,64,128]{2,1,0:T(8,128)(2,1)S(1)}, bf16[32,64,128]{2,1,0:T(8,128)(2,1)S(1)}, u32[]{:S(2)}, u32[]{:S(2)}) collective-permute-start(bf16[32,64,128]{2,1,0:T(8,128)(2,1)S(1)} %get-tuple-element.20.refs_1_), channel_id=1, source_target_pairs={{16,0},{20,4},{24,8},{28,12},{18,16},{22,20},{26,24},{30,28},{0,1}... | collective-permute-start | bytes 1572872 | tf_op jit(solution)/shard_map/ppermute | solution.py:581
  54.8 12.9 %collective-permute-done.4.in_ref = bf16[2,32,64,128]{3,2,1,0:T(8,128)(2,1)} collective-permute-done((bf16[2,32,64,128]{3,2,1,0:T(8,128)(2,1)S(1)}, bf16[2,32,64,128]{3,2,1,0:T(8,128)(2,1)}, u32[]{:S(2)}, u32[]{:S(2)}) %collective-permute-start.4) | collective-permute-done | bytes 1048608 | tf_op jit(solution)/shard_map/ppermute | solution.py:543
  69.0 3.8 %collective-permute-start.9 = (bf16[32,64,128]{2,1,0:T(8,128)(2,1)S(1)}, bf16[32,64,128]{2,1,0:T(8,128)(2,1)S(1)}, u32[]{:S(2)}, u32[]{:S(2)}) collective-permute-start(bf16[32,64,128]{2,1,0:T(8,128)(2,1)S(1)} %get-tuple-element.22.refs_1_.refs_7_), channel_id=1, source_target_pairs={{16,0},{20,4},{24,8},{28,12},{18,16},{22,20},{26,24},{30,28},{0,1}... | collective-permute-start | bytes 1572872 | tf_op jit(solution)/shard_map/ppermute | solution.py:581
  72.9 14.0 %pair_step.4 = (bf16[128,256,128]{2,1,0:T(8,128)(2,1)}, bf16[32,16,256]{2,1,0:T(8,128)(2,1)S(1)}) custom-call(s32[2]{0:T(128)S(1)} %copy-done.21, bf16[32,64,256]{2,1,0:T(8,128)(2,1)S(1)} %own_logits.4.refs_0_.refs_5_.own_ref, bf16[32,64,128]{2,1,0:T(8,128)(2,1)S(1)} %collective-permute-done.6.refs_3_.refs_0_, ...), custom_call_target="tpu_custom_call" | custom-call | flops 16000000000 | bytes 40000000 | tf_op jit(solution)/shard_map/pair_step/pallas_call | solution.py:331
  86.9 3.1 %collective-permute-done.11.in_ref = bf16[2,32,64,128]{3,2,1,0:T(8,128)(2,1)S(1)} collective-permute-done((bf16[2,32,64,128]{3,2,1,0:T(8,128)(2,1)S(1)}, bf16[2,32,64,128]{3,2,1,0:T(8,128)(2,1)S(1)}, u32[]{:S(2)}, u32[]{:S(2)}) %collective-permute-start.11) | collective-permute-done | bytes 1048608 | tf_op jit(solution)/shard_map/ppermute | solution.py:543
  90.2 3.8 %collective-permute-start.14 = (bf16[32,64,128]{2,1,0:T(8,128)(2,1)S(1)}, bf16[32,64,128]{2,1,0:T(8,128)(2,1)S(1)}, u32[]{:S(2)}, u32[]{:S(2)}) collective-permute-start(bf16[32,64,128]{2,1,0:T(8,128)(2,1)S(1)} %get-tuple-element.26.refs_8_), channel_id=1, source_target_pairs={{16,0},{20,4},{24,8},{28,12},{18,16},{22,20},{26,24},{30,28},{0,1}... | collective-permute-start | bytes 1572872 | tf_op jit(solution)/shard_map/ppermute | solution.py:581
  94.8 14.0 %pair_step.5 = (bf16[128,256,128]{2,1,0:T(8,128)(2,1)}, bf16[32,16,256]{2,1,0:T(8,128)(2,1)S(1)}) custom-call(s32[2]{0:T(128)S(1)} %copy-done.21, bf16[32,64,256]{2,1,0:T(8,128)(2,1)S(1)} %own_logits.5.refs_6_.refs_0_.own_ref, bf16[32,64,128]{2,1,0:T(8,128)(2,1)S(1)} %collective-permute-done.9.refs_0_, ...), custom_call_target="tpu_custom_call", output_to_operand_aliasing={{0}: (8, {})} | custom-call | flops 16000000000 | bytes 40000000 | tf_op jit(solution)/shard_map/pair_step/pallas_call | solution.py:331
  110.9 3.6 %collective-permute-start.12 = (bf16[32,64,128]{2,1,0:T(8,128)(2,1)S(1)}, bf16[32,64,128]{2,1,0:T(8,128)(2,1)S(1)}, u32[]{:S(2)}, u32[]{:S(2)}) collective-permute-start(bf16[32,64,128]{2,1,0:T(8,128)(2,1)S(1)} %get-tuple-element.29.refs_7_), channel_id=1, source_target_pairs={{16,0},{20,4},{24,8},{28,12},{18,16},{22,20},{26,24},{30,28},{0,1}... | collective-permute-start | bytes 1572872 | tf_op jit(solution)/shard_map/ppermute | solution.py:581
  114.5 2.8 %collective-permute-done.15.refs_1_ = bf16[32,64,128]{2,1,0:T(8,128)(2,1)S(1)} collective-permute-done((bf16[32,64,128]{2,1,0:T(8,128)(2,1)S(1)}, bf16[32,64,128]{2,1,0:T(8,128)(2,1)S(1)}, u32[]{:S(2)}, u32[]{:S(2)}) %collective-permute-start.15) | collective-permute-done | bytes 524320 | tf_op jit(solution)/shard_map/ppermute | solution.py:581
  117.3 14.0 %pair_step.6 = (bf16[128,256,128]{2,1,0:T(8,128)(2,1)}, bf16[32,16,256]{2,1,0:T(8,128)(2,1)S(1)}) custom-call(s32[2]{0:T(128)S(1)} %copy-done.21, bf16[32,64,256]{2,1,0:T(8,128)(2,1)S(1)} %own_logits.6.refs_0_.refs_1_.own_ref, bf16[32,64,128]{2,1,0:T(8,128)(2,1)S(1)} %collective-permute-done.14.refs_0_, ...), custom_call_target="tpu_custom_call", output_to_operand_aliasing={{0}: (8, {})} | custom-call | flops 16000000000 | bytes 40000000 | tf_op jit(solution)/shard_map/pair_step/pallas_call | solution.py:331
  131.3 7.7 %collective-permute-done.13.refs_4_.refs_1_ = bf16[32,64,128]{2,1,0:T(8,128)(2,1)S(1)} collective-permute-done((bf16[32,64,128]{2,1,0:T(8,128)(2,1)S(1)}, bf16[32,64,128]{2,1,0:T(8,128)(2,1)S(1)}, u32[]{:S(2)}, u32[]{:S(2)}) %collective-permute-start.13) | collective-permute-done | bytes 524320 | tf_op jit(solution)/shard_map/ppermute | solution.py:581
  141.6 6.0 %all-to-all-start = ((bf16[32,48,256]{2,1,0:T(8,128)(2,1)}), bf16[32,48,256]{2,1,0:T(8,128)(2,1)S(1)}, u32[]{:S(2)}, u32[]{:S(2)}) async-start(bf16[32,48,256]{2,1,0:T(8,128)(2,1)} %join.5.refs_7_), calls=%async_computation | async-start | bytes 1572864 | tf_op jit(solution)/shard_map/all_to_all | solution.py:557
  147.7 15.8 %pair_step.7 = (bf16[128,256,128]{2,1,0:T(8,128)(2,1)}, bf16[32,16,256]{2,1,0:T(8,128)(2,1)}) custom-call(s32[2]{0:T(128)} %pad_add_fusion.part_ref, bf16[32,64,256]{2,1,0:T(8,128)(2,1)} %copy-done.9, bf16[32,64,128]{2,1,0:T(8,128)(2,1)} %copy-done.16, bf16[32,64,128]{2,1,0:T(8,128)(2,1)} %copy-done.17, ...), custom_call_target="tpu_custom_call", output_to_operand_aliasing={{0}: (8, {})} | custom-call | flops 16000000000 | bytes 40000000 | tf_op jit(solution)/shard_map/pair_step/pallas_call | solution.py:331
  163.4 3.8 %all-to-all-done.refs_0_ = bf16[32,48,256]{2,1,0:T(8,128)(2,1)S(1)} async-done(((bf16[32,48,256]{2,1,0:T(8,128)(2,1)}), bf16[32,48,256]{2,1,0:T(8,128)(2,1)S(1)}, u32[]{:S(2)}, u32[]{:S(2)}) %all-to-all-start) | async-done | bytes 786464 | tf_op jit(solution)/shard_map/all_to_all | solution.py:557
  167.2 4.4 %all-to-all-start.1 = ((bf16[32,16,256]{2,1,0:T(8,128)(2,1)}), bf16[32,16,256]{2,1,0:T(8,128)(2,1)S(1)}, u32[]{:S(2)}, u32[]{:S(2)}) async-start(bf16[32,16,256]{2,1,0:T(8,128)(2,1)} %get-tuple-element.37), calls=%async_computation.1 | async-start | bytes 524288 | tf_op jit(solution)/shard_map/all_to_all | solution.py:588
  174.6 7.2 %all-to-all-done.1.refs_1_ = bf16[32,16,256]{2,1,0:T(8,128)(2,1)S(1)} async-done(((bf16[32,16,256]{2,1,0:T(8,128)(2,1)}), bf16[32,16,256]{2,1,0:T(8,128)(2,1)S(1)}, u32[]{:S(2)}, u32[]{:S(2)}) %all-to-all-start.1) | async-done | bytes 262176 | tf_op jit(solution)/shard_map/all_to_all | solution.py:588
  182.5 5.0 %transition.1 = bf16[2,64,1024]{2,1,0:T(8,128)(2,1)} custom-call(bf16[2,64,1024]{2,1,0:T(8,128)(2,1)} %entry_ref.1, bf16[2,64,1024]{2,1,0:T(8,128)(2,1)} %arriving_ref.1, f32[64,1]{1,0:T(8,128)} %copy.27.mean_gain_ref, f32[64,1]{1,0:T(8,128)} %copy.28.gain_ref, bf16[512,64]{1,0:T(8,128)(2,1)} %copy.29.gate_up_t_ref, bf16[64,512]{1,0:T(8,128)(2,1)} %copy-done.25, ...), custom_call_target="tpu_custom_call" | custom-call | tf_op jit(solution)/shard_map/transition/pallas_call | solution.py:443
  (124 shorter events, 30.5 us)
Async XLA Ops:
  2.5 16.3 %collective-permute-start = (bf16[8,64,256]{2,1,0:T(8,128)(2,1)S(1)}, bf16[8,64,256]{2,1,0:T(8,128)(2,1)S(1)}, u32[]{:S(2)}, u32[]{:S(2)}) collective-permute-start(bf16[8,64,256]{2,1,0:T(8,128)(2,1)S(1)} %join.3.refs_0_), channel_id=1, source_target_pairs={{8,0},{12,4},{0,8},{4,12},{24,16},{28,20},{16,24},{20,28},{9,1},{1... | collective-permute-start | bytes 786440 | tf_op jit(solution)/shard_map/ppermute | solution.py:498
  5.5 13.4 %collective-permute-start.1 = (bf16[8,64,256]{2,1,0:T(8,128)(2,1)S(1)}, bf16[8,64,256]{2,1,0:T(8,128)(2,1)S(1)}, u32[]{:S(2)}, u32[]{:S(2)}) collective-permute-start(bf16[8,64,256]{2,1,0:T(8,128)(2,1)S(1)} %join.3.refs_0_), channel_id=1, source_target_pairs={{16,0},{20,4},{24,8},{28,12},{0,16},{4,20},{8,24},{12,28},{17,1},{... | collective-permute-start | bytes 786440 | tf_op jit(solution)/shard_map/ppermute | solution.py:498
  7.0 11.9 %collective-permute-start.2 = (bf16[8,64,256]{2,1,0:T(8,128)(2,1)S(1)}, bf16[8,64,256]{2,1,0:T(8,128)(2,1)S(1)}, u32[]{:S(2)}, u32[]{:S(2)}) collective-permute-start(bf16[8,64,256]{2,1,0:T(8,128)(2,1)S(1)} %join.3.refs_0_), channel_id=1, source_target_pairs={{24,0},{28,4},{16,8},{20,12},{8,16},{12,20},{0,24},{4,28},{25,1},{... | collective-permute-start | bytes 786440 | tf_op jit(solution)/shard_map/ppermute | solution.py:498
  18.8 26.3 %copy-start.14 = (bf16[32,8,4,128]{3,1,2,0:T(8,128)(2,1)}, bf16[32,8,4,128]{3,1,2,0:T(8,128)(2,1)S(1)}, u32[]{:S(2)}) copy-start(bf16[32,8,4,128]{3,1,2,0:T(8,128)(2,1)S(1)} %copy.35) | copy-start | bytes 786436
  18.9 26.1 %collective-permute-start.3 = (bf16[2,32,64,128]{3,2,1,0:T(8,128)(2,1)S(1)}, bf16[2,32,64,128]{3,2,1,0:T(8,128)(2,1)S(1)}, u32[]{:S(2)}, u32[]{:S(2)}) collective-permute-start(bf16[2,32,64,128]{3,2,1,0:T(8,128)(2,1)S(1)} %tie.5), channel_id=1, source_target_pairs={{0,16},{4,20},{1,24},{5,28},{2,18},{6,22},{3,26},{7,30},{8,0},{12,... | collective-permute-start | bytes 3145736 | tf_op jit(solution)/shard_map/ppermute | solution.py:543
  21.2 30.5 %collective-permute-start.5 = (bf16[32,64,256]{2,1,0:T(8,128)(2,1)S(1)}, bf16[32,64,256]{2,1,0:T(8,128)(2,1)}, u32[]{:S(2)}, u32[]{:S(2)}) collective-permute-start(bf16[32,64,256]{2,1,0:T(8,128)(2,1)S(1)} %join.4.refs_0_), channel_id=1, source_target_pairs={{4,0},{0,4},{12,8},{8,12},{20,16},{16,20},{28,24},{24,28},{5,1},{1... | collective-permute-start | bytes 3145736 | tf_op jit(solution)/shard_map/ppermute | solution.py:507
  22.3 45.3 %collective-permute-start.4 = (bf16[2,32,64,128]{3,2,1,0:T(8,128)(2,1)S(1)}, bf16[2,32,64,128]{3,2,1,0:T(8,128)(2,1)}, u32[]{:S(2)}, u32[]{:S(2)}) collective-permute-start(bf16[2,32,64,128]{3,2,1,0:T(8,128)(2,1)S(1)} %tie.4.refs_0_), channel_id=1, source_target_pairs={{0,16},{4,20},{1,24},{5,28},{2,18},{6,22},{3,26},{7,30},{8,0},{12,... | collective-permute-start | bytes 3145736 | tf_op jit(solution)/shard_map/ppermute | solution.py:543
  45.3 27.5 %collective-permute-start.6 = (bf16[32,64,128]{2,1,0:T(8,128)(2,1)S(1)}, bf16[32,64,128]{2,1,0:T(8,128)(2,1)S(1)}, u32[]{:S(2)}, u32[]{:S(2)}) collective-permute-start(bf16[32,64,128]{2,1,0:T(8,128)(2,1)S(1)} %get-tuple-element.20.refs_1_), channel_id=1, source_target_pairs={{16,0},{20,4},{24,8},{28,12},{18,16},{22,20},{26,24},{30,28},{0,1}... | collective-permute-start | bytes 1572872 | tf_op jit(solution)/shard_map/ppermute | solution.py:581
  49.1 23.7 %collective-permute-start.7 = (bf16[32,64,128]{2,1,0:T(8,128)(2,1)S(1)}, bf16[32,64,128]{2,1,0:T(8,128)(2,1)S(1)}, u32[]{:S(2)}, u32[]{:S(2)}) collective-permute-start(bf16[32,64,128]{2,1,0:T(8,128)(2,1)S(1)} %get-tuple-element.21.refs_2_), channel_id=1, source_target_pairs={{16,4},{20,0},{24,12},{28,8},{18,20},{22,16},{26,28},{30,24},{0,5}... | collective-permute-start | bytes 1572872 | tf_op jit(solution)/shard_map/ppermute | solution.py:581
  54.7 62.6 %copy-start.8 = (bf16[64,64,256]{2,1,0:T(8,128)(2,1)}, bf16[64,64,256]{2,1,0:T(8,128)(2,1)S(1)}, u32[]{:S(2)}) copy-start(bf16[64,64,256]{2,1,0:T(8,128)(2,1)S(1)} %copy.26) | copy-start | bytes 6291460
  54.7 35.3 %collective-permute-start.11 = (bf16[2,32,64,128]{3,2,1,0:T(8,128)(2,1)S(1)}, bf16[2,32,64,128]{3,2,1,0:T(8,128)(2,1)S(1)}, u32[]{:S(2)}, u32[]{:S(2)}) collective-permute-start(bf16[2,32,64,128]{3,2,1,0:T(8,128)(2,1)S(1)} %tie.7.refs_6_), channel_id=1, source_target_pairs={{0,16},{4,20},{1,24},{5,28},{2,18},{6,22},{3,26},{7,30},{8,0},{12,... | collective-permute-start | bytes 3145736 | tf_op jit(solution)/shard_map/ppermute | solution.py:543
  68.9 25.1 %collective-permute-start.10 = (bf16[32,64,128]{2,1,0:T(8,128)(2,1)S(1)}, bf16[32,64,128]{2,1,0:T(8,128)(2,1)S(1)}, u32[]{:S(2)}, u32[]{:S(2)}) collective-permute-start(bf16[32,64,128]{2,1,0:T(8,128)(2,1)S(1)} %get-tuple-element.23.refs_2_.refs_8_), channel_id=1, source_target_pairs={{16,4},{20,0},{24,12},{28,8},{18,20},{22,16},{26,28},{30,24},{0,5}... | collective-permute-start | bytes 1572872 | tf_op jit(solution)/shard_map/ppermute | solution.py:581
  69.0 25.8 %collective-permute-start.9 = (bf16[32,64,128]{2,1,0:T(8,128)(2,1)S(1)}, bf16[32,64,128]{2,1,0:T(8,128)(2,1)S(1)}, u32[]{:S(2)}, u32[]{:S(2)}) collective-permute-start(bf16[32,64,128]{2,1,0:T(8,128)(2,1)S(1)} %get-tuple-element.22.refs_1_.refs_7_), channel_id=1, source_target_pairs={{16,0},{20,4},{24,8},{28,12},{18,16},{22,20},{26,24},{30,28},{0,1}... | collective-permute-start | bytes 1572872 | tf_op jit(solution)/shard_map/ppermute | solution.py:581
  72.8 37.8 %collective-permute-start.8 = (bf16[2,32,64,128]{3,2,1,0:T(8,128)(2,1)S(1)}, bf16[2,32,64,128]{3,2,1,0:T(8,128)(2,1)S(1)}, u32[]{:S(2)}, u32[]{:S(2)}) collective-permute-start(bf16[2,32,64,128]{3,2,1,0:T(8,128)(2,1)S(1)} %tie.6.refs_7_), channel_id=1, source_target_pairs={{0,16},{4,20},{1,24},{5,28},{2,18},{6,22},{3,26},{7,30},{8,0},{12,... | collective-permute-start | bytes 3145736 | tf_op jit(solution)/shard_map/ppermute | solution.py:543
  90.2 24.3 %collective-permute-start.14 = (bf16[32,64,128]{2,1,0:T(8,128)(2,1)S(1)}, bf16[32,64,128]{2,1,0:T(8,128)(2,1)S(1)}, u32[]{:S(2)}, u32[]{:S(2)}) collective-permute-start(bf16[32,64,128]{2,1,0:T(8,128)(2,1)S(1)} %get-tuple-element.26.refs_8_), channel_id=1, source_target_pairs={{16,0},{20,4},{24,8},{28,12},{18,16},{22,20},{26,24},{30,28},{0,1}... | collective-permute-start | bytes 1572872 | tf_op jit(solution)/shard_map/ppermute | solution.py:581
  94.0 23.2 %collective-permute-start.15 = (bf16[32,64,128]{2,1,0:T(8,128)(2,1)S(1)}, bf16[32,64,128]{2,1,0:T(8,128)(2,1)S(1)}, u32[]{:S(2)}, u32[]{:S(2)}) collective-permute-start(bf16[32,64,128]{2,1,0:T(8,128)(2,1)S(1)} %get-tuple-element.27.refs_9_), channel_id=1, source_target_pairs={{16,4},{20,0},{24,12},{28,8},{18,20},{22,16},{26,28},{30,24},{0,5}... | collective-permute-start | bytes 1572872 | tf_op jit(solution)/shard_map/ppermute | solution.py:581
  110.9 20.4 %collective-permute-start.12 = (bf16[32,64,128]{2,1,0:T(8,128)(2,1)S(1)}, bf16[32,64,128]{2,1,0:T(8,128)(2,1)S(1)}, u32[]{:S(2)}, u32[]{:S(2)}) collective-permute-start(bf16[32,64,128]{2,1,0:T(8,128)(2,1)S(1)} %get-tuple-element.29.refs_7_), channel_id=1, source_target_pairs={{16,0},{20,4},{24,8},{28,12},{18,16},{22,20},{26,24},{30,28},{0,1}... | collective-permute-start | bytes 1572872 | tf_op jit(solution)/shard_map/ppermute | solution.py:581
  114.5 24.5 %collective-permute-start.13 = (bf16[32,64,128]{2,1,0:T(8,128)(2,1)S(1)}, bf16[32,64,128]{2,1,0:T(8,128)(2,1)S(1)}, u32[]{:S(2)}, u32[]{:S(2)}) collective-permute-start(bf16[32,64,128]{2,1,0:T(8,128)(2,1)S(1)} %get-tuple-element.30.refs_8_), channel_id=1, source_target_pairs={{16,4},{20,0},{24,12},{28,8},{18,20},{22,16},{26,28},{30,24},{0,5}... | collective-permute-start | bytes 1572872 | tf_op jit(solution)/shard_map/ppermute | solution.py:581
  141.6 25.7 %all-to-all-start = ((bf16[32,48,256]{2,1,0:T(8,128)(2,1)}), bf16[32,48,256]{2,1,0:T(8,128)(2,1)S(1)}, u32[]{:S(2)}, u32[]{:S(2)}) async-start(bf16[32,48,256]{2,1,0:T(8,128)(2,1)} %join.5.refs_7_), calls=%async_computation | async-start | bytes 1572864 | tf_op jit(solution)/shard_map/all_to_all | solution.py:557
  147.6 24.0 %copy-start.28 = (bf16[64,256]{1,0:T(8,128)(2,1)S(1)}, bf16[64,256]{1,0:T(8,128)(2,1)}, u32[]{:S(2)}) copy-start(bf16[64,256]{1,0:T(8,128)(2,1)} %param.28) | copy-start | bytes 98308
  147.6 24.8 %copy-start.26 = (bf16[256,64]{0,1:T(8,128)(2,1)S(1)}, bf16[256,64]{0,1:T(8,128)(2,1)}, u32[]{:S(2)}) copy-start(bf16[256,64]{0,1:T(8,128)(2,1)} %param.29) | copy-start | bytes 98308
  147.7 25.5 %copy-start.31 = (f32[64]{0:T(128)S(1)}, f32[64]{0:T(128)}, u32[]{:S(2)}) copy-start(f32[64]{0:T(128)} %param.25) | copy-start | bytes 772
  147.7 26.2 %copy-start.32 = (f32[64]{0:T(128)S(1)}, f32[64]{0:T(128)}, u32[]{:S(2)}) copy-start(f32[64]{0:T(128)} %param.26) | copy-start | bytes 772
  167.2 14.6 %all-to-all-start.1 = ((bf16[32,16,256]{2,1,0:T(8,128)(2,1)}), bf16[32,16,256]{2,1,0:T(8,128)(2,1)S(1)}, u32[]{:S(2)}, u32[]{:S(2)}) async-start(bf16[32,16,256]{2,1,0:T(8,128)(2,1)} %get-tuple-element.37), calls=%async_computation.1 | async-start | bytes 524288 | tf_op jit(solution)/shard_map/all_to_all | solution.py:588
  (29 other events, 178.7 us)

commit v6 on v5

--- a/solution.py
+++ b/solution.py
@@ -315,7 +315,7 @@
     step_rows = min(16, chunk_rows)
     groups = chunk_rows // GROUP
     xs = factors.shape[0] // seqs
-    tile = max(1, min(8, 512 // seqs))
+    tile = max(1, min(16, 1024 // seqs))
     front = chunk_rows // step_rows
     near = lambda s: jnp.minimum(s, front - 1)
     anywhere = pl.BlockSpec(memory_space=pl.ANY)

time: 188 us -> 188 us (level)
  Pallas kernels: 92.6 us -> 90.2 us
  waiting for transfers between devices: 41.1 us -> 43.3 us
    pallas_call x4, Pallas kernels: 57.8 us -> 55.4 us  [pair_step(): pl.pallas_call(functools.partial(pair_kernel, parts, slots, front, tile,...]
  transfers between devices with their start and end apart: 18 -> 18, of which waited for: 10 -> 10; matrix products, arithmetic and copies ran while one was open for 5% -> 5% of each run, Pallas kernels for 46% -> 45%
where the time goes in v6:
time: 188 us
  Pallas kernels  90.2 us (48%)
  waiting for transfers between devices  43.3 us (23%)
  starting transfers between devices  34 us (18%)
  local copies, waits for them, and re-layouts  13.1 us (7%)
  other arithmetic  3.45 us (2%)
  matrix products  2.37 us (1%)
    pallas_call x4, Pallas kernels, pair_step(): pl.pallas_call(functools.partial(pair_kernel, parts, slots, front, tile,...  55.4 us
    pallas_call x4, Pallas kernels, mirror_logits(): pl.pallas_call(mirror_logits_kernel, grid_spec=pltpu.PrefetchScalarGridSp...  21.8 us
    ppermute x4, waiting for transfers between devices, per_device(): sent.append(lax.ppermute(logits[m], AXES, leg_pairs))  19.9 us
    ppermute x8, starting transfers between devices, per_device(): lax.ppermute(piece, AXES, second_leg(col_devices, parts, shift))  15.1 us
    ppermute x8, waiting for transfers between devices, per_device(): lax.ppermute(piece, AXES, second_leg(col_devices, parts, shift))  11.9 us
    unnamed x73, local copies, waits for them, and re-layouts  9.69 us
    all_to_all x1, waiting for transfers between devices, per_device(): arrived.append(exchange(final))  7.23 us
    all_to_all x1, starting transfers between devices, per_device(): arrived.append(exchange(early))  6.26 us
  transfers between devices with their start and end apart: 18, of which 10 were waited for; matrix products, arithmetic and copies ran while one was open for 5% of the time, Pallas kernels for 45%

profile of v6, /device:TPU:0, one launch (start us, length us, event | category | flops | bytes accessed | tf_op | source)
XLA Modules:
  0.0 187.5 jit_solution(12874797203209037522)
XLA Ops:
  2.5 3.0 %collective-permute-start = (bf16[8,64,256]{2,1,0:T(8,128)(2,1)S(1)}, bf16[8,64,256]{2,1,0:T(8,128)(2,1)S(1)}, u32[]{:S(2)}, u32[]{:S(2)}) collective-permute-start(bf16[8,64,256]{2,1,0:T(8,128)(2,1)S(1)} %join.3.refs_0_), channel_id=1, source_target_pairs={{8,0},{12,4},{0,8},{4,12},{24,16},{28,20},{16,24},{20,28},{9,1},{1... | collective-permute-start | bytes 786440 | tf_op jit(solution)/shard_map/ppermute | solution.py:498
  7.7 5.3 %mirror_logits.4.refs_0_ = bf16[2,32,64,128]{3,2,1,0:T(8,128)(2,1)} custom-call(s32[2]{0:T(128)} %pad_add_fusion.part_ref, bf16[128,256,128]{2,1,0:T(8,128)(2,1)} %pair_ref.15, bf16[64,128]{1,0:T(8,128)(2,1)} %bitcast.40, f32[1,64]{1,0:T(1,128)} %bitcast.54), custom_call_target="tpu_custom_call" | custom-call | tf_op jit(solution)/shard_map/mirror_logits/pallas_call | solution.py:88
  13.0 5.5 %mirror_logits.5.refs_0_ = bf16[2,32,64,128]{3,2,1,0:T(8,128)(2,1)} custom-call(s32[2]{0:T(128)} %pad_add_fusion.part_ref, bf16[128,256,128]{2,1,0:T(8,128)(2,1)} %pair_ref.15, bf16[64,128]{1,0:T(8,128)(2,1)} %bitcast.41, f32[1,64]{1,0:T(1,128)} %bitcast.55, bf16[2,32,64,128]{3,2,1,0:T(8,128)(2,1)} %mirror_logits.4.refs_0_), custom_call_target="tpu_custom_call" | custom-call | tf_op jit(solution)/shard_map/mirror_logits/pallas_call | solution.py:88
  26.1 5.4 %mirror_logits.6.refs_0_.refs_3_ = bf16[2,32,64,128]{3,2,1,0:T(8,128)(2,1)} custom-call(s32[2]{0:T(128)} %pad_add_fusion.part_ref, bf16[128,256,128]{2,1,0:T(8,128)(2,1)} %pair_ref.15, bf16[64,128]{1,0:T(8,128)(2,1)} %bitcast.42, f32[1,64]{1,0:T(1,128)} %bitcast.56, bf16[2,32,64,128]{3,2,1,0:T(8,128)(2,1)} %copy-done.7), custom_call_target="tpu_custom_call" | custom-call | tf_op jit(solution)/shard_map/mirror_logits/pallas_call | solution.py:88
  31.5 5.5 %mirror_logits.7.refs_0_.refs_1_.refs_4_ = bf16[2,32,64,128]{3,2,1,0:T(8,128)(2,1)} custom-call(s32[2]{0:T(128)} %pad_add_fusion.part_ref, bf16[128,256,128]{2,1,0:T(8,128)(2,1)} %pair_ref.15, bf16[64,128]{1,0:T(8,128)(2,1)} %bitcast.43, f32[1,64]{1,0:T(1,128)} %bitcast.57, bf16[2,32,64,128]{3,2,1,0:T(8,128)(2,1)} %mirror_logits.6.refs_0_.refs_3_), custom_call_target="tpu_custom_call" | custom-call | tf_op jit(solution)/shard_map/mirror_logits/pallas_call | solution.py:88
  37.0 3.4 %copy-done.1 = bf16[128,256,128]{2,1,0:T(8,128)(2,1)S(1)} copy-done((bf16[128,256,128]{2,1,0:T(8,128)(2,1)S(1)}, bf16[128,256,128]{2,1,0:T(8,128)(2,1)}, u32[]{:S(2)}) %copy-start.1) | copy-done | bytes 8388632
  45.3 3.8 %collective-permute-start.6 = (bf16[32,64,128]{2,1,0:T(8,128)(2,1)S(1)}, bf16[32,64,128]{2,1,0:T(8,128)(2,1)S(1)}, u32[]{:S(2)}, u32[]{:S(2)}) collective-permute-start(bf16[32,64,128]{2,1,0:T(8,128)(2,1)S(1)} %get-tuple-element.20.refs_1_), channel_id=1, source_target_pairs={{16,0},{20,4},{24,8},{28,12},{18,16},{22,20},{26,24},{30,28},{0,1}... | collective-permute-start | bytes 1572872 | tf_op jit(solution)/shard_map/ppermute | solution.py:581
  54.8 12.9 %collective-permute-done.4.in_ref = bf16[2,32,64,128]{3,2,1,0:T(8,128)(2,1)} collective-permute-done((bf16[2,32,64,128]{3,2,1,0:T(8,128)(2,1)S(1)}, bf16[2,32,64,128]{3,2,1,0:T(8,128)(2,1)}, u32[]{:S(2)}, u32[]{:S(2)}) %collective-permute-start.4) | collective-permute-done | bytes 1048608 | tf_op jit(solution)/shard_map/ppermute | solution.py:543
  69.0 3.8 %collective-permute-start.9 = (bf16[32,64,128]{2,1,0:T(8,128)(2,1)S(1)}, bf16[32,64,128]{2,1,0:T(8,128)(2,1)S(1)}, u32[]{:S(2)}, u32[]{:S(2)}) collective-permute-start(bf16[32,64,128]{2,1,0:T(8,128)(2,1)S(1)} %get-tuple-element.22.refs_1_.refs_7_), channel_id=1, source_target_pairs={{16,0},{20,4},{24,8},{28,12},{18,16},{22,20},{26,24},{30,28},{0,1}... | collective-permute-start | bytes 1572872 | tf_op jit(solution)/shard_map/ppermute | solution.py:581
  72.9 13.4 %pair_step.4 = (bf16[128,256,128]{2,1,0:T(8,128)(2,1)}, bf16[32,16,256]{2,1,0:T(8,128)(2,1)S(1)}) custom-call(s32[2]{0:T(128)S(1)} %copy-done.21, bf16[32,64,256]{2,1,0:T(8,128)(2,1)S(1)} %own_logits.4.refs_0_.refs_5_.own_ref, bf16[32,64,128]{2,1,0:T(8,128)(2,1)S(1)} %collective-permute-done.6.refs_3_.refs_0_, ...), custom_call_target="tpu_custom_call" | custom-call | flops 16000000000 | bytes 40000000 | tf_op jit(solution)/shard_map/pair_step/pallas_call | solution.py:331
  86.3 3.7 %collective-permute-done.11.in_ref = bf16[2,32,64,128]{3,2,1,0:T(8,128)(2,1)S(1)} collective-permute-done((bf16[2,32,64,128]{3,2,1,0:T(8,128)(2,1)S(1)}, bf16[2,32,64,128]{3,2,1,0:T(8,128)(2,1)S(1)}, u32[]{:S(2)}, u32[]{:S(2)}) %collective-permute-start.11) | collective-permute-done | bytes 1048608 | tf_op jit(solution)/shard_map/ppermute | solution.py:543
  90.2 3.8 %collective-permute-start.14 = (bf16[32,64,128]{2,1,0:T(8,128)(2,1)S(1)}, bf16[32,64,128]{2,1,0:T(8,128)(2,1)S(1)}, u32[]{:S(2)}, u32[]{:S(2)}) collective-permute-start(bf16[32,64,128]{2,1,0:T(8,128)(2,1)S(1)} %get-tuple-element.26.refs_8_), channel_id=1, source_target_pairs={{16,0},{20,4},{24,8},{28,12},{18,16},{22,20},{26,24},{30,28},{0,1}... | collective-permute-start | bytes 1572872 | tf_op jit(solution)/shard_map/ppermute | solution.py:581
  94.8 13.4 %pair_step.5 = (bf16[128,256,128]{2,1,0:T(8,128)(2,1)}, bf16[32,16,256]{2,1,0:T(8,128)(2,1)S(1)}) custom-call(s32[2]{0:T(128)S(1)} %copy-done.21, bf16[32,64,256]{2,1,0:T(8,128)(2,1)S(1)} %own_logits.5.refs_6_.refs_0_.own_ref, bf16[32,64,128]{2,1,0:T(8,128)(2,1)S(1)} %collective-permute-done.9.refs_0_, ...), custom_call_target="tpu_custom_call", output_to_operand_aliasing={{0}: (8, {})} | custom-call | flops 16000000000 | bytes 40000000 | tf_op jit(solution)/shard_map/pair_step/pallas_call | solution.py:331
  108.2 2.4 %collective-permute-done.8.in_ref = bf16[2,32,64,128]{3,2,1,0:T(8,128)(2,1)S(1)} collective-permute-done((bf16[2,32,64,128]{3,2,1,0:T(8,128)(2,1)S(1)}, bf16[2,32,64,128]{3,2,1,0:T(8,128)(2,1)S(1)}, u32[]{:S(2)}, u32[]{:S(2)}) %collective-permute-start.8) | collective-permute-done | bytes 1048608 | tf_op jit(solution)/shard_map/ppermute | solution.py:543
  110.9 3.6 %collective-permute-start.12 = (bf16[32,64,128]{2,1,0:T(8,128)(2,1)S(1)}, bf16[32,64,128]{2,1,0:T(8,128)(2,1)S(1)}, u32[]{:S(2)}, u32[]{:S(2)}) collective-permute-start(bf16[32,64,128]{2,1,0:T(8,128)(2,1)S(1)} %get-tuple-element.29.refs_7_), channel_id=1, source_target_pairs={{16,0},{20,4},{24,8},{28,12},{18,16},{22,20},{26,24},{30,28},{0,1}... | collective-permute-start | bytes 1572872 | tf_op jit(solution)/shard_map/ppermute | solution.py:581
  114.5 2.8 %collective-permute-done.15.refs_1_ = bf16[32,64,128]{2,1,0:T(8,128)(2,1)S(1)} collective-permute-done((bf16[32,64,128]{2,1,0:T(8,128)(2,1)S(1)}, bf16[32,64,128]{2,1,0:T(8,128)(2,1)S(1)}, u32[]{:S(2)}, u32[]{:S(2)}) %collective-permute-start.15) | collective-permute-done | bytes 524320 | tf_op jit(solution)/shard_map/ppermute | solution.py:581
  117.3 13.4 %pair_step.6 = (bf16[128,256,128]{2,1,0:T(8,128)(2,1)}, bf16[32,16,256]{2,1,0:T(8,128)(2,1)S(1)}) custom-call(s32[2]{0:T(128)S(1)} %copy-done.21, bf16[32,64,256]{2,1,0:T(8,128)(2,1)S(1)} %own_logits.6.refs_0_.refs_1_.own_ref, bf16[32,64,128]{2,1,0:T(8,128)(2,1)S(1)} %collective-permute-done.14.refs_0_, ...), custom_call_target="tpu_custom_call", output_to_operand_aliasing={{0}: (8, {})} | custom-call | flops 16000000000 | bytes 40000000 | tf_op jit(solution)/shard_map/pair_step/pallas_call | solution.py:331
  130.7 8.3 %collective-permute-done.13.refs_4_.refs_1_ = bf16[32,64,128]{2,1,0:T(8,128)(2,1)S(1)} collective-permute-done((bf16[32,64,128]{2,1,0:T(8,128)(2,1)S(1)}, bf16[32,64,128]{2,1,0:T(8,128)(2,1)S(1)}, u32[]{:S(2)}, u32[]{:S(2)}) %collective-permute-start.13) | collective-permute-done | bytes 524320 | tf_op jit(solution)/shard_map/ppermute | solution.py:581
  141.6 6.3 %all-to-all-start = ((bf16[32,48,256]{2,1,0:T(8,128)(2,1)}), bf16[32,48,256]{2,1,0:T(8,128)(2,1)S(1)}, u32[]{:S(2)}, u32[]{:S(2)}) async-start(bf16[32,48,256]{2,1,0:T(8,128)(2,1)} %join.5.refs_7_), calls=%async_computation | async-start | bytes 1572864 | tf_op jit(solution)/shard_map/all_to_all | solution.py:557
  147.9 15.2 %pair_step.7 = (bf16[128,256,128]{2,1,0:T(8,128)(2,1)}, bf16[32,16,256]{2,1,0:T(8,128)(2,1)}) custom-call(s32[2]{0:T(128)} %pad_add_fusion.part_ref, bf16[32,64,256]{2,1,0:T(8,128)(2,1)} %copy-done.9, bf16[32,64,128]{2,1,0:T(8,128)(2,1)} %copy-done.16, bf16[32,64,128]{2,1,0:T(8,128)(2,1)} %copy-done.17, ...), custom_call_target="tpu_custom_call", output_to_operand_aliasing={{0}: (8, {})} | custom-call | flops 16000000000 | bytes 40000000 | tf_op jit(solution)/shard_map/pair_step/pallas_call | solution.py:331
  163.1 4.2 %all-to-all-done.refs_0_ = bf16[32,48,256]{2,1,0:T(8,128)(2,1)S(1)} async-done(((bf16[32,48,256]{2,1,0:T(8,128)(2,1)}), bf16[32,48,256]{2,1,0:T(8,128)(2,1)S(1)}, u32[]{:S(2)}, u32[]{:S(2)}) %all-to-all-start) | async-done | bytes 786464 | tf_op jit(solution)/shard_map/all_to_all | solution.py:557
  167.2 4.4 %all-to-all-start.1 = ((bf16[32,16,256]{2,1,0:T(8,128)(2,1)}), bf16[32,16,256]{2,1,0:T(8,128)(2,1)S(1)}, u32[]{:S(2)}, u32[]{:S(2)}) async-start(bf16[32,16,256]{2,1,0:T(8,128)(2,1)} %get-tuple-element.37), calls=%async_computation.1 | async-start | bytes 524288 | tf_op jit(solution)/shard_map/all_to_all | solution.py:588
  174.6 7.2 %all-to-all-done.1.refs_1_ = bf16[32,16,256]{2,1,0:T(8,128)(2,1)S(1)} async-done(((bf16[32,16,256]{2,1,0:T(8,128)(2,1)}), bf16[32,16,256]{2,1,0:T(8,128)(2,1)S(1)}, u32[]{:S(2)}, u32[]{:S(2)}) %all-to-all-start.1) | async-done | bytes 262176 | tf_op jit(solution)/shard_map/all_to_all | solution.py:588
  182.5 5.0 %transition.1 = bf16[2,64,1024]{2,1,0:T(8,128)(2,1)} custom-call(bf16[2,64,1024]{2,1,0:T(8,128)(2,1)} %entry_ref.1, bf16[2,64,1024]{2,1,0:T(8,128)(2,1)} %arriving_ref.1, f32[64,1]{1,0:T(8,128)} %copy.27.mean_gain_ref, f32[64,1]{1,0:T(8,128)} %copy.28.gain_ref, bf16[512,64]{1,0:T(8,128)(2,1)} %copy.29.gate_up_t_ref, bf16[64,512]{1,0:T(8,128)(2,1)} %copy-done.25, ...), custom_call_target="tpu_custom_call" | custom-call | tf_op jit(solution)/shard_map/transition/pallas_call | solution.py:443
  (124 shorter events, 30.6 us)
Async XLA Ops:
  2.5 16.3 %collective-permute-start = (bf16[8,64,256]{2,1,0:T(8,128)(2,1)S(1)}, bf16[8,64,256]{2,1,0:T(8,128)(2,1)S(1)}, u32[]{:S(2)}, u32[]{:S(2)}) collective-permute-start(bf16[8,64,256]{2,1,0:T(8,128)(2,1)S(1)} %join.3.refs_0_), channel_id=1, source_target_pairs={{8,0},{12,4},{0,8},{4,12},{24,16},{28,20},{16,24},{20,28},{9,1},{1... | collective-permute-start | bytes 786440 | tf_op jit(solution)/shard_map/ppermute | solution.py:498
  5.5 13.4 %collective-permute-start.1 = (bf16[8,64,256]{2,1,0:T(8,128)(2,1)S(1)}, bf16[8,64,256]{2,1,0:T(8,128)(2,1)S(1)}, u32[]{:S(2)}, u32[]{:S(2)}) collective-permute-start(bf16[8,64,256]{2,1,0:T(8,128)(2,1)S(1)} %join.3.refs_0_), channel_id=1, source_target_pairs={{16,0},{20,4},{24,8},{28,12},{0,16},{4,20},{8,24},{12,28},{17,1},{... | collective-permute-start | bytes 786440 | tf_op jit(solution)/shard_map/ppermute | solution.py:498
  7.0 11.9 %collective-permute-start.2 = (bf16[8,64,256]{2,1,0:T(8,128)(2,1)S(1)}, bf16[8,64,256]{2,1,0:T(8,128)(2,1)S(1)}, u32[]{:S(2)}, u32[]{:S(2)}) collective-permute-start(bf16[8,64,256]{2,1,0:T(8,128)(2,1)S(1)} %join.3.refs_0_), channel_id=1, source_target_pairs={{24,0},{28,4},{16,8},{20,12},{8,16},{12,20},{0,24},{4,28},{25,1},{... | collective-permute-start | bytes 786440 | tf_op jit(solution)/shard_map/ppermute | solution.py:498
  18.8 26.3 %copy-start.14 = (bf16[32,8,4,128]{3,1,2,0:T(8,128)(2,1)}, bf16[32,8,4,128]{3,1,2,0:T(8,128)(2,1)S(1)}, u32[]{:S(2)}) copy-start(bf16[32,8,4,128]{3,1,2,0:T(8,128)(2,1)S(1)} %copy.35) | copy-start | bytes 786436
  18.9 26.1 %collective-permute-start.3 = (bf16[2,32,64,128]{3,2,1,0:T(8,128)(2,1)S(1)}, bf16[2,32,64,128]{3,2,1,0:T(8,128)(2,1)S(1)}, u32[]{:S(2)}, u32[]{:S(2)}) collective-permute-start(bf16[2,32,64,128]{3,2,1,0:T(8,128)(2,1)S(1)} %tie.5), channel_id=1, source_target_pairs={{0,16},{4,20},{1,24},{5,28},{2,18},{6,22},{3,26},{7,30},{8,0},{12,... | collective-permute-start | bytes 3145736 | tf_op jit(solution)/shard_map/ppermute | solution.py:543
  21.2 30.5 %collective-permute-start.5 = (bf16[32,64,256]{2,1,0:T(8,128)(2,1)S(1)}, bf16[32,64,256]{2,1,0:T(8,128)(2,1)}, u32[]{:S(2)}, u32[]{:S(2)}) collective-permute-start(bf16[32,64,256]{2,1,0:T(8,128)(2,1)S(1)} %join.4.refs_0_), channel_id=1, source_target_pairs={{4,0},{0,4},{12,8},{8,12},{20,16},{16,20},{28,24},{24,28},{5,1},{1... | collective-permute-start | bytes 3145736 | tf_op jit(solution)/shard_map/ppermute | solution.py:507
  22.3 45.3 %collective-permute-start.4 = (bf16[2,32,64,128]{3,2,1,0:T(8,128)(2,1)S(1)}, bf16[2,32,64,128]{3,2,1,0:T(8,128)(2,1)}, u32[]{:S(2)}, u32[]{:S(2)}) collective-permute-start(bf16[2,32,64,128]{3,2,1,0:T(8,128)(2,1)S(1)} %tie.4.refs_0_), channel_id=1, source_target_pairs={{0,16},{4,20},{1,24},{5,28},{2,18},{6,22},{3,26},{7,30},{8,0},{12,... | collective-permute-start | bytes 3145736 | tf_op jit(solution)/shard_map/ppermute | solution.py:543
  45.3 27.5 %collective-permute-start.6 = (bf16[32,64,128]{2,1,0:T(8,128)(2,1)S(1)}, bf16[32,64,128]{2,1,0:T(8,128)(2,1)S(1)}, u32[]{:S(2)}, u32[]{:S(2)}) collective-permute-start(bf16[32,64,128]{2,1,0:T(8,128)(2,1)S(1)} %get-tuple-element.20.refs_1_), channel_id=1, source_target_pairs={{16,0},{20,4},{24,8},{28,12},{18,16},{22,20},{26,24},{30,28},{0,1}... | collective-permute-start | bytes 1572872 | tf_op jit(solution)/shard_map/ppermute | solution.py:581
  49.1 23.7 %collective-permute-start.7 = (bf16[32,64,128]{2,1,0:T(8,128)(2,1)S(1)}, bf16[32,64,128]{2,1,0:T(8,128)(2,1)S(1)}, u32[]{:S(2)}, u32[]{:S(2)}) collective-permute-start(bf16[32,64,128]{2,1,0:T(8,128)(2,1)S(1)} %get-tuple-element.21.refs_2_), channel_id=1, source_target_pairs={{16,4},{20,0},{24,12},{28,8},{18,20},{22,16},{26,28},{30,24},{0,5}... | collective-permute-start | bytes 1572872 | tf_op jit(solution)/shard_map/ppermute | solution.py:581
  54.7 62.6 %copy-start.8 = (bf16[64,64,256]{2,1,0:T(8,128)(2,1)}, bf16[64,64,256]{2,1,0:T(8,128)(2,1)S(1)}, u32[]{:S(2)}) copy-start(bf16[64,64,256]{2,1,0:T(8,128)(2,1)S(1)} %copy.26) | copy-start | bytes 6291460
  54.7 35.3 %collective-permute-start.11 = (bf16[2,32,64,128]{3,2,1,0:T(8,128)(2,1)S(1)}, bf16[2,32,64,128]{3,2,1,0:T(8,128)(2,1)S(1)}, u32[]{:S(2)}, u32[]{:S(2)}) collective-permute-start(bf16[2,32,64,128]{3,2,1,0:T(8,128)(2,1)S(1)} %tie.7.refs_6_), channel_id=1, source_target_pairs={{0,16},{4,20},{1,24},{5,28},{2,18},{6,22},{3,26},{7,30},{8,0},{12,... | collective-permute-start | bytes 3145736 | tf_op jit(solution)/shard_map/ppermute | solution.py:543
  68.9 25.1 %collective-permute-start.10 = (bf16[32,64,128]{2,1,0:T(8,128)(2,1)S(1)}, bf16[32,64,128]{2,1,0:T(8,128)(2,1)S(1)}, u32[]{:S(2)}, u32[]{:S(2)}) collective-permute-start(bf16[32,64,128]{2,1,0:T(8,128)(2,1)S(1)} %get-tuple-element.23.refs_2_.refs_8_), channel_id=1, source_target_pairs={{16,4},{20,0},{24,12},{28,8},{18,20},{22,16},{26,28},{30,24},{0,5}... | collective-permute-start | bytes 1572872 | tf_op jit(solution)/shard_map/ppermute | solution.py:581
  69.0 25.8 %collective-permute-start.9 = (bf16[32,64,128]{2,1,0:T(8,128)(2,1)S(1)}, bf16[32,64,128]{2,1,0:T(8,128)(2,1)S(1)}, u32[]{:S(2)}, u32[]{:S(2)}) collective-permute-start(bf16[32,64,128]{2,1,0:T(8,128)(2,1)S(1)} %get-tuple-element.22.refs_1_.refs_7_), channel_id=1, source_target_pairs={{16,0},{20,4},{24,8},{28,12},{18,16},{22,20},{26,24},{30,28},{0,1}... | collective-permute-start | bytes 1572872 | tf_op jit(solution)/shard_map/ppermute | solution.py:581
  72.8 37.8 %collective-permute-start.8 = (bf16[2,32,64,128]{3,2,1,0:T(8,128)(2,1)S(1)}, bf16[2,32,64,128]{3,2,1,0:T(8,128)(2,1)S(1)}, u32[]{:S(2)}, u32[]{:S(2)}) collective-permute-start(bf16[2,32,64,128]{3,2,1,0:T(8,128)(2,1)S(1)} %tie.6.refs_7_), channel_id=1, source_target_pairs={{0,16},{4,20},{1,24},{5,28},{2,18},{6,22},{3,26},{7,30},{8,0},{12,... | collective-permute-start | bytes 3145736 | tf_op jit(solution)/shard_map/ppermute | solution.py:543
  90.2 24.3 %collective-permute-start.14 = (bf16[32,64,128]{2,1,0:T(8,128)(2,1)S(1)}, bf16[32,64,128]{2,1,0:T(8,128)(2,1)S(1)}, u32[]{:S(2)}, u32[]{:S(2)}) collective-permute-start(bf16[32,64,128]{2,1,0:T(8,128)(2,1)S(1)} %get-tuple-element.26.refs_8_), channel_id=1, source_target_pairs={{16,0},{20,4},{24,8},{28,12},{18,16},{22,20},{26,24},{30,28},{0,1}... | collective-permute-start | bytes 1572872 | tf_op jit(solution)/shard_map/ppermute | solution.py:581
  94.0 23.2 %collective-permute-start.15 = (bf16[32,64,128]{2,1,0:T(8,128)(2,1)S(1)}, bf16[32,64,128]{2,1,0:T(8,128)(2,1)S(1)}, u32[]{:S(2)}, u32[]{:S(2)}) collective-permute-start(bf16[32,64,128]{2,1,0:T(8,128)(2,1)S(1)} %get-tuple-element.27.refs_9_), channel_id=1, source_target_pairs={{16,4},{20,0},{24,12},{28,8},{18,20},{22,16},{26,28},{30,24},{0,5}... | collective-permute-start | bytes 1572872 | tf_op jit(solution)/shard_map/ppermute | solution.py:581
  110.9 19.8 %collective-permute-start.12 = (bf16[32,64,128]{2,1,0:T(8,128)(2,1)S(1)}, bf16[32,64,128]{2,1,0:T(8,128)(2,1)S(1)}, u32[]{:S(2)}, u32[]{:S(2)}) collective-permute-start(bf16[32,64,128]{2,1,0:T(8,128)(2,1)S(1)} %get-tuple-element.29.refs_7_), channel_id=1, source_target_pairs={{16,0},{20,4},{24,8},{28,12},{18,16},{22,20},{26,24},{30,28},{0,1}... | collective-permute-start | bytes 1572872 | tf_op jit(solution)/shard_map/ppermute | solution.py:581
  114.5 24.5 %collective-permute-start.13 = (bf16[32,64,128]{2,1,0:T(8,128)(2,1)S(1)}, bf16[32,64,128]{2,1,0:T(8,128)(2,1)S(1)}, u32[]{:S(2)}, u32[]{:S(2)}) collective-permute-start(bf16[32,64,128]{2,1,0:T(8,128)(2,1)S(1)} %get-tuple-element.30.refs_8_), channel_id=1, source_target_pairs={{16,4},{20,0},{24,12},{28,8},{18,20},{22,16},{26,28},{30,24},{0,5}... | collective-permute-start | bytes 1572872 | tf_op jit(solution)/shard_map/ppermute | solution.py:581
  141.6 25.7 %all-to-all-start = ((bf16[32,48,256]{2,1,0:T(8,128)(2,1)}), bf16[32,48,256]{2,1,0:T(8,128)(2,1)S(1)}, u32[]{:S(2)}, u32[]{:S(2)}) async-start(bf16[32,48,256]{2,1,0:T(8,128)(2,1)} %join.5.refs_7_), calls=%async_computation | async-start | bytes 1572864 | tf_op jit(solution)/shard_map/all_to_all | solution.py:557
  147.8 23.8 %copy-start.28 = (bf16[64,256]{1,0:T(8,128)(2,1)S(1)}, bf16[64,256]{1,0:T(8,128)(2,1)}, u32[]{:S(2)}) copy-start(bf16[64,256]{1,0:T(8,128)(2,1)} %param.28) | copy-start | bytes 98308
  147.9 24.6 %copy-start.26 = (bf16[256,64]{0,1:T(8,128)(2,1)S(1)}, bf16[256,64]{0,1:T(8,128)(2,1)}, u32[]{:S(2)}) copy-start(bf16[256,64]{0,1:T(8,128)(2,1)} %param.29) | copy-start | bytes 98308
  147.9 25.3 %copy-start.31 = (f32[64]{0:T(128)S(1)}, f32[64]{0:T(128)}, u32[]{:S(2)}) copy-start(f32[64]{0:T(128)} %param.25) | copy-start | bytes 772
  147.9 26.0 %copy-start.32 = (f32[64]{0:T(128)S(1)}, f32[64]{0:T(128)}, u32[]{:S(2)}) copy-start(f32[64]{0:T(128)} %param.26) | copy-start | bytes 772
  167.2 14.6 %all-to-all-start.1 = ((bf16[32,16,256]{2,1,0:T(8,128)(2,1)}), bf16[32,16,256]{2,1,0:T(8,128)(2,1)S(1)}, u32[]{:S(2)}, u32[]{:S(2)}) async-start(bf16[32,16,256]{2,1,0:T(8,128)(2,1)} %get-tuple-element.37), calls=%async_computation.1 | async-start | bytes 524288 | tf_op jit(solution)/shard_map/all_to_all | solution.py:588
  (29 other events, 178.5 us)
